TPU v7x, 32 devices: a whole 2x2x4 slice. The times are simulated.
32 devices in a mesh: section: 2 (over x), dp: 16 (over z, y, core).
Axes of the slice: x: 2, y: 2, z: 4, core: 2. Of those that a mesh axis runs over, the one named last changes fastest.
Arguments:
- inputs: bfloat16 [2, 32, 256, 768], P('section', 'dp'), may hold values from -6 to 6
- cotangent: bfloat16 [2, 32, 256, 768], P('section', 'dp'), may hold values from -6 to 6
- enc_segments: int32 [32, 256], P('dp'), may hold values from 0 to 3, as said below
- dec_segments: int32 [32, 256], P('dp'), may hold values from 0 to 3, as said below
- rel_bias: float32 [32, 12], replicated, may hold values from -4 to 4
- attn_norm: bfloat16 [2, 768], P('section'), may hold values from 0.099609375 to 1.8984375
- ffn_norm: bfloat16 [2, 768], P('section'), may hold values from 0.099609375 to 1.8984375
- w_qkv: bfloat16 [2, 768, 2304], P('section'), may hold values from -0.078125 to 0.078125
- w_attn_out: bfloat16 [2, 768, 768], P('section'), may hold values from -3 to 3
- w_gate_up: bfloat16 [2, 768, 4096], P('section'), may hold values from -0.21875 to 0.21875
- w_down: bfloat16 [2, 2048, 768], P('section'), may hold values from -0.1875 to 0.1875
- cross_norm: bfloat16 [768], replicated, may hold values from 0.099609375 to 1.8984375
- cross_query: bfloat16 [768, 768], replicated, may hold values from -0.078125 to 0.078125
- cross_kv: bfloat16 [768, 1536], replicated, may hold values from -0.078125 to 0.078125
- cross_out: bfloat16 [768, 768], replicated, may hold values from -3 to 3
- final_norm: bfloat16 [768], replicated, may hold values from 0.099609375 to 1.8984375
Outputs:
- layer_out: bfloat16 [2, 32, 256, 768], P('section', 'dp')
- grad_inputs: float32 [2, 32, 256, 768], P('section', 'dp')
- grad_qkv: float32 [2, 768, 2304], P('section', 'dp')
- grad_attn_out: float32 [2, 768, 768], P('section', 'dp')
- grad_gate_up: float32 [2, 768, 4096], P('section', 'dp')
- grad_down: float32 [2, 2048, 768], P('section', 'dp')
- grad_attn_norm: float32 [2, 768], P('section', 'dp')
- grad_ffn_norm: float32 [2, 768], P('section', 'dp')
- grad_cross_query: float32 [768, 768], P('dp')
- grad_cross_kv: float32 [768, 1536], P('dp')
- grad_cross_out: float32 [768, 768], P('dp')
- grad_cross_norm: float32 [768], P('dp')
- grad_final_norm: float32 [768], P('dp')
- grad_rel_bias: float32 [32, 12], replicated
Inputs may be any that keep to these rules, and one draw needn't show every extreme that they name: `enc_segments`: each row holds documents 0 to 3 in order, each of one token or more; every row of the targets has the same 4 documents as the encoder row of the same index. `dec_segments`: as enc_segments: documents 0 to 3 in order, each of one token or more.
All inputs are finite; a program needn't handle non-finite values.
Results may differ from a plain program's by a relative error of at most 0.024.
Values may be sent and summed in bfloat16 or wider, within the bound.
A program may use at most 448 MiB of HBM per device.

v0:
```python
import jax
import jax.numpy as jnp
import numpy as np
from jax import lax
from jax.sharding import PartitionSpec as P

H = 12
HD = 64
NBUCKET = 32
MAXDIST = 128
MICRO = 2


EPSILON = 1e-06
MASKED = -1000000000.0
PRECISE = lax.Precision.HIGHEST
HALF_TYPE = jnp.bfloat16
FULL_TYPE = jnp.float32


def shifted(value, axis, by):
    devices = lax.axis_size(axis)
    pairs = [(i, i + by) for i in range(devices) if 0 <= i + by < devices]
    return lax.ppermute(value, axis, pairs)


def bucket_grid(length, causal, buckets, reach_max):
    offsets = np.arange(length)[None, :] - np.arange(length)[:, None]
    if causal:
        half_count = buckets
        side_offset = offsets * 0
        distance = np.maximum(-offsets, 0)
    else:
        half_count = buckets // 2
        side_offset = (offsets > 0).astype(np.int32) * half_count
        distance = np.abs(offsets)
    exact_count = half_count // 2
    clipped = np.maximum(distance, exact_count)
    spread = exact_count + np.floor(
        np.log(clipped / exact_count) / np.log(reach_max / exact_count) * (half_count - exact_count)
        + 1e-09
    ).astype(np.int32)
    spread = np.minimum(spread, half_count - 1)
    return (side_offset + np.where(distance < exact_count, distance, spread)).astype(np.int32)


def matmul(left_side, right_side):
    return jnp.dot(left_side, right_side, preferred_element_type=FULL_TYPE)


def inner_rows(left_side, right_side):
    return lax.dot_general(
        left_side, right_side, (((0,), (0,)), ((), ())), preferred_element_type=FULL_TYPE
    )


def outer_cols(left_side, right_side):
    return lax.dot_general(
        left_side, right_side, (((1,), (1,)), ((), ())), preferred_element_type=FULL_TYPE
    )


def flatten_for(grads, ways):
    return jnp.concatenate([grad_part.reshape(ways, -1) for grad_part in grads], 1)


def unflatten_from(flat, grads, ways):
    pieces = []
    offset = 0
    for grad_part in grads:
        count = grad_part.size // ways
        shape = (grad_part.shape[0] // ways,) + tuple(grad_part.shape[1:])
        pieces.append(flat[0, offset : offset + count].reshape(shape))
        offset = offset + count
    return tuple(pieces)


def norm_forward(values, gain_vec):
    inverse = lax.rsqrt(jnp.mean(values * values, -1, keepdims=True) + EPSILON)
    unit_rows = values * inverse
    return (unit_rows * gain_vec, unit_rows, inverse)


def norm_backward(grad_normed, unit_rows, inverse, gain_vec):
    grad_unit = grad_normed * gain_vec
    grad_values = inverse * (
        grad_unit - unit_rows * jnp.mean(grad_unit * unit_rows, -1, keepdims=True)
    )
    grad_gain = jnp.sum((grad_normed * unit_rows).reshape(-1, unit_rows.shape[-1]), axis=0)
    return (grad_values, grad_gain)


def relative_terms(rel_bias, length, causal):
    bucket_ids = jnp.asarray(bucket_grid(length, causal, NBUCKET, MAXDIST))
    one_hot = bucket_ids[:, :, None] == jnp.arange(rel_bias.shape[0])[None, None, :]
    rel_terms = jnp.einsum("qkb,bh->hqk", one_hot.astype(FULL_TYPE), rel_bias, precision=PRECISE)
    return (rel_terms, one_hot.astype(HALF_TYPE))


def bias_gradient(grad_scores, one_hot):
    return jnp.einsum("rhqk,qkb->bh", grad_scores, one_hot, preferred_element_type=FULL_TYPE)


def scores_of(queries, key_rows, rel_terms, allowed):
    scores = jnp.einsum("rqhd,rkhd->rhqk", queries, key_rows, preferred_element_type=FULL_TYPE)
    if rel_terms is not None:
        scores = scores + rel_terms[None]
    return jnp.where(allowed[:, None], scores, MASKED)


def attend_forward(queries, key_rows, value_rows, rel_terms, allowed):
    scores = scores_of(queries, key_rows, rel_terms, allowed)
    row_max = jnp.max(scores, -1, keepdims=True)
    raised = jnp.exp(scores - row_max)
    row_total = jnp.sum(raised, -1, keepdims=True)
    softmaxed = (raised / row_total).astype(HALF_TYPE)
    mixture = jnp.einsum("rhqk,rkhd->rqhd", softmaxed, value_rows, preferred_element_type=FULL_TYPE)
    return (mixture, row_max + jnp.log(row_total))


def attend_backward(queries, key_rows, value_rows, rel_terms, allowed, log_total, grad_mixture):
    scores = scores_of(queries, key_rows, rel_terms, allowed)
    softmaxed = jnp.exp(scores - log_total)
    grad_value = jnp.einsum(
        "rhqk,rqhd->rkhd",
        softmaxed.astype(HALF_TYPE),
        grad_mixture,
        preferred_element_type=FULL_TYPE,
    )
    grad_probs = jnp.einsum(
        "rqhd,rkhd->rhqk", grad_mixture, value_rows, preferred_element_type=FULL_TYPE
    )
    grad_scores = (
        softmaxed * (grad_probs - jnp.sum(softmaxed * grad_probs, -1, keepdims=True))
    ).astype(HALF_TYPE)
    grad_query = jnp.einsum(
        "rhqk,rkhd->rqhd", grad_scores, key_rows, preferred_element_type=FULL_TYPE
    )
    grad_key = jnp.einsum("rhqk,rqhd->rkhd", grad_scores, queries, preferred_element_type=FULL_TYPE)
    return (grad_query, grad_key, grad_value, grad_scores)


def self_forward(values, gain_vec, w_in, w_outer, rel_terms, allowed):
    row_count, length, model_width = values.shape
    normed, unit_rows, inverse = norm_forward(values, gain_vec)
    normed_low = normed.astype(HALF_TYPE).reshape(-1, model_width)
    packed = matmul(normed_low, w_in).astype(HALF_TYPE).reshape(row_count, length, 3, H, HD)
    mixture, log_total = attend_forward(
        packed[:, :, 0], packed[:, :, 1], packed[:, :, 2], rel_terms, allowed
    )
    mixture_low = mixture.astype(HALF_TYPE).reshape(-1, model_width)
    branch = matmul(mixture_low, w_outer).reshape(values.shape)
    return (values + branch, (unit_rows, inverse, normed_low, packed, log_total, mixture_low))


def self_backward(grad_after, gain_vec, w_in, w_outer, rel_terms, allowed, kept_state):
    unit_rows, inverse, normed_low, packed, log_total, mixture_low = kept_state
    grad_low = grad_after.reshape(-1, grad_after.shape[-1]).astype(HALF_TYPE)
    grad_w_outer = inner_rows(mixture_low, grad_low)
    grad_mixture = outer_cols(grad_low, w_outer).astype(HALF_TYPE).reshape(packed[:, :, 0].shape)
    grad_query, grad_key, grad_value, grad_scores = attend_backward(
        packed[:, :, 0],
        packed[:, :, 1],
        packed[:, :, 2],
        rel_terms,
        allowed,
        log_total,
        grad_mixture,
    )
    grad_packed = (
        jnp.stack([grad_query, grad_key, grad_value], 2)
        .astype(HALF_TYPE)
        .reshape(normed_low.shape[0], -1)
    )
    grad_w_in = inner_rows(normed_low, grad_packed)
    grad_normed = outer_cols(grad_packed, w_in).reshape(grad_after.shape)
    grad_values, grad_gain = norm_backward(grad_normed, unit_rows, inverse, gain_vec)
    return (grad_after + grad_values, grad_w_in, grad_w_outer, grad_gain, grad_scores)


def cross_forward(values, gain_vec, w_query, w_pair, w_outer, memory, allowed):
    row_count, length, model_width = values.shape
    normed, unit_rows, inverse = norm_forward(values, gain_vec)
    normed_low = normed.astype(HALF_TYPE).reshape(-1, model_width)
    queries = matmul(normed_low, w_query).astype(HALF_TYPE).reshape(row_count, length, H, HD)
    memory_flat = memory.reshape(-1, model_width)
    key_value = (
        matmul(memory_flat, w_pair).astype(HALF_TYPE).reshape(row_count, memory.shape[1], 2, H, HD)
    )
    mixture, log_total = attend_forward(
        queries, key_value[:, :, 0], key_value[:, :, 1], None, allowed
    )
    mixture_low = mixture.astype(HALF_TYPE).reshape(-1, model_width)
    branch = matmul(mixture_low, w_outer).reshape(values.shape)
    return (
        values + branch,
        (unit_rows, inverse, normed_low, queries, key_value, log_total, mixture_low),
    )


def cross_backward(grad_after, gain_vec, w_query, w_pair, w_outer, memory, allowed, kept_state):
    unit_rows, inverse, normed_low, queries, key_value, log_total, mixture_low = kept_state
    model_width = grad_after.shape[-1]
    grad_low = grad_after.reshape(-1, model_width).astype(HALF_TYPE)
    grad_w_outer = inner_rows(mixture_low, grad_low)
    grad_mixture = outer_cols(grad_low, w_outer).astype(HALF_TYPE).reshape(queries.shape)
    grad_query, grad_key, grad_value, unused = attend_backward(
        queries, key_value[:, :, 0], key_value[:, :, 1], None, allowed, log_total, grad_mixture
    )
    grad_query_low = grad_query.astype(HALF_TYPE).reshape(normed_low.shape[0], -1)
    grad_pairs = jnp.stack([grad_key, grad_value], 2).astype(HALF_TYPE).reshape(-1, 2 * model_width)
    memory_flat = memory.reshape(-1, model_width)
    grad_w_query = inner_rows(normed_low, grad_query_low)
    grad_w_pair = inner_rows(memory_flat, grad_pairs)
    grad_memory = outer_cols(grad_pairs, w_pair).reshape(memory.shape)
    grad_normed = outer_cols(grad_query_low, w_query).reshape(grad_after.shape)
    grad_values, grad_gain = norm_backward(grad_normed, unit_rows, inverse, gain_vec)
    return (
        grad_after + grad_values,
        grad_w_query,
        grad_w_pair,
        grad_w_outer,
        grad_gain,
        grad_memory,
    )


def gated(gate_part, up_part):
    return jax.nn.gelu(gate_part, approximate=True) * up_part


def ffn_forward(values, gain_vec, w_pair, w_lower):
    model_width = values.shape[-1]
    hidden_units = w_lower.shape[0]
    normed, unit_rows, inverse = norm_forward(values, gain_vec)
    normed_low = normed.astype(HALF_TYPE).reshape(-1, model_width)
    joined = matmul(normed_low, w_pair)
    hidden_low = gated(joined[:, :hidden_units], joined[:, hidden_units:]).astype(HALF_TYPE)
    branch = matmul(hidden_low, w_lower).reshape(values.shape)
    return (values + branch, (unit_rows, inverse, normed_low, joined, hidden_low))


def ffn_backward(grad_after, gain_vec, w_pair, w_lower, kept_state):
    unit_rows, inverse, normed_low, joined, hidden_low = kept_state
    hidden_units = w_lower.shape[0]
    grad_low = grad_after.reshape(-1, grad_after.shape[-1]).astype(HALF_TYPE)
    grad_w_lower = inner_rows(hidden_low, grad_low)
    grad_hidden = outer_cols(grad_low, w_lower)
    unused, pullback = jax.vjp(gated, joined[:, :hidden_units], joined[:, hidden_units:])
    grad_gate, grad_up = pullback(grad_hidden)
    grad_joined = jnp.concatenate([grad_gate, grad_up], -1).astype(HALF_TYPE)
    grad_w_pair = inner_rows(normed_low, grad_joined)
    grad_normed = outer_cols(grad_joined, w_pair).reshape(grad_after.shape)
    grad_values, grad_gain = norm_backward(grad_normed, unit_rows, inverse, gain_vec)
    return (grad_after + grad_values, grad_w_pair, grad_w_lower, grad_gain)


def on_section(active, section_work, *operands):
    return lax.cond(
        active,
        section_work,
        lambda *passed: jax.tree.map(jnp.zeros_like, section_work(*passed)),
        *operands
    )


def add_trees(first_tree, second_tree):
    return tuple(
        jax.tree.map(
            lambda first_part, second_part: first_part + second_part, first_tree, second_tree
        )
    )


def shards(
    inputs,
    cotangent,
    enc_segments,
    dec_segments,
    rel_bias,
    attn_norm,
    ffn_norm,
    w_qkv,
    w_attn_out,
    w_gate_up,
    w_down,
    cross_norm,
    cross_query,
    cross_kv,
    cross_out,
    final_norm,
):
    section_id = lax.axis_index("section")
    ways = lax.axis_size("dp")
    encoder_side = section_id == 0
    decoder_side = section_id == 1
    length = inputs.shape[2]
    model_width = inputs.shape[3]
    rows_each = inputs.shape[1] // MICRO
    self_gain = attn_norm[0].astype(FULL_TYPE)
    ffn_gain = ffn_norm[0].astype(FULL_TYPE)
    cross_gain = cross_norm.astype(FULL_TYPE)
    final_gain = final_norm.astype(FULL_TYPE)
    qkv_local = w_qkv[0]
    out_local = w_attn_out[0]
    pair_local = w_gate_up[0]
    lower_local = w_down[0]
    lower_tri = jnp.arange(length)[:, None] >= jnp.arange(length)[None, :]
    width_zeros = jnp.zeros((model_width,), FULL_TYPE)

    def encoder_forward(values, segments):
        allowed = segments[:, :, None] == segments[:, None, :]
        rel_terms, one_hot = relative_terms(rel_bias, length, False)
        after_attn, kept_attn = self_forward(
            values, self_gain, qkv_local, out_local, rel_terms, allowed
        )
        second, kept_ffn = ffn_forward(after_attn, ffn_gain, pair_local, lower_local)
        normed, unit_rows, inverse = norm_forward(second, final_gain)
        return (normed.astype(HALF_TYPE), (kept_attn, kept_ffn, unit_rows, inverse))

    def encoder_top(kept_state, grad_memory):
        kept_attn, kept_ffn, unit_rows, inverse = kept_state
        grad_second, grad_final = norm_backward(grad_memory, unit_rows, inverse, final_gain)
        grad_middle, grad_pair, grad_lower, grad_ffn_gain = ffn_backward(
            grad_second, ffn_gain, pair_local, lower_local, kept_ffn
        )
        return (grad_middle, grad_pair, grad_lower, grad_ffn_gain, grad_final)

    def encoder_attn(segments, kept_state, grad_middle):
        allowed = segments[:, :, None] == segments[:, None, :]
        rel_terms, one_hot = relative_terms(rel_bias, length, False)
        grad_input, grad_in, grad_outer, grad_self_gain, grad_scores = self_backward(
            grad_middle, self_gain, qkv_local, out_local, rel_terms, allowed, kept_state[0]
        )
        return (
            grad_input,
            grad_in,
            grad_outer,
            grad_self_gain,
            bias_gradient(grad_scores, one_hot),
        )

    def encoder_backward(segments, kept_state, grad_memory):
        grad_middle, grad_pair, grad_lower, grad_ffn_gain, grad_final = encoder_top(
            kept_state, grad_memory
        )
        grad_input, grad_in, grad_outer, grad_self_gain, grad_rel = encoder_attn(
            segments, kept_state, grad_middle
        )
        grads = (
            grad_in,
            grad_outer,
            grad_pair,
            grad_lower,
            grad_self_gain,
            grad_ffn_gain,
            jnp.zeros(cross_query.shape, FULL_TYPE),
            jnp.zeros(cross_kv.shape, FULL_TYPE),
            jnp.zeros(cross_out.shape, FULL_TYPE),
            width_zeros,
            grad_final,
            grad_rel,
        )
        return (grad_input, grads)

    def decoder_step(values, grad_result, segments, memory_segments, memory):
        allowed = (segments[:, :, None] == segments[:, None, :]) & lower_tri[None]
        cross_allowed = segments[:, :, None] == memory_segments[:, None, :]
        rel_terms, one_hot = relative_terms(rel_bias, length, True)
        dec_attn, kept_attn = self_forward(
            values, self_gain, qkv_local, out_local, rel_terms, allowed
        )
        middle, kept_cross = cross_forward(
            dec_attn, cross_gain, cross_query, cross_kv, cross_out, memory, cross_allowed
        )
        result, kept_ffn = ffn_forward(middle, ffn_gain, pair_local, lower_local)
        grad_middle, grad_pair, grad_lower, grad_ffn_gain = ffn_backward(
            grad_result, ffn_gain, pair_local, lower_local, kept_ffn
        )
        (
            grad_upper,
            grad_cross_query,
            grad_cross_kv,
            grad_cross_out,
            grad_cross_gain,
            grad_memory,
        ) = cross_backward(
            grad_middle,
            cross_gain,
            cross_query,
            cross_kv,
            cross_out,
            memory,
            cross_allowed,
            kept_cross,
        )
        grad_input, grad_in, grad_outer, grad_self_gain, grad_scores = self_backward(
            grad_upper, self_gain, qkv_local, out_local, rel_terms, allowed, kept_attn
        )
        grads = (
            grad_in,
            grad_outer,
            grad_pair,
            grad_lower,
            grad_self_gain,
            grad_ffn_gain,
            grad_cross_query,
            grad_cross_kv,
            grad_cross_out,
            grad_cross_gain,
            width_zeros,
            bias_gradient(grad_scores, one_hot),
        )
        return (result.astype(HALF_TYPE), grad_input, grads, grad_memory.astype(HALF_TYPE))

    collected = None
    out_pieces = []
    grad_pieces = []
    for number in range(MICRO):
        row_slice = slice(number * rows_each, (number + 1) * rows_each)
        values = inputs[0, row_slice].astype(FULL_TYPE)
        grad_result = cotangent[0, row_slice].astype(FULL_TYPE)
        enc_segment = enc_segments[row_slice]
        dec_segment = dec_segments[row_slice]
        memory, kept_state = on_section(encoder_side, encoder_forward, values, enc_segment)
        received = shifted(memory, "section", 1)
        result, grad_dec_input, grads_dec, grad_memory = on_section(
            decoder_side, decoder_step, values, grad_result, dec_segment, enc_segment, received
        )
        returned = shifted(grad_memory, "section", -1)
        grad_top = grad_result + returned.astype(FULL_TYPE)
        out_pieces.append(memory + result)
        grad_enc_input, grads_enc = on_section(
            encoder_side, encoder_backward, enc_segment, kept_state, grad_top
        )
        micro_grads = add_trees(grads_dec, grads_enc)
        if collected is None:
            collected = micro_grads
        else:
            collected = add_trees(collected, micro_grads)
        grad_pieces.append(grad_dec_input + grad_enc_input)
    total_group = tuple(collected[:11])
    total_flat = lax.psum_scatter(
        flatten_for(total_group, ways), "dp", scatter_dimension=0, tiled=True
    )
    collected = unflatten_from(total_flat, total_group, ways) + (collected[11],)
    (
        shard_qkv,
        shard_out,
        shard_pair,
        shard_lower,
        shard_attn,
        shard_ffn,
        shard_query,
        shard_kv,
        shard_cross_out,
        shard_cross_gain,
        shard_final,
        shard_rel,
    ) = collected
    shared_query, shared_kv, shared_cross_out, shared_cross_gain, shared_final = (
        lax.psum(shard_query.astype(jnp.bfloat16), "section").astype(jnp.float32),
        lax.psum(shard_kv.astype(jnp.bfloat16), "section").astype(jnp.float32),
        lax.psum(shard_cross_out.astype(jnp.bfloat16), "section").astype(jnp.float32),
        lax.psum(shard_cross_gain.astype(jnp.bfloat16), "section").astype(jnp.float32),
        lax.psum(shard_final.astype(jnp.bfloat16), "section").astype(jnp.float32),
    )
    rel_total = lax.psum(shard_rel, ("section", "dp"))
    layer_out = jnp.concatenate(out_pieces, 0)[None]
    grad_inputs = jnp.concatenate(grad_pieces, 0)[None]
    return (
        layer_out,
        grad_inputs,
        shard_qkv[None],
        shard_out[None],
        shard_pair[None],
        shard_lower[None],
        shard_attn[None],
        shard_ffn[None],
        shared_query,
        shared_kv,
        shared_cross_out,
        shared_cross_gain,
        shared_final,
        rel_total,
    )


def solution(mesh):
    return jax.shard_map(
        shards,
        mesh=mesh,
        in_specs=(
            P("section", "dp", None, None),
            P("section", "dp", None, None),
            P("dp", None),
            P("dp", None),
            P(),
            P("section", None),
            P("section", None),
            P("section", None, None),
            P("section", None, None),
            P("section", None, None),
            P("section", None, None),
            P(),
            P(),
            P(),
            P(),
            P(),
        ),
        out_specs=(
            P("section", "dp", None, None),
            P("section", "dp", None, None),
            P("section", "dp", None),
            P("section", "dp", None),
            P("section", "dp", None),
            P("section", "dp", None),
            P("section", "dp"),
            P("section", "dp"),
            P("dp", None),
            P("dp", None),
            P("dp", None),
            P("dp"),
            P("dp"),
            P(),
        ),
        check_vma=False,
    )
```

profile of v0, /device:TPU:0, one launch (start us, length us, event | category | flops | bytes accessed | tf_op | source)
XLA Modules:
  0.0 1231.8 jit_solution(12785621263967854734)
XLA Ops:
  9.9 35.2 %conditional.8 = (bf16[1,256,768]{2,1,0:T(8,128)(2,1)}, f32[1,256,768]{2,1,0:T(8,128)S(1)}, f32[1,256,1]{1,2,0:T(1,128)}, bf16[256,768]{1,0:T(8,128)(2,1)}, bf16...) conditional(s32[]{:T(128)} %convert_element_type.575, () %tuple.68, ...), branch_computations={%region_24.0_spmd, %region_25.31_spmd} | conditional | flops 4145018624 | bytes 119947224 | solution.py:259
  47.2 40.7 %conditional.6 = (bf16[1,256,768]{2,1,0:T(8,128)(2,1)}, f32[1,256,768]{2,1,0:T(8,128)S(1)}, f32[1,256,1]{1,2,0:T(1,128)}, bf16[256,768]{1,0:T(8,128)(2,1)}, bf16...) conditional(s32[]{:T(128)} %convert_element_type.575, () %tuple.64, ...), branch_computations={%region_0.0_spmd, %region_1.7_spmd} | conditional | flops 4145018624 | bytes 101588824 | solution.py:259
  93.7 25.8 %conditional.9 = (bf16[1,256,768]{2,1,0:T(8,128)(2,1)}, f32[1,256,768]{2,1,0:T(8,128)S(1)}, f32[768]{0:T(1024)S(1)}, f32[768]{0:T(1024)}, f32[768,768]{1,0:T(8,1...) conditional(s32[]{:T(128)} %convert_element_type.583, () %tuple.70, ...), branch_computations={%region_31.0_spmd.clone, %region_32.48_spmd.clone} | conditional | flops 16129771520 | bytes 471866656 | solution.py:259
  106.1 5.4 broadcast.992.clone
  120.9 30.8 %conditional.7 = (bf16[1,256,768]{2,1,0:T(8,128)(2,1)}, f32[1,256,768]{2,1,0:T(8,128)S(1)}, f32[768]{0:T(1024)S(1)}, f32[768]{0:T(1024)}, f32[768,768]{1,0:T(8,1...) conditional(s32[]{:T(128)} %convert_element_type.583, () %tuple.66, ...), branch_computations={%region_7.8_spmd.clone, %region_8.24_spmd.clone} | conditional | flops 16129771520 | bytes 484031520 | solution.py:259
  131.2 5.4 broadcast.976.clone
  153.0 15.7 %collective-permute-done.3 = bf16[1,256,768]{2,1,0:T(8,128)(2,1)} collective-permute-done((bf16[1,256,768]{2,1,0:T(8,128)(2,1)}, bf16[1,256,768]{2,1,0:T(8,128)(2,1)}, u32[]{:S(2)}, u32[]{:S(2)}) %collective-permute-start.3) | collective-permute-done | bytes 393248 | tf_op jit(solution)/shard_map/ppermute | solution.py:24
  169.9 46.4 %conditional.11 = (f32[1,256,768]{2,1,0:T(8,128)}, f32[768,2304]{0,1:T(8,128)}, f32[768,768]{0,1:T(8,128)}, f32[768,4096]{0,1:T(8,128)}, f32[2048,768]{0,1:T(8,1...) conditional(s32[]{:T(128)} %convert_element_type.575, () %tuple.74, ...), branch_computations={%region_57.0_spmd.clone, %region_58.66_spmd.clone} | conditional | flops 8144546816 | bytes 219190128 | solution.py:259
  203.0 6.4 convolution_bitcast_fusion.22
  218.7 53.6 %collective-permute-done.2 = bf16[1,256,768]{2,1,0:T(8,128)(2,1)} collective-permute-done((bf16[1,256,768]{2,1,0:T(8,128)(2,1)}, bf16[1,256,768]{2,1,0:T(8,128)(2,1)}, u32[]{:S(2)}, u32[]{:S(2)}) %collective-permute-start.2) | collective-permute-done | bytes 393248 | tf_op jit(solution)/shard_map/ppermute | solution.py:24
  273.4 52.3 %conditional.10 = (f32[1,256,768]{2,1,0:T(8,128)}, f32[768,2304]{0,1:T(8,128)}, f32[768,768]{0,1:T(8,128)}, f32[768,4096]{0,1:T(8,128)}, f32[2048,768]{0,1:T(8,1...) conditional(s32[]{:T(128)} %convert_element_type.575, () %tuple.72, ...), branch_computations={%region_48.0_spmd.clone, %region_49.57_spmd.clone} | conditional | flops 8144546816 | bytes 192918096 | solution.py:259
  311.4 6.4 convolution_bitcast_fusion.18
  325.7 13.1 %add_add_fusion.1 = f32[768,2304]{0,1:T(8,128)} fusion(f32[768,2304]{0,1:T(8,128)} %get-tuple-element.1146, f32[768,2304]{0,1:T(8,128)} %get-tuple-element.646, f32[768,2304]{0,1:T(8,128)} %get-tuple-element.1142, f32[768,2304]{0,1:T(8,128)} %get-tuple-element.635), kind=kLoop, calls=%fused_computation.549 | loop fusion | flops 5308416 | bytes 35389440 | tf_op jit(solution)/shard_map/add | solution.py:270
  338.8 8.0 copy.257
  346.8 5.5 reshape.1890
  352.3 6.6 constant_dynamic-update-slice_fusion.3
  366.5 21.8 %add_add_fusion = f32[768,4096]{0,1:T(8,128)} fusion(f32[768,4096]{0,1:T(8,128)} %get-tuple-element.1148, f32[768,4096]{0,1:T(8,128)} %get-tuple-element.648, f32[768,4096]{0,1:T(8,128)} %get-tuple-element.1144, f32[768,4096]{0,1:T(8,128)} %get-tuple-element.637), kind=kLoop, calls=%fused_computation.548 | loop fusion | flops 9437184 | bytes 62914560 | tf_op jit(solution)/shard_map/add | solution.py:270
  388.2 12.6 %copy.263 = f32[768,4096]{1,0:T(8,128)} copy(f32[768,4096]{0,1:T(8,128)} %add_add_fusion) | data formatting | bytes 25165824 | tf_op jit(solution)/shard_map/add | solution.py:270
  400.8 13.0 %reshape.1892 = f32[16,196608]{1,0:T(8,128)} reshape(f32[768,4096]{1,0:T(8,128)} %copy.263) | data formatting | bytes 25165824 | tf_op jit(solution)/shard_map/reshape | solution.py:64
  413.8 14.4 %add_add_fusion.2 = f32[2048,768]{0,1:T(8,128)} fusion(f32[2048,768]{0,1:T(8,128)} %get-tuple-element.1149, f32[2048,768]{0,1:T(8,128)} %get-tuple-element.649, f32[2048,768]{0,1:T(8,128)} %get-tuple-element.1145, f32[2048,768]{0,1:T(8,128)} %get-tuple-element.638), kind=kLoop, calls=%fused_computation.550 | loop fusion | flops 4718592 | bytes 31457280 | tf_op jit(solution)/shard_map/add | solution.py:270
  428.2 6.6 copy.266
  448.0 6.5 add_add_fusion.3
  454.5 6.1 copy.267
  474.3 11.2 constant_dynamic-update-slice_fusion.1
  491.3 7.6 dynamic-update-slice.6
  498.9 15.1 %dynamic-update-slice.7 = f32[16,590016]{1,0:T(8,128)} dynamic-update-slice(f32[16,590016]{1,0:T(8,128)} %dynamic-update-slice.6, f32[16,73728]{1,0:T(8,128)} %reshape.1897, s32[]{} %constant.285, s32[]{} %constant.292) | dynamic-update-slice | bytes 9437188
  514.0 7.5 dynamic-update-slice.8
  532.5 41.8 %psum.47 = f32[32,12]{0,1:T(8,128)} all-reduce(f32[32,12]{0,1:T(8,128)S(1)} %add_add_fusion.7), channel_id=1, replica_groups=mesh['section'=2,'dp'=16] {'section','dp'}, use_global_device_ids=true, to_apply=%region_72.73 | all-reduce | flops 384 | bytes 3072 | tf_op jit(solution)/shard_map/psum | solution.py:468
  575.5 584.3 %all-reduce.6.cloned.1.call-done = f32[16,590016]{1,0:T(8,128)} async-done(((f32[16,590016]{1,0:T(8,128)}), f32[16,590016]{1,0:T(8,128)}) %all-reduce.6.cloned.1.call-update) | async-done | bytes 37761040
  1159.8 8.4 dynamic-slice_convert_fusion
  1177.6 10.7 dynamic-slice_reduce_fusion
  1204.3 15.8 %all-reduce.8.cloned.1.call-done = (bf16[48,768]{1,0:T(8,128)(2,1)}, bf16[48,1536]{1,0:T(8,128)(2,1)}, bf16[48,768]{1,0:T(8,128)(2,1)}) async-done(((bf16[48,768]{1,0:T(8,128)(2,1)}, bf16[48,1536]{1,0:T(8,128)(2,1)}, bf16[48,768]{1,0:T(8,128)(2,1)}), (bf16[48,768]{1,0:T(8,128)(2,1)}, bf16[48,1536]{1,0:T(8,128)(2,1)}, bf16[48,768]{1,0:T(8,128)(2,1)})) %all-reduce.8.cloned.1.call-update) | async-done | bytes 294928 | tf_op jit(solution)/shard_map/psum | solution.py:462
  (409 shorter events, 292.8 us)
Async XLA Ops:
  7.2 1152.6 %all-reduce.6.cloned.1.call-start = ((), (), s32[]{:S(2)}) async-start(), calls=%async_computation | async-start | bytes 75530240
  8.6 38.5 %copy-start.11 = (f32[1,256,768]{2,1,0:T(8,128)}, f32[1,256,768]{2,1,0:T(8,128)S(1)}, u32[]{:S(2)}) copy-start(f32[1,256,768]{2,1,0:T(8,128)S(1)} %get-tuple-element.1263) | copy-start | bytes 2359300
  45.1 48.5 %collective-permute-start.1 = (bf16[1,256,768]{2,1,0:T(8,128)(2,1)}, bf16[1,256,768]{2,1,0:T(8,128)(2,1)}, u32[]{:S(2)}, u32[]{:S(2)}) collective-permute-start(bf16[1,256,768]{2,1,0:T(8,128)(2,1)} %get-tuple-element.522), channel_id=1, source_target_pairs={{0,16},{1,17},{2,18},{3,19},{4,20},{5,21},{6,22},{7,23},{8,24},{9,... | collective-permute-start | bytes 1179656 | tf_op jit(solution)/shard_map/ppermute | solution.py:24
  69.7 5.2 slice-start.2
  87.9 5.8 copy-start.77
  87.9 5.8 copy-start.114
  87.9 5.8 copy-start.170
  87.9 32.9 %collective-permute-start = (bf16[1,256,768]{2,1,0:T(8,128)(2,1)}, bf16[1,256,768]{2,1,0:T(8,128)(2,1)}, u32[]{:S(2)}, u32[]{:S(2)}) collective-permute-start(bf16[1,256,768]{2,1,0:T(8,128)(2,1)} %get-tuple-element.520), channel_id=1, source_target_pairs={{0,16},{1,17},{2,18},{3,19},{4,20},{5,21},{6,22},{7,23},{8,24},{9,... | collective-permute-start | bytes 1179656 | tf_op jit(solution)/shard_map/ppermute | solution.py:24
  119.5 49.2 %collective-permute-start.3 = (bf16[1,256,768]{2,1,0:T(8,128)(2,1)}, bf16[1,256,768]{2,1,0:T(8,128)(2,1)}, u32[]{:S(2)}, u32[]{:S(2)}) collective-permute-start(bf16[1,256,768]{2,1,0:T(8,128)(2,1)} %get-tuple-element.631), channel_id=1, source_target_pairs={{16,0},{17,1},{18,2},{19,3},{20,4},{21,5},{22,6},{23,7},{24,8},{25... | collective-permute-start | bytes 1179656 | tf_op jit(solution)/shard_map/ppermute | solution.py:24
  120.8 49.0 %copy-start.83 = (s32[256,256]{0,1:T(8,128)S(1)}, s32[256,256]{0,1:T(8,128)}, u32[]{:S(2)}) copy-start(s32[256,256]{0,1:T(8,128)} %constant.246.clone) | copy-start | bytes 786436
  151.7 18.1 %copy-start.65 = (f32[768,768]{0,1:T(8,128)}, f32[768,768]{0,1:T(8,128)S(1)}, u32[]{:S(2)}) copy-start(f32[768,768]{0,1:T(8,128)S(1)} %get-tuple-element.1143) | copy-start | bytes 7077892
  151.7 18.1 %copy-start.107 = (f32[1,256,768]{2,1,0:T(8,128)}, f32[1,256,768]{2,1,0:T(8,128)S(1)}, u32[]{:S(2)}) copy-start(f32[1,256,768]{2,1,0:T(8,128)S(1)} %get-tuple-element.603) | copy-start | bytes 2359300
  151.7 18.2 %copy-start.174 = (f32[32,12]{0,1:T(8,128)}, f32[32,12]{0,1:T(8,128)S(1)}, u32[]{:S(2)}) copy-start(f32[32,12]{0,1:T(8,128)S(1)} %get-tuple-element.614) | copy-start | bytes 4612
  151.7 18.2 %copy-start.186 = (f32[768]{0:T(1024)}, f32[768]{0:T(1024)S(1)}, u32[]{:S(2)}) copy-start(f32[768]{0:T(1024)S(1)} %get-tuple-element.608) | copy-start | bytes 9220
  151.7 120.6 %collective-permute-start.2 = (bf16[1,256,768]{2,1,0:T(8,128)(2,1)}, bf16[1,256,768]{2,1,0:T(8,128)(2,1)}, u32[]{:S(2)}, u32[]{:S(2)}) collective-permute-start(bf16[1,256,768]{2,1,0:T(8,128)(2,1)} %get-tuple-element.615), channel_id=1, source_target_pairs={{16,0},{17,1},{18,2},{19,3},{20,4},{21,5},{22,6},{23,7},{24,8},{25... | collective-permute-start | bytes 1179656 | tf_op jit(solution)/shard_map/ppermute | solution.py:24
  169.9 103.5 %copy-start.26 = (f32[1,256,768]{2,1,0:T(8,128)S(1)}, f32[1,256,768]{2,1,0:T(8,128)}, u32[]{:S(2)}) copy-start(f32[1,256,768]{2,1,0:T(8,128)} %get-tuple-element.1261) | copy-start | bytes 2359300
  171.7 6.1 slice-start.8
  173.3 6.7 copy-start.67
  203.0 6.4 copy-start.68
  275.6 5.3 slice-start.10
  303.9 5.3 copy-start.90
  352.3 6.6 copy-start.66
  434.8 5.1 copy-start.187
  434.8 5.1 copy-start.190
  434.8 5.2 copy-start.184
  434.8 5.2 copy-start.188
  434.8 5.2 copy-start.192
  472.7 12.8 %slice-start.12 = ((s8[6291456]{0:T(1024)(128)(4,1)}), s8[4194304]{0:T(1024)(128)(4,1)S(1)}, s32[]{:S(2)}) async-start(s8[6291456]{0:T(1024)(128)(4,1)} %bitcast.831), calls=%async_computation.14 | async-start | bytes 8388608
  474.3 11.2 slice-start.13
  485.5 5.8 copy-start.63
  498.9 15.1 %copy-start.64 = (f32[16,36864]{1,0:T(8,128)S(1)}, f32[16,36864]{1,0:T(8,128)}, u32[]{:S(2)}) copy-start(f32[16,36864]{1,0:T(8,128)} %reshape.1898) | copy-start | bytes 7077892
  524.4 695.7 %all-reduce.8.cloned.1.call-start = ((), (), s32[]{:S(2)}) async-start(), calls=%async_computation.1 | async-start | bytes 589824 | tf_op jit(solution)/shard_map/psum | solution.py:462
  (82 other events, 209.3 us)
Sparse Core Ops, SparseCore 0:
  524.5 635.3 all-reduce.5
  1196.4 23.6 all-reduce.7
where the time goes:
time: 1240 us; the launch traced here: 1230 us
  waiting for transfers between devices  670 us (54%)
  local copies, waits for them, and re-layouts  240 us (19%)
  other arithmetic  122 us (10%)
  matrix products  117 us (9%)
  blocking collectives  46.7 us (4%)
  loops' own time  14.8 us (1%)
  between operations  14.8 us (1%)
    unnamed x3, waiting for transfers between devices  584 us
    add x12, other arithmetic, add_trees(): first_part + second_part  69.8 us
    ppermute x4, waiting for transfers between devices, shifted(): return lax.ppermute(value, axis, pairs)  69.4 us
    unnamed x101, local copies, waits for them, and re-layouts  60.5 us
    another operation x31, local copies, waits for them, and re-layouts  54.1 us
    psum x1, blocking collectives, shards(): rel_total = lax.psum(shard_rel, ('section', 'dp'))  41.8 us
    reshape x11, local copies, waits for them, and re-layouts, flatten_for(): grad_part.reshape(ways, -1)  35.9 us
    dot_general x8, matrix products, inner_rows(): lax.dot_general(left_side, right_side, (((0,), (0,)), ((), ())), preferre...  35.8 us
  transfers between devices with their start and end apart: 6, of which 4 were waited for; matrix products, arithmetic and copies ran while one was open for 12% of the time, Pallas kernels for 0%

commit v1 on v0

--- a/solution.py
+++ b/solution.py
@@ -1,7 +1,11 @@
+import functools
+
 import jax
 import jax.numpy as jnp
 import numpy as np
 from jax import lax
+from jax.experimental import pallas as pl
+from jax.experimental.pallas import tpu as pltpu
 from jax.sharding import PartitionSpec as P
 
 H = 12
@@ -16,6 +20,156 @@
 PRECISE = lax.Precision.HIGHEST
 HALF_TYPE = jnp.bfloat16
 FULL_TYPE = jnp.float32
+
+
+MESH = pl.DeviceIdType.MESH
+
+
+class Item:
+    def __init__(self, rows, cols):
+        self.rows, self.cols = rows, cols
+
+
+def reduce_scratch(items):
+    shapes = []
+    for item in items:
+        r, n = item.rows, item.cols
+        shapes += [
+            pltpu.VMEM((4, 2, 2, r, n), HALF_TYPE),
+            pltpu.VMEM((4, 2, r, n), HALF_TYPE),
+            pltpu.VMEM((4, r, n), HALF_TYPE),
+            pltpu.VMEM((3, r, n), HALF_TYPE),
+        ]
+    count = len(items)
+    return shapes + [pltpu.SemaphoreType.DMA((count, 10)), pltpu.SemaphoreType.DMA((count,))]
+
+
+def reduce_kernel(items, *refs):
+    count = len(items)
+    ins, outs, scratch = refs[:count], refs[count : 2 * count], refs[2 * count :]
+    sem, local_sem = scratch[4 * count], scratch[4 * count + 1]
+    me, section = lax.axis_index("dp"), lax.axis_index("section")
+    z, y, c = me // 4, (me // 2) % 2, me % 2
+
+    def device(zz, yy, cc):
+        return (section, zz * 4 + yy * 2 + cc)
+
+    sibling, beside = device(z, y, 1 - c), device(z, 1 - y, c)
+    peers = [(z + d) % 4 for d in (1, 2, 3)]
+    barrier = pltpu.get_barrier_semaphore()
+    for target in [sibling, beside] + [device(peer, y, c) for peer in peers]:
+        pl.semaphore_signal(barrier, inc=1, device_id=target, device_id_type=MESH)
+    pl.semaphore_wait(barrier, 5)
+
+    def buffers(i):
+        return scratch[4 * i : 4 * i + 4]
+
+    def to_sibling(i):
+        own, first, _, _ = buffers(i)
+        return pltpu.make_async_remote_copy(
+            own.at[:, :, 1 - c], first, sem.at[i, 0], sem.at[i, 1], device_id=sibling, device_id_type=MESH
+        )
+
+    def to_beside(i):
+        own, _, second, _ = buffers(i)
+        return pltpu.make_async_remote_copy(
+            own.at[:, 1 - y, c], second, sem.at[i, 2], sem.at[i, 3], device_id=beside, device_id_type=MESH
+        )
+
+    def to_peer(i, d):
+        own, _, _, third = buffers(i)
+        return pltpu.make_async_remote_copy(
+            own.at[peers[d], y, c],
+            third.at[d],
+            sem.at[i, 4 + d],
+            sem.at[i, 7 + d],
+            device_id=device(peers[d], y, c),
+            device_id_type=MESH,
+        )
+
+    def add_first(i):
+        own, first, _, _ = buffers(i)
+        to_sibling(i).wait_recv()
+
+        def body(j, carry):
+            own[j // 2, j % 2, c] = own[j // 2, j % 2, c] + first[j // 2, j % 2]
+            return carry
+
+        lax.fori_loop(0, 8, body, 0)
+
+    def add_second(i):
+        own, _, second, _ = buffers(i)
+        to_beside(i).wait_recv()
+
+        def body(j, carry):
+            own[j, y, c] = own[j, y, c] + second[j]
+            return carry
+
+        lax.fori_loop(0, 4, body, 0)
+
+    def add_third(i):
+        own, _, _, third = buffers(i)
+        for d in range(3):
+            to_peer(i, d).wait_recv()
+        outs[i][...] = (own[z, y, c].astype(FULL_TYPE) + third[0].astype(FULL_TYPE)) + (
+            third[1].astype(FULL_TYPE) + third[2].astype(FULL_TYPE)
+        )
+
+    local = [pltpu.make_async_copy(ins[i], buffers(i)[0], local_sem.at[i]) for i in range(count)]
+    for copy in local:
+        copy.start()
+    for i in range(count):
+        local[i].wait()
+        to_sibling(i).start()
+    for i in range(count):
+        add_first(i)
+        to_beside(i).start()
+    for i in range(count):
+        add_second(i)
+        for d in range(3):
+            to_peer(i, d).start()
+    for i in range(count):
+        add_third(i)
+    for i in range(count):
+        to_sibling(i).wait_send()
+        to_beside(i).wait_send()
+        for d in range(3):
+            to_peer(i, d).wait_send()
+
+
+def reduce_all(grads, width, ways):
+    if ways != 16:
+        return [
+            lax.psum_scatter(g.astype(HALF_TYPE), "dp", scatter_dimension=0, tiled=True).astype(FULL_TYPE)
+            for g in grads
+        ]
+    items, pieces = [], []
+    for g in grads:
+        rows = g.shape[0] // ways
+        step = 512 if g.shape[1] % 768 else (768 if rows <= 48 else 256)
+        for at in range(0, g.shape[1], step):
+            items.append(Item(rows, step))
+            pieces.append(g[:, at : at + step].astype(HALF_TYPE).reshape(4, 2, 2, rows, step))
+    out = pl.pallas_call(
+        functools.partial(reduce_kernel, items),
+        out_shape=[jax.ShapeDtypeStruct((it.rows, it.cols), FULL_TYPE) for it in items],
+        in_specs=[pl.BlockSpec(memory_space=pl.ANY)] * len(items),
+        out_specs=[pl.BlockSpec(memory_space=pltpu.VMEM)] * len(items),
+        scratch_shapes=reduce_scratch(items),
+        compiler_params=pltpu.CompilerParams(
+            collective_id=1, has_side_effects=True, vmem_limit_bytes=62 * 2**20
+        ),
+    )(*pieces)
+    results, at = [], 0
+    for g in grads:
+        n = 0
+        parts = []
+        while n < g.shape[1]:
+            parts.append(out[at])
+            n += items[at].cols
+            at += 1
+        results.append(parts[0] if len(parts) == 1 else jnp.concatenate(parts, 1))
+    return results
 
 
 def shifted(value, axis, by):
@@ -439,11 +593,24 @@
         else:
             collected = add_trees(collected, micro_grads)
         grad_pieces.append(grad_dec_input + grad_enc_input)
-    total_group = tuple(collected[:11])
-    total_flat = lax.psum_scatter(
-        flatten_for(total_group, ways), "dp", scatter_dimension=0, tiled=True
-    )
-    collected = unflatten_from(total_flat, total_group, ways) + (collected[11],)
+    big = [collected[i] for i in (0, 1, 2, 3, 6, 7, 8)]
+    small = [collected[i] for i in (4, 5, 9, 10)]
+    big = reduce_all(big, model_width, ways)
+    small = lax.psum_scatter(jnp.stack(small, 1), "dp", scatter_dimension=0, tiled=True)
+    collected = (
+        big[0],
+        big[1],
+        big[2],
+        big[3],
+        small[:, 0],
+        small[:, 1],
+        big[4],
+        big[5],
+        big[6],
+        small[:, 2],
+        small[:, 3],
+        collected[11],
+    )
     (
         shard_qkv,
         shard_out,

time: 1240 us -> 644 us (0.52)
  waiting for transfers between devices: 670 us -> 71.8 us
  local copies, waits for them, and re-layouts: 240 us -> 113 us
  Pallas kernels: 0 us -> 125 us
    unnamed x3, waiting for transfers between devices: 584 us -> 0.05 us
    pallas_call x0 -> x1, Pallas kernels: none -> 125 us  [reduce_all(): pl.pallas_call(functools.partial(reduce_kernel, items), out_shape=[jax.Sh...]
    add x12 -> x5, other arithmetic: 69.8 us -> 3.51 us  [add_trees(): first_part + second_part]
    unnamed x101 -> x126, local copies, waits for them, and re-layouts: 60.5 us -> 10.4 us
    another operation x0 -> x8, other arithmetic: none -> 44.3 us
    reshape x11 -> x0, local copies, waits for them, and re-layouts: 35.9 us -> none  [flatten_for(): grad_part.reshape(ways, -1)]
    add x5 -> x0, local copies, waits for them, and re-layouts: 35.2 us -> none  [add_trees(): first_part + second_part]
    another operation x35, local copies, waits for them, and re-layouts: 57.5 us -> 40.5 us
  transfers between devices with their start and end apart: 6 -> 6, of which waited for: 4 -> 3; matrix products, arithmetic and copies ran while one was open for 12% -> 29% of each run, Pallas kernels for 0% -> 20%
where the time goes in v1:
time: 644 us; the launch traced here: 634 us
  matrix products  127 us (20%)
  Pallas kernels  125 us (19%)
  other arithmetic  119 us (18%)
  local copies, waits for them, and re-layouts  113 us (18%)
  waiting for transfers between devices  71.8 us (11%)
  blocking collectives  44.4 us (7%)
  between operations  16.5 us (3%)
  loops' own time  9.45 us (1%)
  starting transfers between devices  7.08 us (1%)
    pallas_call x1, Pallas kernels, reduce_all(): pl.pallas_call(functools.partial(reduce_kernel, items), out_shape=[jax.Sh...  125 us
    ppermute x4, waiting for transfers between devices, shifted(): return lax.ppermute(value, axis, pairs)  54.5 us
    another operation x7, other arithmetic  43.6 us
    psum x1, blocking collectives, shards(): rel_total = lax.psum(shard_rel, ('section', 'dp'))  39.2 us
    dot_general x8, matrix products, inner_rows(): lax.dot_general(left_side, right_side, (((0,), (0,)), ((), ())), preferre...  39.2 us
    another operation x30, local copies, waits for them, and re-layouts  38.2 us
    slice x20, local copies, waits for them, and re-layouts, reduce_all(): g[:, at:at + step].astype(HALF_TYPE).reshape(4, 2, 2, rows, step)  37.9 us
    dot_general x8, matrix products, matmul(): return jnp.dot(left_side, right_side, preferred_element_type=FULL_TYPE)  24 us
  transfers between devices with their start and end apart: 6, of which 3 were waited for; matrix products, arithmetic and copies ran while one was open for 29% of the time, Pallas kernels for 20%

profile of v1, /device:TPU:0, one launch (start us, length us, event | category | flops | bytes accessed | tf_op | source)
XLA Modules:
  0.0 634.0 jit_solution(18420636196939655123)
XLA Ops:
  12.0 38.1 %conditional.6 = (bf16[1,256,768]{2,1,0:T(8,128)(2,1)}, f32[1,256,768]{2,1,0:T(8,128)S(1)}, f32[1,256,1]{1,2,0:T(1,128)}, bf16[256,768]{1,0:T(8,128)(2,1)}, bf16...) conditional(s32[]{:T(128)} %convert_element_type.595, () %tuple.64, ...), branch_computations={%region_0.0_spmd, %region_1.7_spmd} | conditional | flops 4145018624 | bytes 103165848 | solution.py:413
  14.4 4.2 convolution_convert_fusion
  21.0 4.1 fusion
  25.2 5.0 copy.227
  41.5 4.1 fusion.12
  52.1 44.2 %conditional.8 = (bf16[1,256,768]{2,1,0:T(8,128)(2,1)}, f32[1,256,768]{2,1,0:T(8,128)}, f32[1,256,1]{1,2,0:T(1,128)}, bf16[256,768]{1,0:T(8,128)(2,1)}, bf16[1,2...) conditional(s32[]{:T(128)} %convert_element_type.595, () %tuple.68, ...), branch_computations={%region_24.0_spmd, %region_25.31_spmd} | conditional | flops 4145018624 | bytes 95293144 | solution.py:413
  56.6 4.3 convolution_convert_fusion.1
  63.3 4.1 fusion.20
  67.4 5.0 copy.231
  83.0 4.8 fusion.360
  101.8 27.2 %conditional.7 = (bf16[1,256,768]{2,1,0:T(8,128)(2,1)}, f32[1,256,768]{2,1,0:T(8,128)}, f32[768]{0:T(1024)S(1)}, f32[768]{0:T(1024)}, f32[768,768]{1,0:T(8,128)}...) conditional(s32[]{:T(128)} %convert_element_type.603, () %tuple.66, ...), branch_computations={%region_7.8_spmd.clone, %region_8.24_spmd.clone} | conditional | flops 16129771520 | bytes 439249792 | solution.py:413
  117.9 5.4 broadcast.976.clone
  130.4 16.8 %conditional.9 = (bf16[1,256,768]{2,1,0:T(8,128)(2,1)}, f32[1,256,768]{2,1,0:T(8,128)}, f32[768]{0:T(1024)S(1)}, f32[768]{0:T(1024)}, f32[768,768]{1,0:T(8,128)}...) conditional(s32[]{:T(128)} %convert_element_type.603, () %tuple.70, ...), branch_computations={%region_31.0_spmd.clone, %region_32.48_spmd.clone} | conditional | flops 16129771520 | bytes 434537344 | solution.py:413
  158.5 18.5 %collective-permute-done.2 = bf16[1,256,768]{2,1,0:T(8,128)(2,1)} collective-permute-done((bf16[1,256,768]{2,1,0:T(8,128)(2,1)}, bf16[1,256,768]{2,1,0:T(8,128)(2,1)}, u32[]{:S(2)}, u32[]{:S(2)}) %collective-permute-start.2) | collective-permute-done | bytes 393248 | tf_op jit(solution)/shard_map/ppermute | solution.py:178
  178.1 51.0 %conditional.10 = (f32[1,256,768]{2,1,0:T(8,128)S(1)}, f32[768,2304]{0,1:T(8,128)}, f32[768,768]{0,1:T(8,128)}, f32[768,4096]{0,1:T(8,128)}, f32[2048,768]{0,1:T...) conditional(s32[]{:T(128)} %convert_element_type.595, () %tuple.72, ...), branch_computations={%region_48.0_spmd.clone, %region_49.57_spmd.clone} | conditional | flops 8144546816 | bytes 213154704 | solution.py:413
  181.4 5.0 fusion.243
  213.4 5.0 convolution_bitcast_fusion.20
  222.5 6.4 %convolution_bitcast_fusion.18 = f32[768,4096]{0,1:T(8,128)} fusion(bf16[256,768]{1,0:T(8,128)(2,1)S(1)} %copy-done.86, bf16[256,2048]{1,0:T(8,128)(2,1)S(1)} %copy-done.125, bf16[256,2048]{1,0:T(8,128)(2,1)S(1)} %copy-done.123), kind=kOutput, calls=%fused_computation.385 | convolution fusion | flops 1614807040 | bytes 15073280 | tf_op jit(solution)/shard_map/cond/branch_1_fun/dot_general | solution.py:206
  230.0 36.0 %collective-permute-done.3 = bf16[1,256,768]{2,1,0:T(8,128)(2,1)} collective-permute-done((bf16[1,256,768]{2,1,0:T(8,128)(2,1)}, bf16[1,256,768]{2,1,0:T(8,128)(2,1)}, u32[]{:S(2)}, u32[]{:S(2)}) %collective-permute-start.3) | collective-permute-done | bytes 393248 | tf_op jit(solution)/shard_map/ppermute | solution.py:178
  267.1 54.1 %conditional.11 = (f32[1,256,768]{2,1,0:T(8,128)S(1)}, f32[768,2304]{0,1:T(8,128)}, f32[768,768]{0,1:T(8,128)S(1)}, f32[768,4096]{0,1:T(8,128)}, f32[2048,768]{0...) conditional(s32[]{:T(128)} %convert_element_type.595, () %tuple.74, ...), branch_computations={%region_57.0_spmd.clone, %region_58.66_spmd.clone} | conditional | flops 8144546816 | bytes 191601136 | solution.py:413
  270.3 4.3 fusion.303
  303.0 4.8 convolution_bitcast_fusion.24
  307.8 5.2 convolution_bitcast_fusion.23
  313.1 7.6 %convolution_bitcast_fusion.22 = f32[768,4096]{0,1:T(8,128)} fusion(bf16[256,768]{1,0:T(8,128)(2,1)} %get-tuple-element.868, bf16[256,2048]{1,0:T(8,128)(2,1)S(1)} %copy-done.129, bf16[256,2048]{1,0:T(8,128)(2,1)S(1)} %copy-done.127), kind=kOutput, calls=%fused_computation.468 | convolution fusion | flops 1614807040 | bytes 15073280 | tf_op jit(solution)/shard_map/cond/branch_1_fun/dot_general | solution.py:206
  331.2 16.7 %add_convert_fusion = bf16[768,4096]{0,1:T(8,128)(2,1)S(1)} fusion(f32[768,4096]{0,1:T(8,128)} %copy-done.11, f32[768,4096]{0,1:T(8,128)} %get-tuple-element.686, f32[768,4096]{0,1:T(8,128)} %get-tuple-element.1182, f32[768,4096]{0,1:T(8,128)} %get-tuple-element.675), kind=kLoop, calls=%fused_computation.548 | loop fusion | flops 12582912 | bytes 56623104 | tf_op jit(solution)/shard_map/convert.58
  351.6 10.6 %add_convert_fusion.2 = bf16[2048,768]{0,1:T(8,128)(2,1)S(1)} fusion(f32[2048,768]{0,1:T(8,128)} %copy-done.28, f32[2048,768]{0,1:T(8,128)} %get-tuple-element.687, f32[2048,768]{0,1:T(8,128)} %get-tuple-element.1183, f32[2048,768]{0,1:T(8,128)} %get-tuple-element.676), kind=kLoop, calls=%fused_computation.550 | loop fusion | flops 6291456 | bytes 28311552 | tf_op jit(solution)/shard_map/convert.50
  366.2 9.9 %add_convert_fusion.1 = bf16[768,2304]{0,1:T(8,128)(2,1)S(1)} fusion(f32[768,2304]{0,1:T(8,128)} %copy-done.19, f32[768,2304]{0,1:T(8,128)} %get-tuple-element.684, f32[768,2304]{0,1:T(8,128)} %get-tuple-element.1180, f32[768,2304]{0,1:T(8,128)} %get-tuple-element.673), kind=kLoop, calls=%fused_computation.549 | loop fusion | flops 7077888 | bytes 31850496 | tf_op jit(solution)/shard_map/convert.61
  377.8 4.4 add_convert_fusion.3
  420.3 125.4 %shard_map.290 = (f32[48,768]{1,0:T(8,128)}, f32[48,768]{1,0:T(8,128)}, f32[48,768]{1,0:T(8,128)}, f32[48,768]{1,0:T(8,128)}, f32[48,512]{1,0:T(8,128)}, /*index...) custom-call(bf16[4,2,2,48,768]{4,3,2,1,0:T(8,128)(2,1)} %bitcast.898, ...), custom_call_target="tpu_custom_call" | custom-call | tf_op jit(solution)/shard_map/pallas_call | solution.py:153
  556.9 39.2 %psum.47 = f32[32,12]{0,1:T(8,128)} all-reduce(f32[32,12]{0,1:T(8,128)S(1)} %add_add_fusion), channel_id=1, replica_groups=mesh['section'=2,'dp'=16] {'section','dp'}, use_global_device_ids=true, to_apply=%region_72.73 | all-reduce | flops 384 | bytes 3072 | tf_op jit(solution)/shard_map/psum | solution.py:635
  597.0 5.2 all-reduce
  603.7 17.2 %all-reduce.4.cloned.1.call-done = (bf16[48,768]{1,0:T(8,128)(2,1)}, bf16[48,1536]{1,0:T(8,128)(2,1)}, bf16[48,768]{1,0:T(8,128)(2,1)}) async-done(((bf16[48,768]{1,0:T(8,128)(2,1)}, bf16[48,1536]{1,0:T(8,128)(2,1)}, bf16[48,768]{1,0:T(8,128)(2,1)}), (bf16[48,768]{1,0:T(8,128)(2,1)}, bf16[48,1536]{1,0:T(8,128)(2,1)}, bf16[48,768]{1,0:T(8,128)(2,1)})) %all-reduce.4.cloned.1.call-update) | async-done | bytes 294928 | tf_op jit(solution)/shard_map/psum | solution.py:629
  (422 shorter events, 245.3 us)
Async XLA Ops:
  8.1 588.1 %reduce-scatter.4.cloned.1.call-start = ((), (), s32[]{:S(2)}) async-start(), calls=%async_computation.1 | async-start | bytes 417792
  11.9 40.2 %copy-start.12 = (f32[1,256,768]{2,1,0:T(8,128)}, f32[1,256,768]{2,1,0:T(8,128)S(1)}, u32[]{:S(2)}) copy-start(f32[1,256,768]{2,1,0:T(8,128)S(1)} %get-tuple-element.1312) | copy-start | bytes 2359300
  12.2 6.5 %copy-start.200 = (f32[256]{0:T(256)}, f32[256]{0:T(256)S(1)}, u32[]{:S(2)}) copy-start(f32[256]{0:T(256)S(1)} %add_rsqrt_fusion.2) | copy-start | bytes 3076 | tf_op jit(solution)/shard_map/cond
  50.1 51.7 %collective-permute-start = (bf16[1,256,768]{2,1,0:T(8,128)(2,1)}, bf16[1,256,768]{2,1,0:T(8,128)(2,1)}, u32[]{:S(2)}, u32[]{:S(2)}) collective-permute-start(bf16[1,256,768]{2,1,0:T(8,128)(2,1)} %get-tuple-element.539), channel_id=1, source_target_pairs={{0,16},{1,17},{2,18},{3,19},{4,20},{5,21},{6,22},{7,23},{8,24},{9,... | collective-permute-start | bytes 1179656 | tf_op jit(solution)/shard_map/ppermute | solution.py:178
  75.2 7.7 %slice-start.2 = ((s8[6291456]{0:T(1024)(128)(4,1)}), s8[4194304]{0:T(1024)(128)(4,1)S(1)}, s32[]{:S(2)}) async-start(s8[6291456]{0:T(1024)(128)(4,1)} %bitcast.844), calls=%async_computation.5 | async-start | bytes 8388608 | tf_op jit(solution)/shard_map/cond
  75.7 7.3 %slice-start.3 = ((s8[6291456]{0:T(1024)(128)(4,1)}), s8[2097152]{0:T(1024)(128)(4,1)S(1)}, s32[]{:S(2)}) async-start(s8[6291456]{0:T(1024)(128)(4,1)} %bitcast.844), calls=%async_computation.6 | async-start | bytes 4194304 | tf_op jit(solution)/shard_map/cond
  96.4 5.4 copy-start.65
  96.4 5.4 copy-start.130
  96.4 5.4 copy-start.137
  96.4 5.4 copy-start.169
  96.4 5.4 copy-start.204
  96.4 34.0 %collective-permute-start.1 = (bf16[1,256,768]{2,1,0:T(8,128)(2,1)}, bf16[1,256,768]{2,1,0:T(8,128)(2,1)}, u32[]{:S(2)}, u32[]{:S(2)}) collective-permute-start(bf16[1,256,768]{2,1,0:T(8,128)(2,1)} %get-tuple-element.541), channel_id=1, source_target_pairs={{0,16},{1,17},{2,18},{3,19},{4,20},{5,21},{6,22},{7,23},{8,24},{9,... | collective-permute-start | bytes 1179656 | tf_op jit(solution)/shard_map/ppermute | solution.py:178
  129.1 47.9 %collective-permute-start.2 = (bf16[1,256,768]{2,1,0:T(8,128)(2,1)}, bf16[1,256,768]{2,1,0:T(8,128)(2,1)}, u32[]{:S(2)}, u32[]{:S(2)}) collective-permute-start(bf16[1,256,768]{2,1,0:T(8,128)(2,1)} %get-tuple-element.653), channel_id=1, source_target_pairs={{16,0},{17,1},{18,2},{19,3},{20,4},{21,5},{22,6},{23,7},{24,8},{25... | collective-permute-start | bytes 1179656 | tf_op jit(solution)/shard_map/ppermute | solution.py:178
  147.2 6.6 %copy-start.19 = (f32[768,2304]{0,1:T(8,128)}, f32[768,2304]{0,1:T(8,128)S(1)}, u32[]{:S(2)}) copy-start(f32[768,2304]{0,1:T(8,128)S(1)} %get-tuple-element.1184) | copy-start | bytes 21233668
  147.2 9.1 %copy-start.28 = (f32[2048,768]{0,1:T(8,128)}, f32[2048,768]{0,1:T(8,128)S(1)}, u32[]{:S(2)}) copy-start(f32[2048,768]{0,1:T(8,128)S(1)} %get-tuple-element.1187) | copy-start | bytes 18874372
  147.2 11.3 %copy-start.173 = (f32[32,12]{0,1:T(8,128)}, f32[32,12]{0,1:T(8,128)S(1)}, u32[]{:S(2)}) copy-start(f32[32,12]{0,1:T(8,128)S(1)} %get-tuple-element.668) | copy-start | bytes 4612
  147.2 11.3 %copy-start.187 = (f32[768]{0:T(1024)}, f32[768]{0:T(1024)S(1)}, u32[]{:S(2)}) copy-start(f32[768]{0:T(1024)S(1)} %get-tuple-element.662) | copy-start | bytes 9220
  147.2 118.8 %collective-permute-start.3 = (bf16[1,256,768]{2,1,0:T(8,128)(2,1)}, bf16[1,256,768]{2,1,0:T(8,128)(2,1)}, u32[]{:S(2)}, u32[]{:S(2)}) collective-permute-start(bf16[1,256,768]{2,1,0:T(8,128)(2,1)} %get-tuple-element.669), channel_id=1, source_target_pairs={{16,0},{17,1},{18,2},{19,3},{20,4},{21,5},{22,6},{23,7},{24,8},{25... | collective-permute-start | bytes 1179656 | tf_op jit(solution)/shard_map/ppermute | solution.py:178
  153.8 24.3 %copy-start.5 = (bf16[1,768,768]{2,1,0:T(8,128)(2,1)S(1)}, bf16[1,768,768]{2,1,0:T(8,128)(2,1)}, u32[]{:S(2)}) copy-start(bf16[1,768,768]{2,1,0:T(8,128)(2,1)} %param.39) | copy-start | bytes 3538948
  153.8 24.3 %copy-start.32 = (f32[1,256,768]{2,1,0:T(8,128)S(1)}, f32[1,256,768]{2,1,0:T(8,128)}, u32[]{:S(2)}) copy-start(f32[1,256,768]{2,1,0:T(8,128)} %get-tuple-element.1309) | copy-start | bytes 2359300
  153.8 24.3 %copy-start.138 = (f32[32,12]{0,1:T(8,128)S(1)}, f32[32,12]{0,1:T(8,128)}, u32[]{:S(2)}) copy-start(f32[32,12]{0,1:T(8,128)} %param.35) | copy-start | bytes 4612
  178.1 89.0 %copy-start.29 = (f32[1,256,768]{2,1,0:T(8,128)S(1)}, f32[1,256,768]{2,1,0:T(8,128)}, u32[]{:S(2)}) copy-start(f32[1,256,768]{2,1,0:T(8,128)} %get-tuple-element.1310) | copy-start | bytes 2359300
  180.3 7.0 %slice-start.8 = ((s8[6291456]{0:T(1024)(128)(4,1)}), s8[4194304]{0:T(1024)(128)(4,1)S(1)}, s32[]{:S(2)}) async-start(s8[6291456]{0:T(1024)(128)(4,1)} %bitcast.850), calls=%async_computation.11 | async-start | bytes 8388608 | tf_op jit(solution)/shard_map/cond
  181.3 8.5 %copy-start.57 = (f32[1,256,768]{2,1,0:T(8,128)}, f32[1,256,768]{2,1,0:T(8,128)S(1)}, u32[]{:S(2)}) copy-start(f32[1,256,768]{2,1,0:T(8,128)S(1)} %subtract_multiply_fusion) | copy-start | bytes 2359300 | tf_op jit(solution)/shard_map/cond
  181.3 6.0 slice-start.9
  181.3 6.0 copy-start.88
  269.3 6.3 slice-start.10
  313.1 7.6 %copy-start.56 = (f32[768,768]{0,1:T(8,128)S(1)}, f32[768,768]{0,1:T(8,128)}, u32[]{:S(2)}) copy-start(f32[768,768]{0,1:T(8,128)} %convolution_bitcast_fusion.25) | copy-start | bytes 7077892 | tf_op jit(solution)/shard_map/cond
  387.4 233.5 %all-reduce.4.cloned.1.call-start = ((), (), s32[]{:S(2)}) async-start(), calls=%async_computation.2 | async-start | bytes 589824 | tf_op jit(solution)/shard_map/psum | solution.py:629
  420.3 128.3 %copy-start.93 = (f32[1,256,768]{2,1,0:T(8,128)S(1)}, f32[1,256,768]{2,1,0:T(8,128)}, u32[]{:S(2)}) copy-start(f32[1,256,768]{2,1,0:T(8,128)} %copy-done.92) | copy-start | bytes 2359300
  553.1 72.6 %copy-start.153 = (f32[48,768]{1,0:T(8,128)S(1)}, f32[48,768]{1,0:T(8,128)}, u32[]{:S(2)}) copy-start(f32[48,768]{1,0:T(8,128)} %get-tuple-element.604) | copy-start | bytes 442372
  555.6 70.8 %copy-start.193 = (f32[48,4096]{1,0:T(8,128)}, f32[48,4096]{1,0:T(8,128)S(1)}, u32[]{:S(2)}) copy-start(f32[48,4096]{1,0:T(8,128)S(1)} %constant_dynamic-update-slice_fusion) | copy-start | bytes 2359300
  (87 other events, 255.9 us)
Sparse Core Ops, SparseCore 0:
  387.6 58.8 reduce-scatter.3
Sparse Core Ops, SparseCore 1:
  596.2 24.7 all-reduce.3

commit v2 on v0

v2 whole, which is shorter than its diff:
```python
import functools
import math
import types

import jax
import jax.numpy as jnp
import numpy as np
from jax import lax
from jax.experimental import pallas as pl
from jax.experimental.pallas import tpu as pltpu
from jax.sharding import PartitionSpec as P

H = 12
HD = 64
NBUCKET = 32
MAXDIST = 128
EPSILON = 1e-06
MASKED = -1000000000.0
MESH = pl.DeviceIdType.MESH
PRECISE = lax.Precision.HIGHEST
HALF = jnp.bfloat16
FULL = jnp.float32
PAIRS = H // 2
CHUNK = 256
BLOCK = 64
GATE_UP, DOWN, CROSS, SELF = range(4)
GELU_SCALE = math.sqrt(2.0 / math.pi)
GELU_CUBE = 0.044715


def bucket_of(offsets, causal, buckets, reach_max):
    if causal:
        half_count = buckets
        side_offset = offsets * 0
        distance = np.maximum(-offsets, 0)
    else:
        half_count = buckets // 2
        side_offset = (offsets > 0).astype(np.int32) * half_count
        distance = np.abs(offsets)
    exact_count = half_count // 2
    clipped = np.maximum(distance, exact_count)
    spread = exact_count + np.floor(
        np.log(clipped / exact_count) / np.log(reach_max / exact_count) * (half_count - exact_count)
        + 1e-09
    ).astype(np.int32)
    spread = np.minimum(spread, half_count - 1)
    return (side_offset + np.where(distance < exact_count, distance, spread)).astype(np.int32)


def bucket_tables(length):
    lane = np.arange(length)
    spread = np.concatenate([-lane, length - lane])
    summed = np.concatenate([-(lane + 1), length - 1 - lane])
    tables = []
    for offsets in (spread, summed):
        clipped = np.clip(offsets, -(length - 1), length - 1)
        tables.append(
            np.stack(
                [
                    (bucket_of(clipped, causal, NBUCKET, MAXDIST)[None] == np.arange(NBUCKET)[:, None])
                    for causal in (False, True)
                ]
            ).astype(np.float32)
        )
    return tables


def dot(left, right):
    return jnp.dot(left, right, preferred_element_type=FULL)


def dot_inner(left, right):
    return lax.dot_general(left, right, (((0,), (0,)), ((), ())), preferred_element_type=FULL)


def dot_outer(left, right):
    return lax.dot_general(left, right, (((1,), (1,)), ((), ())), preferred_element_type=FULL)


def repeat(count, step):
    def body(index, carry):
        step(index)
        return carry

    lax.fori_loop(0, count, body, 0)


def at128(index, scale):
    return pl.multiple_of(index * scale, 128)


class Group:
    def __init__(self, name, count, rows, cols):
        self.name, self.count, self.rows, self.cols = name, count, rows, cols


def layer_kernel(names, groups, reduce, rows, length, width, hidden, *refs):
    v = types.SimpleNamespace(**dict(zip(names, refs)))
    tokens = rows * length
    chunks = hidden // CHUNK
    ways_rows = width // 16
    me, section = lax.axis_index("dp"), lax.axis_index("section")
    encoder, decoder = section == 0, section == 1
    z, y, c = me // 4, (me // 2) % 2, me % 2
    other = (1 - section, me)

    x_send, x_recv = v.x_send, v.x_recv
    low, low_t = v.low, v.low_t
    unit_ffn, unit_mid, cot = v.unit_ffn, v.unit_mid, v.cot
    grad_mix = cot
    res, grad = v.res, v.grad
    w_att, w_out, w_pair, w_lower = v.w_att, v.w_out, v.w_pair, v.w_lower
    qkv_self, qkv_cross = v.qkv_self, v.qkv_cross
    mix_self, mix_cross = v.mix_self, v.mix_cross
    probs, big = v.probs, v.big
    inverse, table, sums = v.inverse, v.table, v.sums
    joint, wide, narrow = v.joint, v.wide, v.narrow
    bias = [wide.at[e * length : (e + 1) * length, :length] for e in range(2)]
    mask = [wide.at[row * length : (row + 1) * length, length : 2 * length] for row in range(rows)]
    misc = v.misc
    load, sem_x, sem_misc, sem_out = v.load, v.sem_x, v.sem_misc, v.sem_out

    def device(zz, yy, cc):
        return (section, zz * 4 + yy * 2 + cc)

    partners = [other]
    if reduce:
        sibling, beside = device(z, y, 1 - c), device(z, 1 - y, c)
        peer_z = [(z + d) % 4 for d in (1, 2, 3)]
        partners += [sibling, beside] + [device(p, y, c) for p in peer_z]
    barrier = pltpu.get_barrier_semaphore()
    for target in partners:
        pl.semaphore_signal(barrier, inc=1, device_id=target, device_id_type=MESH)

    def copy_in(source, target, slot):
        return pltpu.make_async_copy(source, target, load.at[slot])

    def load_x():
        return copy_in(v.inputs, x_send, 0)

    def load_cot():
        return copy_in(v.cotangent, cot, 1)

    def load_att():
        return copy_in(v.w_qkv.at[0], w_att, 2)

    def load_out():
        return copy_in(v.w_attn_out.at[0], w_out, 3)

    def load_cross():
        return [
            copy_in(v.cross_query, w_att.at[:, pl.ds(0, width)], 2),
            copy_in(v.cross_kv, w_att.at[:, pl.ds(width, 2 * width)], 4),
        ]

    def load_cross_out():
        return copy_in(v.cross_out, w_out, 3)

    def load_chunk(index):
        slot = index % 2
        at = at128(index, CHUNK)
        return [
            copy_in(
                v.w_gate_up.at[0, :, pl.ds(at, CHUNK)], w_pair.at[slot, :, pl.ds(0, CHUNK)], 5 + slot
            ),
            copy_in(
                v.w_gate_up.at[0, :, pl.ds(pl.multiple_of(hidden + at, 128), CHUNK)],
                w_pair.at[slot, :, pl.ds(CHUNK, CHUNK)],
                7 + slot,
            ),
            copy_in(v.w_down.at[0, pl.ds(at, CHUNK), :], w_lower.at[slot], 9 + slot),
        ]

    load_x().start()
    load_att().start()
    load_out().start()
    load_cot().start()
    for copy in load_chunk(0):
        copy.start()

    by_name = {group.name: group for group in groups}
    stacks = {
        group.name: (big if group.name == SELF else getattr(v, f"own{group.name}")) for group in groups
    }

    def block_place(shard):
        if not reduce:
            return shard
        return (shard % 2) * 8 + ((shard // 2) % 2) * 4 + shard // 4

    def put(name, item, columns, tile):
        own, r = stacks[name], by_name[name].rows
        low_tile = tile.astype(HALF)
        for shard in range(16):
            own[item, block_place(shard) * r : (block_place(shard) + 1) * r, columns] = low_tile[
                shard * r : (shard + 1) * r
            ]

    def send_first(name, i):
        r = by_name[name].rows
        return pltpu.make_async_remote_copy(
            stacks[name].at[i, pl.ds(pl.multiple_of((1 - c) * 8 * r, 16), 8 * r)],
            getattr(v, f"first{name}").at[i],
            getattr(v, f"sem{name}").at[i, 0],
            getattr(v, f"sem{name}").at[i, 1],
            device_id=sibling,
            device_id_type=MESH,
        )

    def send_second(name, i):
        r = by_name[name].rows
        return pltpu.make_async_remote_copy(
            stacks[name].at[i, pl.ds(pl.multiple_of(c * 8 * r + (1 - y) * 4 * r, 16), 4 * r)],
            getattr(v, f"second{name}").at[i],
            getattr(v, f"sem{name}").at[i, 2],
            getattr(v, f"sem{name}").at[i, 3],
            device_id=beside,
            device_id_type=MESH,
        )

    def send_third(name, i, d):
        r = by_name[name].rows
        return pltpu.make_async_remote_copy(
            stacks[name].at[i, pl.ds(pl.multiple_of(c * 8 * r + y * 4 * r + peer_z[d] * r, 16), r)],
            getattr(v, f"third{name}").at[i, d],
            getattr(v, f"sem{name}").at[i, 4 + d],
            getattr(v, f"sem{name}").at[i, 7 + d],
            device_id=device(peer_z[d], y, c),
            device_id_type=MESH,
        )

    def kept_rows(name):
        r = by_name[name].rows
        return pl.ds(pl.multiple_of(c * 8 * r + y * 4 * r + z * r, 16), r)

    def write_out(name, i):
        if reduce:
            source = stacks[name].at[i, kept_rows(name)]
        else:
            source = stacks[name].at[i]
        return pltpu.make_async_copy(source, getattr(v, f"out{name}").at[i], getattr(v, f"sem{name}").at[i, 10])

    def cross_over(i):
        return pltpu.make_async_remote_copy(
            stacks[CROSS].at[i, kept_rows(CROSS)],
            v.out2.at[i],
            v.sem2.at[i, 11],
            v.sem2.at[i, 12],
            device_id=other,
            device_id_type=MESH,
        )

    def begin(name, i):
        if reduce:
            send_first(name, i).start()
        else:
            write_out(name, i).start()

    def add_first(name, i):
        if not reduce:
            return
        own, first, r = stacks[name], getattr(v, f"first{name}"), by_name[name].rows
        send_first(name, i).wait_recv()

        def step(m):
            kept = pl.ds(pl.multiple_of(c * 8 * r + m * r, 16), r)
            own[i, kept] = own[i, kept] + first[i, pl.ds(pl.multiple_of(m * r, 16), r)]

        repeat(8, step)
        send_second(name, i).start()

    def add_second(name, i):
        if not reduce:
            return
        own, second, r = stacks[name], getattr(v, f"second{name}"), by_name[name].rows
        send_second(name, i).wait_recv()

        def step(m):
            kept = pl.ds(pl.multiple_of(c * 8 * r + y * 4 * r + m * r, 16), r)
            own[i, kept] = own[i, kept] + second[i, pl.ds(pl.multiple_of(m * r, 16), r)]

        repeat(4, step)
        for d in range(3):
            send_third(name, i, d).start()

    def add_third(name, i):
        if reduce:
            own, third = stacks[name], getattr(v, f"third{name}")
            for d in range(3):
                send_third(name, i, d).wait_recv()
            kept = kept_rows(name)
            total = (own[i, kept].astype(FULL) + third[i, 0].astype(FULL)) + (
                third[i, 1].astype(FULL) + third[i, 2].astype(FULL)
            )
            own[i, kept] = total.astype(HALF)
            write_out(name, i).start()
            if name == CROSS:
                cross_over(i).start()

    def finish(name, i):
        write_out(name, i).wait()
        if reduce:
            send_first(name, i).wait_send()
            send_second(name, i).wait_send()
            for d in range(3):
                send_third(name, i, d).wait_send()
            if name == CROSS:
                cross_over(i).wait_send()

    def block_of(ref, b):
        return ref.at[b // 9, pl.ds(at128((b % 9) // 3, 256), 256), pl.ds(at128(b % 3, 256), 256)]

    def self_probs(head, row):
        return probs.at[head * rows + row]

    def cross_probs(head, row):
        return block_of(big, head * rows + row)

    def row_slice(row):
        return slice(row * length, (row + 1) * length)

    lanes = lax.broadcasted_iota(jnp.int32, (1, 128), 1)
    half_lanes = [(lanes < HD).astype(HALF), (lanes >= HD).astype(HALF)]

    def make_mask(key_segments, query_segments, causal):
        for row in range(rows):
            keys = jnp.broadcast_to(key_segments[row : row + 1].astype(FULL), (8, length)).T[:, :1]
            queries = query_segments[row : row + 1].astype(FULL)
            same = keys == queries
            if causal is not None:
                key_at = lax.broadcasted_iota(jnp.int32, (length, length), 0)
                query_at = lax.broadcasted_iota(jnp.int32, (length, length), 1)
                same = same & ((key_at <= query_at) | causal)
            mask[row][...] = jnp.where(same, 0.0, MASKED).astype(FULL)

    def attend(qkv, probs_of, mix, with_bias):
        def pair(hp):
            if with_bias:
                key_at = lax.broadcasted_iota(jnp.int32, (length, length), 0)
                lane = lax.broadcasted_iota(jnp.int32, (length, length), 1)
                for e in range(2):
                    line = table[pl.ds(hp * 2 + e, 1), :]
                    skewed = jnp.where(
                        lane + key_at < length,
                        jnp.broadcast_to(line[:, :length], (length, length)),
                        jnp.broadcast_to(line[:, length:], (length, length)),
                    )
                    bias[e][...] = pltpu.roll(skewed, 0, 1, stride=1, stride_axis=0)
            for row in range(rows):
                at = row_slice(row)
                queries = qkv[at, pl.ds(at128(hp, 128), 128)]
                keys = qkv[at, pl.ds(pl.multiple_of(width + hp * 128, 128), 128)]
                values_t = qkv[at, pl.ds(pl.multiple_of(2 * width + hp * 128, 128), 128)].T
                for e in range(2):
                    scores = dot_outer(keys * half_lanes[e], queries)
                    soft_parts = []
                    for part in range(length // 128):
                        n = slice(part * 128, (part + 1) * 128)
                        shifted = scores[:, n] + mask[row][:, n]
                        if with_bias:
                            shifted = shifted + bias[e][:, n]
                        raised = jnp.exp(shifted - jnp.max(shifted, 0, keepdims=True))
                        total = jnp.sum(raised, 0, keepdims=True)
                        soft_parts.append((raised * (1.0 / total)).astype(HALF))
                    softmaxed = jnp.concatenate(soft_parts, 1)
                    probs_of(hp * 2 + e, row)[...] = softmaxed
                    mixed = dot(values_t[e * HD : (e + 1) * HD], softmaxed)
                    mix[pl.ds(pl.multiple_of(hp * 128 + e * HD, 16), HD), at] = mixed.astype(HALF)

        repeat(PAIRS, pair)

    def attend_back(qkv, probs_of, with_bias):
        upper = lax.broadcasted_iota(jnp.int32, (128, length), 0) < HD
        left = lax.broadcasted_iota(jnp.int32, (length, 128), 1) < HD
        if with_bias:
            row_at = lax.broadcasted_iota(jnp.int32, (length, length), 0)
            lane_at = lax.broadcasted_iota(jnp.int32, (length, length), 1)
            flip = (row_at + lane_at == length - 1).astype(FULL).astype(HALF)

        def pair(hp):
            turned = [None, None]
            for row in range(rows):
                at = row_slice(row)
                q_lanes = pl.ds(at128(hp, 128), 128)
                k_lanes = pl.ds(pl.multiple_of(width + hp * 128, 128), 128)
                v_lanes = pl.ds(pl.multiple_of(2 * width + hp * 128, 128), 128)
                queries, keys, values = qkv[at, q_lanes], qkv[at, k_lanes], qkv[at, v_lanes]
                outer = grad_mix[at, q_lanes]
                keys_t = keys.T
                parts = []
                for e in range(2):
                    soft_low = probs_of(hp * 2 + e, row)[...]
                    grad_soft = dot_outer(values * half_lanes[e], outer)
                    score_parts = []
                    for part in range(length // 128):
                        n = slice(part * 128, (part + 1) * 128)
                        soft = soft_low[:, n].astype(FULL)
                        weighted = soft * grad_soft[:, n]
                        shared = jnp.sum(weighted, 0, keepdims=True)
                        score_parts.append((weighted - soft * shared).astype(HALF))
                    scores = jnp.concatenate(score_parts, 1)
                    parts.append((dot(keys_t, scores), dot(scores, queries), dot(soft_low, outer)))
                    if with_bias:
                        more = dot(flip, scores)
                        turned[e] = more if turned[e] is None else turned[e] + more
                qkv[at, q_lanes] = jnp.where(upper, parts[0][0], parts[1][0]).T.astype(HALF)
                qkv[at, k_lanes] = jnp.where(left, parts[0][1], parts[1][1]).astype(HALF)
                qkv[at, v_lanes] = jnp.where(left, parts[0][2], parts[1][2]).astype(HALF)
            if with_bias:
                for e in range(2):
                    aligned = pltpu.roll(turned[e], 0, 1, stride=1, stride_axis=0)
                    before = jnp.sum(jnp.where(lane_at < row_at, aligned, 0.0), 0, keepdims=True)
                    after = jnp.sum(jnp.where(lane_at < row_at, 0.0, aligned), 0, keepdims=True)
                    sums[pl.ds(hp * 2 + e, 1), :length] = before
                    sums[pl.ds(hp * 2 + e, 1), length:] = after

        repeat(PAIRS, pair)

    blocks = tokens // BLOCK

    def row_block(b):
        return pl.ds(pl.multiple_of(b * BLOCK, BLOCK), BLOCK)

    def normalise(load_rows, column, gain, unit_ref, target):
        def step(b):
            at = row_block(b)
            value = load_rows(at)
            scale = lax.rsqrt(jnp.mean(value * value, -1, keepdims=True) + EPSILON)
            inverse[at, column : column + 1] = scale
            unit = value * scale
            if unit_ref is not None:
                unit_ref[at, :] = unit.astype(HALF)
            target[at, :] = (unit * gain).astype(HALF)

        repeat(blocks, step)

    def norm_back(load_grad, load_unit, column, gain, misc_row, load_base, copy_low):
        def step(b, gain_sum):
            at = row_block(b)
            normed, unit = load_grad(at), load_unit(at)
            weighted = normed * unit
            grad_unit = normed * gain
            scale = inverse[at, column : column + 1]
            inner = jnp.mean(weighted * gain, -1, keepdims=True)
            result = scale * (grad_unit - unit * inner)
            if load_base is not None:
                result = result + load_base(at)
            grad[at, :] = result
            if copy_low:
                low[at, :] = result.astype(HALF)
            return gain_sum + jnp.sum(weighted.reshape(BLOCK // 8, 8, width), 0)

        gain_sum = lax.fori_loop(0, blocks, step, jnp.zeros((8, width), FULL))
        misc[0, misc_row : misc_row + 1, :width] = jnp.sum(gain_sum, 0, keepdims=True)

    def transpose_into(target, source):
        if source.shape[0] == tokens:

            def step(b):
                at = pl.ds(at128(b, 128), 128)
                target[:, at] = source[at, :].T
        else:

            def step(b):
                at = pl.ds(at128(b, 128), 128)
                target[at, :] = source[:, at].T

        repeat(tokens // 128, step)

    def column_tiles(count, step):
        repeat(count, lambda j: step(pl.ds(at128(j, 256), 256)))

    def add_projection(weights, base):
        def step(columns):
            res[:, columns] = base[:, columns].astype(FULL) + dot(low[...], weights[:, columns])

        column_tiles(width // 256, step)

    def feed_forward(forward, backward, total, grad_result):
        if backward:
            total[...] = jnp.zeros_like(total)

        def step(k):
            slot = k % 2

            @pl.when(k + 1 < chunks)
            def _():
                for copy in load_chunk(k + 1):
                    copy.start()

            for copy in load_chunk(k):
                copy.wait()
            kept = [[block_of(big, k * 4 + 2 * part + side) for side in range(2)] for part in range(2)]
            half = tokens // 2
            if forward:
                for side in range(2):
                    n = slice(side * CHUNK, (side + 1) * CHUNK)
                    if backward:
                        wide[:, n] = dot(low[...], w_pair[slot, :, n])
                    else:
                        product = dot(low[...], w_pair[slot, :, n])
                        wide[:, n] = product
                        for part in range(2):
                            kept[part][side][...] = product[part * half : (part + 1) * half].astype(HALF)
            if backward:
                narrow[...] = dot_outer(grad_result[...], w_lower[slot])
            for part in range(2):

                def bend(b):
                    inside = pl.ds(pl.multiple_of(b * BLOCK, BLOCK), BLOCK)
                    at = pl.ds(pl.multiple_of(part * half + b * BLOCK, BLOCK), BLOCK)
                    if forward:
                        gate, up = wide[at, :CHUNK], wide[at, CHUNK:]
                    else:
                        gate = kept[part][0][inside, :].astype(FULL)
                        up = kept[part][1][inside, :].astype(FULL)
                    squared = gate * gate
                    curve = jnp.tanh(gate * (GELU_SCALE + GELU_SCALE * GELU_CUBE * squared))
                    rising = 0.5 + 0.5 * curve
                    bent = gate * rising
                    v.units[at, :] = (bent * up).astype(HALF)
                    if backward:
                        grad_hidden = narrow[at, :]
                        slope = rising + 0.5 * gate * (1.0 - curve * curve) * (
                            GELU_SCALE + 3.0 * GELU_SCALE * GELU_CUBE * squared
                        )
                        joint[at, :CHUNK] = (grad_hidden * up * slope).astype(HALF)
                        joint[at, CHUNK:] = (grad_hidden * bent).astype(HALF)

                repeat(half // BLOCK, bend)
            if forward:
                for j in range(width // 256):
                    n = slice(j * 256, (j + 1) * 256)
                    res[:, n] = res[:, n] + dot(v.units[...], w_lower[slot, :, n])
            if backward:
                r = by_name[DOWN].rows
                for part in range(3):
                    lower = dot_inner(v.units[...], grad_result[:, part * 256 : (part + 1) * 256])
                    lower = lower.astype(HALF)
                    if reduce:
                        for shard in range(CHUNK // r):
                            place = (shard % 2) * 8 + (k % 2) * 4 + k // 2
                            v.own1[part, pl.ds(pl.multiple_of(place * r, 16), r)] = lower[
                                shard * r : (shard + 1) * r
                            ]
                    else:
                        v.own1[part, pl.ds(at128(k, CHUNK), CHUNK)] = lower
                for part in range(2):
                    columns = slice(part * CHUNK, (part + 1) * CHUNK)
                    put(GATE_UP, k, columns, dot(low_t[...], joint[:, columns]))
                begin(GATE_UP, k)

                @pl.when(k > 0)
                def _():
                    add_first(GATE_UP, k - 1)

                for j in range(width // 256):
                    n = slice(j * 256, (j + 1) * 256)
                    total[:, n] = total[:, n] + dot_outer(joint[...], w_pair[slot, n, :])

        repeat(chunks, step)
        if backward:
            for part in range(3):
                begin(DOWN, part)
            add_first(GATE_UP, chunks - 1)
            for part in range(3):
                add_first(DOWN, part)

    def weight_gradient(name, item, left_t, right, at):
        def step(j):
            tile = dot(left_t[...], right[:, pl.ds(pl.multiple_of(at + j * 256, 128), 256)])
            put(name, item, pl.ds(at128(j, 256), 256), tile)

        repeat(width // 256, step)
        begin(name, item)

    def back_through_out(mix, name):
        def step(j):
            n = pl.ds(at128(j, 256), 256)
            grad_mix[:, n] = dot_outer(low[...], w_out[n, :]).astype(HALF)

        repeat(width // 256, step)
        weight_gradient(name, 0, mix, low, 0)

    def as_full(ref):
        return lambda at: ref[at, :].astype(FULL)

    load_x().wait()
    normalise(as_full(x_send), 0, v.attn_norm[...].astype(FULL), None, low)
    load_att().wait()

    def project(columns):
        qkv_self[:, columns] = dot(low[...], w_att[:, columns]).astype(HALF)

    column_tiles(3 * width // 256, project)

    @pl.when(decoder)
    def _():
        for copy in load_cross():
            copy.start()

    segments = jnp.where(encoder, v.enc_segments[...], v.dec_segments[...])
    make_mask(segments, segments, encoder)
    table[0:H, :] = lax.dot_general(
        v.rel_bias[...],
        v.spread[section],
        (((0,), (0,)), ((), ())),
        precision=PRECISE,
        preferred_element_type=FULL,
    )
    attend(qkv_self, self_probs, mix_self, True)
    transpose_into(low, mix_self)
    load_out().wait()
    add_projection(w_out, x_send)

    @pl.when(decoder)
    def _():
        load_cross_out().start()

    def memory_copy(row):
        return pltpu.make_async_remote_copy(
            x_send.at[pl.ds(row * length, length)],
            x_recv.at[pl.ds(row * length, length)],
            sem_x.at[0, row],
            sem_x.at[1, row],
            device_id=other,
            device_id_type=MESH,
        )

    def memory_back(row):
        return pltpu.make_async_remote_copy(
            x_send.at[pl.ds(row * length, length)],
            x_recv.at[pl.ds(row * length, length)],
            sem_x.at[2, row],
            sem_x.at[3, row],
            device_id=other,
            device_id_type=MESH,
        )

    def write_layer():
        return pltpu.make_async_copy(x_send, v.layer_out, sem_out.at[0])

    pl.semaphore_wait(barrier, len(partners))
    ffn_gain = v.ffn_norm[...].astype(FULL)

    def enter_feed_forward():
        normalise(as_full(res), 1, ffn_gain, unit_ffn, low)
        transpose_into(low_t, low)

    @pl.when(encoder)
    def _():
        enter_feed_forward()
        feed_forward(True, False, None, None)
        for copy in load_chunk(0):
            copy.start()
        final_gain = v.final_norm[...].astype(FULL)
        normalise(as_full(res), 2, final_gain, unit_mid, x_send)
        for row in range(rows):
            memory_copy(row).start()
        write_layer().start()
        load_cot().wait()
        for row in range(rows):
            memory_back(row).wait_recv()

        def memory_grads(at):
            return cot[at, :].astype(FULL) + x_recv[at, :].astype(FULL)

        norm_back(memory_grads, as_full(unit_mid), 2, final_gain, 2, None, True)
        feed_forward(False, True, res, low)
        norm_back(as_full(res), as_full(unit_ffn), 1, ffn_gain, 1, as_full(grad), True)
        for row in range(rows):
            memory_copy(row).wait_send()

    @pl.when(decoder)
    def _():
        cross_gain = v.cross_norm[...].astype(FULL)
        normalise(as_full(res), 2, cross_gain, unit_mid, low)
        for copy in load_cross():
            copy.wait()

        def project_query(columns):
            qkv_cross[:, columns] = dot(low[...], w_att[:, columns]).astype(HALF)

        column_tiles(width // 256, project_query)
        make_mask(v.enc_segments[...], v.dec_segments[...], None)
        for row in range(rows):
            memory_copy(row).wait_recv()

        def project_memory(j):
            columns = pl.ds(pl.multiple_of(width + j * 256, 128), 256)
            qkv_cross[:, columns] = dot(x_recv[...], w_att[:, columns]).astype(HALF)

        repeat(2 * width // 256, project_memory)
        attend(qkv_cross, cross_probs, mix_cross, False)
        transpose_into(low, mix_cross)
        load_cross_out().wait()
        add_projection(w_out, res)
        enter_feed_forward()
        load_cot().wait()
        feed_forward(True, True, grad, cot)
        x_send[...] = res[...].astype(HALF)
        write_layer().start()
        norm_back(as_full(grad), as_full(unit_ffn), 1, ffn_gain, 1, as_full(cot), True)
        back_through_out(mix_cross, CROSS)
        load_out().start()
        attend_back(qkv_cross, cross_probs, False)
        write_layer().wait()

        def memory_grad(j):
            n = pl.ds(at128(j, 256), 256)
            x_send[:, n] = dot_outer(
                qkv_cross[:, pl.ds(width, 2 * width)], w_att[n, pl.ds(width, 2 * width)]
            ).astype(HALF)

        repeat(width // 256, memory_grad)
        for row in range(rows):
            memory_back(row).start()

        def query_grad(j):
            n = pl.ds(at128(j, 256), 256)
            res[:, n] = dot_outer(qkv_cross[:, pl.ds(0, width)], w_att[n, pl.ds(0, width)])

        repeat(width // 256, query_grad)
        load_att().start()

        def gained(b):
            at = pl.ds(at128(b, 128), 128)
            low_t[:, at] = (unit_mid[at, :].astype(FULL) * cross_gain).astype(HALF).T

        repeat(tokens // 128, gained)
        weight_gradient(CROSS, 1, low_t, qkv_cross, 0)
        transpose_into(low_t, x_recv)
        weight_gradient(CROSS, 2, low_t, qkv_cross, width)
        weight_gradient(CROSS, 3, low_t, qkv_cross, 2 * width)
        for item in range(4):
            add_first(CROSS, item)
        norm_back(as_full(res), as_full(unit_mid), 2, cross_gain, 2, as_full(grad), True)
        for row in range(rows):
            memory_back(row).wait_send()
        load_att().wait()
        load_out().wait()

    @pl.when(encoder)
    def _():
        write_layer().wait()

    load_x().start()
    back_through_out(mix_self, SELF)
    attend_back(qkv_self, self_probs, True)
    load_x().wait()
    attn_gain = v.attn_norm[...].astype(FULL)

    def unit_self(at):
        return x_send[at, :].astype(FULL) * inverse[at, 0:1]

    def gained_self(b):
        at = pl.ds(at128(b, 128), 128)
        low_t[:, at] = (unit_self(at) * attn_gain).astype(HALF).T

    repeat(tokens // 128, gained_self)
    add_first(SELF, 0)
    for item in range(1, 4):
        weight_gradient(SELF, item, low_t, qkv_self, (item - 1) * width)
    for item in range(1, 4):
        add_first(SELF, item)

    def input_grad(j):
        n = pl.ds(at128(j, 256), 256)
        res[:, n] = dot_outer(qkv_self[...], w_att[n, :])

    repeat(width // 256, input_grad)
    norm_back(as_full(res), unit_self, 0, attn_gain, 0, as_full(grad), False)
    write_grad = pltpu.make_async_copy(grad, v.grad_inputs, sem_out.at[1])
    write_grad.start()
    misc[0, 0:H, width : width + NBUCKET] = lax.dot_general(
        sums[0:H, :],
        v.summed[section],
        (((1,), (1,)), ((), ())),
        precision=PRECISE,
        preferred_element_type=FULL,
    )

    def misc_copy(source, target, slot, to):
        return pltpu.make_async_remote_copy(
            misc.at[source],
            misc.at[target],
            sem_misc.at[slot, 0],
            sem_misc.at[slot, 1],
            device_id=to,
            device_id_type=MESH,
        )

    def misc_out(source, place, slot):
        return pltpu.make_async_copy(misc.at[source], v.out_misc.at[place], sem_out.at[slot])

    if reduce:
        first = misc_copy(0, 1, 0, sibling)
        first.start()
        first.wait_recv()
        misc[2] = misc[0] + misc[1]
        second = misc_copy(2, 3, 1, beside)
        second.start()

    def drain(name):
        count = by_name[name].count

        def step(i):
            add_second(name, i)

            @pl.when(i >= 2)
            def _():
                add_third(name, i - 2)

        repeat(count, step)
        for i in range(max(count - 2, 0), count):
            add_third(name, i)

    order = [GATE_UP, DOWN]
    for name in order:
        drain(name)

    @pl.when(decoder)
    def _():
        drain(CROSS)

    if reduce:
        second.wait_recv()
        misc[4 + z] = misc[2] + misc[3]
        thirds = [misc_copy(4 + z, 4 + z, 2 + d, device(peer_z[d], y, c)) for d in range(3)]
        for copy in thirds:
            copy.start()
    drain(SELF)
    if reduce:
        for d in range(3):
            came = misc_copy(4 + z, 4 + (z + 3 - d) % 4, 2 + d, device(peer_z[d], y, c))
            came.wait_recv()
        misc[8] = (misc[4] + misc[5]) + (misc[6] + misc[7])
        across = misc_copy(8, 9, 5, other)
        across.start()
        across.wait_recv()
        outs = [misc_out(8, section, 2), misc_out(9, 1 - section, 3)]
    else:
        outs = [misc_out(0, 0, 2)]
    for copy in outs:
        copy.start()
    for name in (GATE_UP, DOWN, SELF):
        repeat(by_name[name].count, functools.partial(finish, name))

    @pl.when(decoder)
    def _():
        repeat(by_name[CROSS].count, functools.partial(finish, CROSS))

    if reduce:

        @pl.when(encoder)
        def _():
            repeat(by_name[CROSS].count, lambda i: cross_over(i).wait_recv())

        for copy in [first, second, across] + thirds:
            copy.wait_send()
    for copy in outs:
        copy.wait()
    write_grad.wait()


def run_layers(args, ways):
    (
        inputs,
        cotangent,
        enc_segments,
        dec_segments,
        rel_bias,
        attn_norm,
        ffn_norm,
        w_qkv,
        w_attn_out,
        w_gate_up,
        w_down,
        cross_norm,
        cross_query,
        cross_kv,
        cross_out,
        final_norm,
    ) = args
    _, rows, length, width = inputs.shape
    hidden = w_down.shape[1]
    tokens = rows * length
    reduce = ways == 16
    spread, summed = bucket_tables(length)
    operands = dict(
        inputs=inputs.reshape(tokens, width),
        cotangent=cotangent.reshape(tokens, width),
        w_qkv=w_qkv,
        w_attn_out=w_attn_out,
        w_gate_up=w_gate_up,
        w_down=w_down,
        cross_query=cross_query,
        cross_kv=cross_kv,
        cross_out=cross_out,
    )
    small = dict(
        enc_segments=enc_segments,
        dec_segments=dec_segments,
        rel_bias=rel_bias,
        attn_norm=attn_norm,
        ffn_norm=ffn_norm,
        cross_norm=cross_norm.reshape(1, width),
        final_norm=final_norm.reshape(1, width),
        spread=jnp.asarray(spread),
        summed=jnp.asarray(summed),
    )
    block = width // 16
    groups = [
        Group(GATE_UP, hidden // CHUNK, block, 2 * CHUNK),
        Group(DOWN, 3, hidden // 16, 256),
        Group(CROSS, 4, block, width),
        Group(SELF, 4, block, width),
    ]
    outs = dict(
        layer_out=((tokens, width), HALF),
        grad_inputs=((tokens, width), FULL),
    )
    for g in groups:
        outs[f"out{g.name}"] = ((g.count, g.rows if reduce else 16 * g.rows, g.cols), HALF)
    outs[MISC] = ((2 if reduce else 1, 16, width + 128), FULL)
    scratch = dict(
        x_send=pltpu.VMEM((tokens, width), HALF),
        x_recv=pltpu.VMEM((tokens, width), HALF),
        low=pltpu.VMEM((tokens, width), HALF),
        low_t=pltpu.VMEM((width, tokens), HALF),
        unit_ffn=pltpu.VMEM((tokens, width), HALF),
        unit_mid=pltpu.VMEM((tokens, width), HALF),
        cot=pltpu.VMEM((tokens, width), HALF),
        res=pltpu.VMEM((tokens, width), FULL),
        grad=pltpu.VMEM((tokens, width), FULL),
        joint=pltpu.VMEM((tokens, 2 * CHUNK), HALF),
        w_att=pltpu.VMEM((width, 3 * width), HALF),
        w_out=pltpu.VMEM((width, width), HALF),
        w_pair=pltpu.VMEM((2, width, 2 * CHUNK), HALF),
        w_lower=pltpu.VMEM((2, CHUNK, width), HALF),
        qkv_self=pltpu.VMEM((tokens, 3 * width), HALF),
        qkv_cross=pltpu.VMEM((tokens, 3 * width), HALF),
        mix_self=pltpu.VMEM((width, tokens), HALF),
        mix_cross=pltpu.VMEM((width, tokens), HALF),
        probs=pltpu.VMEM((H * rows, length, length), HALF),
        big=pltpu.VMEM((4, width, width), HALF),
        inverse=pltpu.VMEM((tokens, 8), FULL),
        wide=pltpu.VMEM((tokens, 2 * CHUNK), FULL),
        narrow=pltpu.VMEM((tokens, CHUNK), FULL),
        units=pltpu.VMEM((tokens, CHUNK), HALF),
        table=pltpu.VMEM((16, 2 * length), FULL),
        sums=pltpu.VMEM((16, 2 * length), FULL),
        misc=pltpu.VMEM((10 if reduce else 1, 16, width + 128), FULL),
        load=pltpu.SemaphoreType.DMA((11,)),
        sem_x=pltpu.SemaphoreType.DMA((4, rows)),
        sem_misc=pltpu.SemaphoreType.DMA((6, 2)),
        sem_out=pltpu.SemaphoreType.DMA((4,)),
    )
    for g in groups:
        if g.name != SELF:
            scratch[f"own{g.name}"] = pltpu.VMEM((g.count, 16 * g.rows, g.cols), HALF)
        if reduce:
            scratch[f"first{g.name}"] = pltpu.VMEM((g.count, 8 * g.rows, g.cols), HALF)
            scratch[f"second{g.name}"] = pltpu.VMEM((g.count, 4 * g.rows, g.cols), HALF)
            scratch[f"third{g.name}"] = pltpu.VMEM((g.count, 3, g.rows, g.cols), HALF)
        scratch[f"sem{g.name}"] = pltpu.SemaphoreType.DMA((g.count, 13))
    names = list(operands) + list(small) + list(outs) + list(scratch)
    results = pl.pallas_call(
        functools.partial(layer_kernel, names, groups, reduce, rows, length, width, hidden),
        out_shape=[jax.ShapeDtypeStruct(*out) for out in outs.values()],
        in_specs=[pl.BlockSpec(memory_space=pl.ANY)] * len(operands)
        + [pl.BlockSpec(memory_space=pltpu.VMEM)] * len(small),
        out_specs=[pl.BlockSpec(memory_space=pl.ANY)] * len(outs),
        scratch_shapes=list(scratch.values()),
        compiler_params=pltpu.CompilerParams(
            collective_id=1, has_side_effects=True, vmem_limit_bytes=VMEM_LIMIT
        ),
    )(*operands.values(), *small.values())
    return dict(zip(outs, results)), reduce


LAYER, INPUT, MISC = "layer_out", "grad_inputs", "out_misc"
VMEM_LIMIT = 64 * 2**20 - 64 * 2**10


def shards(*args):
    inputs, rel_bias = args[0], args[4]
    ways = lax.axis_size("dp")
    _, rows, length, width = inputs.shape
    hidden = args[10].shape[1]
    out, reduce = run_layers(args, ways)

    def wide(name):
        value = out[f"out{name}"]
        if reduce:
            return value.astype(FULL)
        total = lax.psum_scatter(value, "dp", scatter_dimension=1, tiled=True)
        if name == CROSS:
            total = lax.psum(jnp.where(lax.axis_index("section") == 1, total, 0), "section")
        return total.astype(FULL)

    def side_by_side(value):
        return jnp.swapaxes(value, 0, 1).reshape(value.shape[1], -1)

    gate_up = wide(GATE_UP)
    chunks, block, _ = gate_up.shape
    gate_up = gate_up.reshape(chunks, block, 2, CHUNK).transpose(1, 2, 0, 3).reshape(block, 2 * hidden)
    down, cross, late = wide(DOWN), wide(CROSS), wide(SELF)
    misc = out[MISC]
    section = lax.axis_index("section")
    if not reduce:
        mine = lax.psum(misc[0], "dp")
        misc = lax.all_gather(mine, "section", axis=0)
    own = lax.dynamic_index_in_dim(misc, section, 0, keepdims=False)
    start = lax.axis_index("dp") * block

    def piece(vector):
        return lax.dynamic_slice_in_dim(vector, start, block, 0)

    rel = (misc[0] + misc[1])[:H, width : width + NBUCKET].T
    return (
        out[LAYER].reshape(inputs.shape),
        out[INPUT].reshape(inputs.shape),
        side_by_side(late[1:])[None],
        late[0][None],
        gate_up[None],
        side_by_side(down)[None],
        piece(own[0, :width])[None],
        piece(own[1, :width])[None],
        cross[1],
        side_by_side(cross[2:]),
        cross[0],
        piece(misc[1, 2, :width]),
        piece(misc[0, 2, :width]),
        rel,
    )


def solution(mesh):
    layer = P("section", "dp", None, None)
    matrix = P("section", None, None)
    return jax.shard_map(
        shards,
        mesh=mesh,
        in_specs=(layer, layer, P("dp", None), P("dp", None), P())
        + (P("section", None),) * 2
        + (matrix,) * 4
        + (P(),) * 5,
        out_specs=(layer, layer)
        + (P("section", "dp", None),) * 4
        + (P("section", "dp"),) * 2
        + (P("dp", None),) * 3
        + (P("dp"),) * 2
        + (P(),),
        check_vma=False,
    )
```

time: 1240 us -> 286 us (0.23)
  waiting for transfers between devices: 670 us -> 0 us
  Pallas kernels: 0 us -> 270 us
  local copies, waits for them, and re-layouts: 240 us -> 14.3 us
  other arithmetic: 122 us -> 1.08 us
  matrix products: 117 us -> 0 us
  blocking collectives: 46.7 us -> 0 us
  loops' own time: 14.8 us -> 0 us
  between operations: 14.8 us -> 0.77 us
    unnamed x3 -> x0, waiting for transfers between devices: 584 us -> none
    pallas_call x0 -> x1, Pallas kernels: none -> 270 us  [run_layers(): pl.pallas_call(functools.partial(layer_kernel, names, groups, reduce, row...]
    dot_general x44 -> x0, matrix products: 117 us -> none  [the longest x8 35.8 us: inner_rows(): lax.dot_general(left_side, right_side, (((0,), (0,)), ((), ())), preferre...]
    add x22 -> x1, other arithmetic: 80.1 us -> 0.01 us  [shards(): rel = (misc[0] + misc[1])[:H, width:width + NBUCKET].T]
    ppermute x4 -> x0, waiting for transfers between devices: 69.4 us -> none  [shifted(): return lax.ppermute(value, axis, pairs)]
    unnamed x101 -> x19, local copies, waits for them, and re-layouts: 60.5 us -> 4.37 us
    another operation x35 -> x5, local copies, waits for them, and re-layouts: 57.5 us -> 3.19 us  [the longest x3 1.97 us: shards(): gate_up[None]]
    psum x2 -> x0, blocking collectives: 46.7 us -> none  [the longest x1 41.8 us: shards(): rel_total = lax.psum(shard_rel, ('section', 'dp'))]
  transfers between devices with their start and end apart: 6 -> 0, of which waited for: 4 -> 0; matrix products, arithmetic and copies ran while one was open for 12% -> 0% of each run, Pallas kernels for 0% -> 0%
where the time goes in v2:
time: 286 us
  Pallas kernels  270 us (94%)
  local copies, waits for them, and re-layouts  14.3 us (5%)
    pallas_call x1, Pallas kernels, run_layers(): pl.pallas_call(functools.partial(layer_kernel, names, groups, reduce, row...  270 us

profile of v2, /device:TPU:0, one launch (start us, length us, event | category | flops | bytes accessed | tf_op | source)
XLA Modules:
  0.0 285.9 jit_solution(8510832135842572297)
XLA Ops:
  0.6 1.4 copy.34.refs_11_
  2.0 1.3 reshape.62.refs_14_
  3.3 1.3 reshape.63.refs_15_
  4.5 269.7 %shard_map.281 = (bf16[512,768]{1,0:T(8,128)(2,1)}, f32[512,768]{1,0:T(8,128)}, bf16[8,48,512]{2,1,0:T(8,128)(2,1)}, bf16[3,128,256]{2,1,0:T(8,128)(2,1)}, bf16[...) custom-call(bf16[512,768]{1,0:T(8,128)(2,1)} %bitcast.33, bf16[512,768]{1,0:T(8,128)(2,1)} %bitcast.34, ...), custom_call_target="tpu_custom_call" | custom-call | tf_op jit(solution)/shard_map/pallas_call | solution.py:968
  274.3 1.0 convert_element_type.8
  275.3 0.0 copy-start.2
  275.3 0.0 copy-start.3
  275.3 0.3 copy.35
  275.7 1.1 broadcast_in_dim_reshape.15
  276.7 0.0 copy-done.2
  276.7 0.7 slice.49
  277.4 0.0 copy-done.3
  277.4 0.5 reshape.70
  277.9 0.0 copy-start.6
  277.9 0.5 copy.36
  278.4 0.0 copy-start.5
  278.4 1.0 reshape.68
  279.4 0.0 copy-done.6
  279.4 0.2 copy.37
  279.6 0.9 copy.39
  280.5 0.0 copy-done.5
  280.6 0.6 constant_dynamic-slice_fusion.2
  281.1 0.0 copy-done.4
  281.2 0.0 copy-start
  281.2 0.7 slice_bitcast_fusion.2
  282.0 0.7 copy.40
  282.7 0.6 fusion
  283.3 0.6 slice_bitcast_fusion.4
  283.9 0.0 copy-done.1
  283.9 0.9 copy.43
  284.8 0.0 copy-done
  284.8 1.1 copy.44
  (9 shorter events, 0.1 us)
Async XLA Ops:
  275.3 1.4 copy-start.2
  275.3 2.1 copy-start.3
  277.9 1.5 copy-start.6
  278.4 2.2 copy-start.5
  279.4 1.8 copy-start.4
  280.5 3.4 %copy-start.1 = (bf16[512,768]{1,0:T(8,128)(2,1)S(1)}, bf16[512,768]{1,0:T(8,128)(2,1)}, u32[]{:S(2)}) copy-start(bf16[512,768]{1,0:T(8,128)(2,1)} %get-tuple-element.21) | copy-start | bytes 2359300
  281.2 3.6 %copy-start = (f32[512,768]{1,0:T(8,128)S(1)}, f32[512,768]{1,0:T(8,128)}, u32[]{:S(2)}) copy-start(f32[512,768]{1,0:T(8,128)} %get-tuple-element.22) | copy-start | bytes 4718596

commit v3 on v2

v3 whole, which is shorter than its diff:
```python
import functools
import math
import types

import jax
import jax.numpy as jnp
import numpy as np
from jax import lax
from jax.experimental import pallas as pl
from jax.experimental.pallas import tpu as pltpu
from jax.sharding import PartitionSpec as P

H = 12
HD = 64
NBUCKET = 32
MAXDIST = 128
EPSILON = 1e-06
MASKED = -1000000000.0
MESH = pl.DeviceIdType.MESH
PRECISE = lax.Precision.HIGHEST
HALF = jnp.bfloat16
FULL = jnp.float32
PAIRS = H // 2
CHUNK = 256
BLOCK = 64
UNROLL = 2
GATE_UP, DOWN, CROSS, SELF = range(4)
GELU_SCALE = math.sqrt(2.0 / math.pi)
GELU_CUBE = 0.044715


def bucket_of(offsets, causal, buckets, reach_max):
    if causal:
        half_count = buckets
        side_offset = offsets * 0
        distance = np.maximum(-offsets, 0)
    else:
        half_count = buckets // 2
        side_offset = (offsets > 0).astype(np.int32) * half_count
        distance = np.abs(offsets)
    exact_count = half_count // 2
    clipped = np.maximum(distance, exact_count)
    spread = exact_count + np.floor(
        np.log(clipped / exact_count) / np.log(reach_max / exact_count) * (half_count - exact_count)
        + 1e-09
    ).astype(np.int32)
    spread = np.minimum(spread, half_count - 1)
    return (side_offset + np.where(distance < exact_count, distance, spread)).astype(np.int32)


def bucket_tables(length):
    lane = np.arange(length)
    spread = np.concatenate([-lane, length - lane])
    summed = np.concatenate([-(lane + 1), length - 1 - lane])
    tables = []
    for offsets in (spread, summed):
        clipped = np.clip(offsets, -(length - 1), length - 1)
        tables.append(
            np.stack(
                [
                    (bucket_of(clipped, causal, NBUCKET, MAXDIST)[None] == np.arange(NBUCKET)[:, None])
                    for causal in (False, True)
                ]
            ).astype(np.float32)
        )
    return tables


def dot(left, right):
    return jnp.dot(left, right, preferred_element_type=FULL)


def dot_outer(left, right):
    return lax.dot_general(left, right, (((1,), (1,)), ((), ())), preferred_element_type=FULL)


def repeat(count, step):
    def body(index, carry):
        step(index)
        return carry

    lax.fori_loop(0, count, body, 0)


def at128(index, scale):
    return pl.multiple_of(index * scale, 128)


class Group:
    def __init__(self, name, count, rows, cols):
        self.name, self.count, self.rows, self.cols = name, count, rows, cols


def layer_kernel(names, groups, reduce, rows, length, width, hidden, *refs):
    v = types.SimpleNamespace(**dict(zip(names, refs)))
    tokens = rows * length
    chunks = hidden // CHUNK
    ways_rows = width // 16
    me, section = lax.axis_index("dp"), lax.axis_index("section")
    encoder, decoder = section == 0, section == 1
    z, y, c = me // 4, (me // 2) % 2, me % 2
    other = (1 - section, me)

    x_send, x_recv = v.x_send, v.x_recv
    low, low_t, grad_mix = v.low, v.low_t, v.grad_mix
    joint, units = grad_mix.at[:, : 2 * CHUNK], grad_mix.at[:, 2 * CHUNK : 3 * CHUNK]
    unit_ffn, unit_mid, cot = v.unit_ffn, v.unit_mid, v.cot
    res, grad = v.res, v.grad
    w_att, w_out, w_pair, w_lower = v.w_att, v.w_out, v.w_pair, v.w_lower
    qkv_self, qkv_cross = v.qkv_self, v.qkv_cross
    mix_self, mix_cross = v.mix_self, v.mix_cross
    probs, big = v.probs, v.big
    inverse, table, sums, mask = v.inverse, v.table, v.sums, v.mask
    misc = v.misc
    load, sem_x, sem_misc, sem_out = v.load, v.sem_x, v.sem_misc, v.sem_out

    def device(zz, yy, cc):
        return (section, zz * 4 + yy * 2 + cc)

    partners = [other]
    if reduce:
        sibling, beside = device(z, y, 1 - c), device(z, 1 - y, c)
        peer_z = [(z + d) % 4 for d in (1, 2, 3)]
        partners += [sibling, beside] + [device(p, y, c) for p in peer_z]
    barrier = pltpu.get_barrier_semaphore()
    for target in partners:
        pl.semaphore_signal(barrier, inc=1, device_id=target, device_id_type=MESH)

    def copy_in(source, target, slot):
        return pltpu.make_async_copy(source, target, load.at[slot])

    def load_x():
        return copy_in(v.inputs, x_send, 0)

    def load_cot():
        return copy_in(v.cotangent, cot, 1)

    def load_att():
        return copy_in(v.w_qkv.at[0], w_att, 2)

    def load_out():
        return copy_in(v.w_attn_out.at[0], w_out, 3)

    def load_cross():
        return [
            copy_in(v.cross_query, w_att.at[:, pl.ds(0, width)], 2),
            copy_in(v.cross_kv, w_att.at[:, pl.ds(width, 2 * width)], 4),
        ]

    def load_cross_out():
        return copy_in(v.cross_out, w_out, 3)

    def load_chunk(index):
        slot = index % 2
        at = at128(index, CHUNK)
        return [
            copy_in(
                v.w_gate_up.at[0, :, pl.ds(at, CHUNK)], w_pair.at[slot, :, pl.ds(0, CHUNK)], 5 + slot
            ),
            copy_in(
                v.w_gate_up.at[0, :, pl.ds(pl.multiple_of(hidden + at, 128), CHUNK)],
                w_pair.at[slot, :, pl.ds(CHUNK, CHUNK)],
                7 + slot,
            ),
            copy_in(v.w_down.at[0, pl.ds(at, CHUNK), :], w_lower.at[slot], 9 + slot),
        ]

    load_x().start()
    load_att().start()
    load_out().start()
    load_cot().start()
    misc[0] = jnp.zeros_like(misc[0])
    sums[...] = jnp.zeros_like(sums)
    for copy in load_chunk(0):
        copy.start()

    by_name = {group.name: group for group in groups}
    stacks = {
        group.name: (big if group.name == SELF else getattr(v, f"own{group.name}")) for group in groups
    }

    def block_place(shard):
        if not reduce:
            return shard
        return (shard % 2) * 8 + ((shard // 2) % 2) * 4 + shard // 4

    def put(name, item, columns, tile):
        own, r = stacks[name], by_name[name].rows
        low_tile = tile.astype(HALF)
        for shard in range(16):
            own[item, block_place(shard) * r : (block_place(shard) + 1) * r, columns] = low_tile[
                shard * r : (shard + 1) * r
            ]

    def send_first(name, i):
        r = by_name[name].rows
        return pltpu.make_async_remote_copy(
            stacks[name].at[i, pl.ds(pl.multiple_of((1 - c) * 8 * r, 16), 8 * r)],
            getattr(v, f"first{name}").at[i],
            getattr(v, f"sem{name}").at[i, 0],
            getattr(v, f"sem{name}").at[i, 1],
            device_id=sibling,
            device_id_type=MESH,
        )

    def send_second(name, i):
        r = by_name[name].rows
        return pltpu.make_async_remote_copy(
            stacks[name].at[i, pl.ds(pl.multiple_of(c * 8 * r + (1 - y) * 4 * r, 16), 4 * r)],
            getattr(v, f"second{name}").at[i],
            getattr(v, f"sem{name}").at[i, 2],
            getattr(v, f"sem{name}").at[i, 3],
            device_id=beside,
            device_id_type=MESH,
        )

    def send_third(name, i, d):
        r = by_name[name].rows
        return pltpu.make_async_remote_copy(
            stacks[name].at[i, pl.ds(pl.multiple_of(c * 8 * r + y * 4 * r + peer_z[d] * r, 16), r)],
            getattr(v, f"third{name}").at[i, d],
            getattr(v, f"sem{name}").at[i, 4 + d],
            getattr(v, f"sem{name}").at[i, 7 + d],
            device_id=device(peer_z[d], y, c),
            device_id_type=MESH,
        )

    def kept_rows(name):
        r = by_name[name].rows
        return pl.ds(pl.multiple_of(c * 8 * r + y * 4 * r + z * r, 16), r)

    def write_out(name, i):
        if reduce:
            source = stacks[name].at[i, kept_rows(name)]
        else:
            source = stacks[name].at[i]
        return pltpu.make_async_copy(source, getattr(v, f"out{name}").at[i], getattr(v, f"sem{name}").at[i, 10])

    def cross_over(i):
        return pltpu.make_async_remote_copy(
            stacks[CROSS].at[i, kept_rows(CROSS)],
            v.out2.at[i],
            v.sem2.at[i, 11],
            v.sem2.at[i, 12],
            device_id=other,
            device_id_type=MESH,
        )

    def begin(name, i):
        if reduce:
            send_first(name, i).start()
        else:
            write_out(name, i).start()

    def add_first(name, i):
        if not reduce:
            return
        own, first, r = stacks[name], getattr(v, f"first{name}"), by_name[name].rows
        send_first(name, i).wait_recv()

        def step(m):
            kept = pl.ds(pl.multiple_of(c * 8 * r + m * r, 16), r)
            own[i, kept] = own[i, kept] + first[i, pl.ds(pl.multiple_of(m * r, 16), r)]

        repeat(8, step)
        send_second(name, i).start()

    def add_second(name, i):
        if not reduce:
            return
        own, second, r = stacks[name], getattr(v, f"second{name}"), by_name[name].rows
        send_second(name, i).wait_recv()

        def step(m):
            kept = pl.ds(pl.multiple_of(c * 8 * r + y * 4 * r + m * r, 16), r)
            own[i, kept] = own[i, kept] + second[i, pl.ds(pl.multiple_of(m * r, 16), r)]

        repeat(4, step)
        for d in range(3):
            send_third(name, i, d).start()

    def add_third(name, i):
        if reduce:
            own, third = stacks[name], getattr(v, f"third{name}")
            for d in range(3):
                send_third(name, i, d).wait_recv()
            kept = kept_rows(name)
            total = (own[i, kept].astype(FULL) + third[i, 0].astype(FULL)) + (
                third[i, 1].astype(FULL) + third[i, 2].astype(FULL)
            )
            own[i, kept] = total.astype(HALF)
            write_out(name, i).start()
            if name == CROSS:
                cross_over(i).start()

    def finish(name, i):
        write_out(name, i).wait()
        if reduce:
            send_first(name, i).wait_send()
            send_second(name, i).wait_send()
            for d in range(3):
                send_third(name, i, d).wait_send()
            if name == CROSS:
                cross_over(i).wait_send()

    def block_of(ref, b):
        return ref.at[b // 9, pl.ds(at128((b % 9) // 3, 256), 256), pl.ds(at128(b % 3, 256), 256)]

    def decoder_unit(k):
        return block_of(big, H + 2 * chunks + k)

    def encoder_unit(k):
        lanes = pl.ds(pl.multiple_of(width + k // 2 * CHUNK, 128), CHUNK)
        return qkv_cross.at[pl.ds(at128(k % 2, length), length), lanes]

    def self_probs(head, row):
        return probs.at[head * rows + row]

    def cross_probs(head, row):
        return block_of(big, head)

    def row_slice(row):
        return pl.ds(pl.multiple_of(row * length, length), length)

    def part_slice(row, b, size):
        return pl.ds(pl.multiple_of(row * length + b * size, size), size)

    lanes = lax.broadcasted_iota(jnp.int32, (1, 128), 1)
    half_lanes = [(lanes < HD).astype(HALF), (lanes >= HD).astype(HALF)]

    def make_mask(key_segments, query_segments, row, causal):
        keys = key_segments[pl.ds(row, 1), :].astype(FULL)
        keys = jnp.broadcast_to(keys, (8, length)).T[:, :1]
        queries = query_segments[pl.ds(row, 1), :].astype(FULL)
        same = keys == queries
        if causal is not None:
            key_at = lax.broadcasted_iota(jnp.int32, (length, length), 0)
            query_at = lax.broadcasted_iota(jnp.int32, (length, length), 1)
            same = same & ((key_at <= query_at) | causal)
        mask[...] = jnp.where(same, 0.0, MASKED).astype(HALF)

    def lanes_of(offset, hp):
        return pl.ds(pl.multiple_of(offset + hp * 128, 128), 128)

    def attend(qkv, probs_of, mix, row, with_bias):
        at = row_slice(row)

        def pair(hp):
            queries = qkv[at, lanes_of(0, hp)]
            keys = qkv[at, lanes_of(width, hp)]
            values_t = qkv[at, lanes_of(2 * width, hp)].T
            both = jnp.concatenate([keys * half_lanes[0], keys * half_lanes[1]], 0)
            scores = dot_outer(both, queries)
            for e in range(2):
                if with_bias:
                    line = table[pl.ds(hp * 2 + e, 1), :]
                    skewed = line[:, length:] + v.near[...].astype(FULL) * (line[:, :length] - line[:, length:])
                    bias = pltpu.roll(skewed, 0, 1, stride=1, stride_axis=0)
                soft_parts = []
                for part in range(length // 128):
                    n = slice(part * 128, (part + 1) * 128)
                    shifted = scores[e * length : (e + 1) * length, n] + mask[:, n].astype(FULL)
                    if with_bias:
                        shifted = shifted + bias[:, n]
                    raised = jnp.exp(shifted - jnp.max(shifted, 0, keepdims=True))
                    total = jnp.sum(raised, 0, keepdims=True)
                    soft_parts.append((raised * (1.0 / total)).astype(HALF))
                softmaxed = jnp.concatenate(soft_parts, 1)
                probs_of(hp * 2 + e, row)[...] = softmaxed
                mixed = dot(values_t[e * HD : (e + 1) * HD], softmaxed)
                mix[pl.ds(pl.multiple_of(hp * 128 + e * HD, 16), HD), at] = mixed.astype(HALF)

        repeat_pairs(pair)

    def repeat_pairs(pair):
        def step(g):
            for u in range(UNROLL):
                pair(g * UNROLL + u)

        repeat(PAIRS // UNROLL, step)

    def attend_back(qkv, probs_of, row, with_bias, tick):
        at = row_slice(row)
        left = lax.broadcasted_iota(jnp.int32, (length, 128), 1) < HD
        def pair(hp):
            q_lanes, k_lanes, v_lanes = lanes_of(0, hp), lanes_of(width, hp), lanes_of(2 * width, hp)
            queries, keys, values = qkv[at, q_lanes], qkv[at, k_lanes], qkv[at, v_lanes]
            outer = grad_mix[:, q_lanes]
            keys_t = keys.T
            both = jnp.concatenate([values * half_lanes[0], values * half_lanes[1]], 0)
            grad_soft = dot_outer(both, outer)
            softs, scores = [], []
            for e in range(2):
                soft_low = probs_of(hp * 2 + e, row)[...]
                score_parts = []
                for part in range(length // 128):
                    n = slice(part * 128, (part + 1) * 128)
                    soft = soft_low[:, n].astype(FULL)
                    weighted = soft * grad_soft[e * length : (e + 1) * length, n]
                    shared = jnp.sum(weighted, 0, keepdims=True)
                    score_parts.append((weighted - soft * shared).astype(HALF))
                scores.append(jnp.concatenate(score_parts, 1))
                softs.append(soft_low)
            grad_keys = dot(jnp.concatenate(scores, 0), queries)
            grad_values = dot(jnp.concatenate(softs, 0), outer)
            left_side = jnp.concatenate([keys_t, v.flip[...]], 0) if with_bias else keys_t
            parts = []
            for e in range(2):
                product = dot(left_side, scores[e])
                parts.append(product[e * HD : (e + 1) * HD])
                if with_bias:
                    aligned = pltpu.roll(product[128:], 0, 1, stride=1, stride_axis=0)
                    before = jnp.sum(aligned * v.past[...].astype(FULL), 0, keepdims=True)
                    after = jnp.sum(aligned, 0, keepdims=True) - before
                    line = pl.ds(hp * 2 + e, 1)
                    sums[line, :] = sums[line, :] + jnp.concatenate([before, after], 1)
            qkv[at, q_lanes] = jnp.concatenate(parts, 0).T.astype(HALF)
            qkv[at, k_lanes] = jnp.where(left, grad_keys[:length], grad_keys[length:]).astype(HALF)
            qkv[at, v_lanes] = jnp.where(left, grad_values[:length], grad_values[length:]).astype(HALF)
            if tick is not None:
                tick(hp)

        repeat_pairs(pair)

    def normalise(load_rows, row, column, gain, unit_ref, target):
        for b in range(length // BLOCK):
            at = part_slice(row, b, BLOCK)
            value = load_rows(at)
            scale = lax.rsqrt(jnp.mean(value * value, -1, keepdims=True) + EPSILON)
            inverse[at, column : column + 1] = scale
            unit = value * scale
            if unit_ref is not None:
                unit_ref[at, :] = unit.astype(HALF)
            target[at, :] = (unit * gain).astype(HALF)

    def norm_back(load_grad, load_unit, row, column, gain, misc_row, load_base, low_ref):
        def step(b, gain_sum):
            at = part_slice(row, b, BLOCK)
            normed, unit = load_grad(at), load_unit(at)
            weighted = normed * unit
            grad_unit = normed * gain
            scale = inverse[at, column : column + 1]
            inner = jnp.mean(weighted * gain, -1, keepdims=True)
            result = scale * (grad_unit - unit * inner)
            if load_base is not None:
                result = result + load_base(at)
            grad[at, :] = result
            if low_ref is not None:
                low_ref[at, :] = result.astype(HALF)
            return gain_sum + jnp.sum(weighted.reshape(BLOCK // 8, 8, width), 0)

        gain_sum = lax.fori_loop(0, length // BLOCK, step, jnp.zeros((8, width), FULL))
        line = slice(misc_row, misc_row + 1)
        misc[0, line, :width] = misc[0, line, :width] + jnp.sum(gain_sum, 0, keepdims=True)

    def transpose_rows(target, source, row):
        for b in range(length // 128):
            at = part_slice(row, b, 128)
            target[:, at] = source[at, :].T

    def transpose_back(target, source, row):
        for b in range(length // 128):
            at = part_slice(row, b, 128)
            target[at, :] = source[:, at].T

    def add_projection(weights, base, row):
        at = row_slice(row)
        for j in range(width // 256):
            n = slice(j * 256, (j + 1) * 256)
            res[at, n] = base[at, n].astype(FULL) + dot(low[at, :], weights[:, n])

    def feed_forward(row, forward, backward, total, base, unit_block, more):
        at = row_slice(row)
        if backward:
            total[at, :] = jnp.zeros((length, width), FULL)

        def step(k):
            slot = k % 2

            @pl.when((k + 1 < chunks) | more)
            def _():
                for copy in load_chunk((k + 1) % chunks):
                    copy.start()

            for copy in load_chunk(k):
                copy.wait()
            kept = [block_of(big, row * 2 * chunks + k * 2 + side) for side in range(2)]
            if forward:
                joined = dot(low[at, :], w_pair[slot])
                gate, up = joined[:, :CHUNK], joined[:, CHUNK:]
                if not backward:
                    kept[0][...] = gate.astype(HALF)
                    kept[1][...] = up.astype(HALF)
            else:
                gate, up = kept[0][...].astype(FULL), kept[1][...].astype(FULL)
            squared = gate * gate
            curve = jnp.tanh(gate * (GELU_SCALE + GELU_SCALE * GELU_CUBE * squared))
            rising = 0.5 + 0.5 * curve
            bent = gate * rising
            unit = (bent * up).astype(HALF)
            if forward:
                res[at, :] = res[at, :] + dot(unit, w_lower[slot])
            if not backward:
                return
            grad_hidden = dot_outer(cot[at, :], w_lower[slot])
            slope = rising + 0.5 * gate * (1.0 - curve * curve) * (
                GELU_SCALE + 3.0 * GELU_SCALE * GELU_CUBE * squared
            )
            pair = jnp.concatenate(
                [(grad_hidden * up * slope).astype(HALF), (grad_hidden * bent).astype(HALF)], 1
            )
            total[at, :] = total[at, :] + dot_outer(pair, w_pair[slot])
            joint[...] = pair
            units[...] = unit.T
            first = [block_of(big, base + k * 2 + side) for side in range(2)]

            @pl.when(row == 0)
            def _():
                first[0][...] = joint[:, :CHUNK]
                first[1][...] = joint[:, CHUNK:]
                unit_block(k)[...] = units[...]

            @pl.when(row == rows - 1)
            def _():
                for part in range(2):
                    columns = slice(part * CHUNK, (part + 1) * CHUNK)
                    right = jnp.concatenate([first[part][...], joint[:, columns]], 0)
                    put(GATE_UP, k, columns, dot(low_t[...], right))
                begin(GATE_UP, k)
                r = by_name[DOWN].rows
                both = jnp.concatenate([unit_block(k)[...], units[...]], 1)
                for part in range(3):
                    lower = dot(both, cot[:, part * 256 : (part + 1) * 256]).astype(HALF)
                    if reduce:
                        for shard in range(CHUNK // r):
                            place = (shard % 2) * 8 + (k % 2) * 4 + k // 2
                            v.own1[part, pl.ds(pl.multiple_of(place * r, 16), r)] = lower[
                                shard * r : (shard + 1) * r
                            ]
                    else:
                        v.own1[part, pl.ds(at128(k, CHUNK), CHUNK)] = lower

                @pl.when(k > 0)
                def _():
                    add_first(GATE_UP, k - 1)

        repeat(chunks, step)
        if backward:

            @pl.when(row == rows - 1)
            def _():
                for part in range(3):
                    begin(DOWN, part)
                add_first(GATE_UP, chunks - 1)
                for part in range(3):
                    add_first(DOWN, part)

    def weight_gradient(name, item, left_t, right, at):
        def step(j):
            tile = dot(left_t[...], right[:, pl.ds(pl.multiple_of(at + j * 256, 128), 256)])
            put(name, item, pl.ds(at128(j, 256), 256), tile)

        repeat(width // 256, step)
        begin(name, item)

    def back_through_out(row):
        for j in range(width // 256):
            n = slice(j * 256, (j + 1) * 256)
            grad_mix[:, n] = dot_outer(low[row_slice(row), :], w_out[n, :]).astype(HALF)

    def as_full(ref):
        return lambda at: ref[at, :].astype(FULL)

    def memory_copy(row):
        return pltpu.make_async_remote_copy(
            x_send.at[row_slice(row)],
            x_recv.at[row_slice(row)],
            sem_x.at[0, row],
            sem_x.at[1, row],
            device_id=other,
            device_id_type=MESH,
        )

    def memory_back(row):
        return pltpu.make_async_remote_copy(
            x_send.at[row_slice(row)],
            x_recv.at[row_slice(row)],
            sem_x.at[2, row],
            sem_x.at[3, row],
            device_id=other,
            device_id_type=MESH,
        )

    def write_layer(row):
        return pltpu.make_async_copy(
            x_send.at[row_slice(row)], v.layer_out.at[row_slice(row)], sem_out.at[4 + row]
        )

    ffn_gain = v.ffn_norm[...].astype(FULL)
    attn_gain = v.attn_norm[...].astype(FULL)
    cross_gain = v.cross_norm[...].astype(FULL)
    final_gain = v.final_norm[...].astype(FULL)

    def enter_feed_forward(row):
        normalise(as_full(res), row, 1, ffn_gain, unit_ffn, low)
        transpose_rows(low_t, low, row)

    row_at = lax.broadcasted_iota(jnp.int32, (length, length), 0)
    lane_at = lax.broadcasted_iota(jnp.int32, (length, length), 1)
    v.near[...] = (lane_at + row_at < length).astype(FULL).astype(HALF)
    v.past[...] = (lane_at < row_at).astype(FULL).astype(HALF)
    v.flip[...] = (row_at + lane_at == length - 1).astype(FULL).astype(HALF)

    table[0:H, :] = lax.dot_general(
        v.rel_bias[...],
        v.spread[section].astype(FULL),
        (((0,), (0,)), ((), ())),
        precision=PRECISE,
        preferred_element_type=FULL,
    )
    segments = jnp.where(encoder, v.enc_segments[...], v.dec_segments[...])
    v.segments[0:rows, :] = segments
    load_x().wait()
    load_att().wait()
    load_out().wait()
    load_cot().wait()
    pl.semaphore_wait(barrier, len(partners))

    def forward_row(row):
        at = row_slice(row)
        normalise(as_full(x_send), row, 0, attn_gain, None, low)

        def project(j):
            columns = pl.ds(at128(j, 256), 256)
            qkv_self[at, columns] = dot(low[at, :], w_att[:, columns]).astype(HALF)

        repeat(3 * width // 256, project)
        make_mask(v.segments, v.segments, row, encoder)
        attend(qkv_self, self_probs, mix_self, row, True)
        transpose_back(low, mix_self, row)
        add_projection(w_out, x_send, row)

        @pl.when(encoder)
        def _():
            enter_feed_forward(row)
            feed_forward(row, True, False, None, 0, None, True)
            normalise(as_full(res), row, 2, final_gain, unit_mid, x_send)
            memory_copy(row).start()
            write_layer(row).start()

    repeat(rows, forward_row)

    def decoder_row(row):
        at = row_slice(row)
        normalise(as_full(res), row, 2, cross_gain, unit_mid, low)
        for j in range(width // 256):
            n = slice(j * 256, (j + 1) * 256)
            qkv_cross[at, n] = dot(low[at, :], w_att[:, n]).astype(HALF)
        make_mask(v.enc_segments, v.dec_segments, row, None)
        memory_copy(row).wait_recv()

        def project_memory(j):
            columns = pl.ds(pl.multiple_of(width + j * 256, 128), 256)
            qkv_cross[at, columns] = dot(x_recv[at, :], w_att[:, columns]).astype(HALF)

        repeat(2 * width // 256, project_memory)
        attend(qkv_cross, cross_probs, mix_cross, row, False)
        transpose_back(low, mix_cross, row)
        add_projection(w_out, res, row)
        enter_feed_forward(row)
        feed_forward(row, True, True, grad, H, decoder_unit, row + 1 < rows)
        x_send[at, :] = res[at, :].astype(HALF)
        write_layer(row).start()
        norm_back(as_full(grad), as_full(unit_ffn), row, 1, ffn_gain, 1, as_full(cot), low)
        back_through_out(row)
        attend_back(qkv_cross, cross_probs, row, False, None)
        write_layer(row).wait()
        for j in range(width // 256):
            n = slice(j * 256, (j + 1) * 256)
            x_send[at, n] = dot_outer(
                qkv_cross[at, width : 3 * width], w_att[n, width : 3 * width]
            ).astype(HALF)
        memory_back(row).start()
        for j in range(width // 256):
            n = slice(j * 256, (j + 1) * 256)
            res[at, n] = dot_outer(qkv_cross[at, :width], w_att[n, :width])

    def load_x_again():
        return copy_in(v.inputs, qkv_cross.at[:, pl.ds(0, width)], 0)

    @pl.when(encoder)
    def _():
        load_x_again().start()

    @pl.when(decoder)
    def _():
        for copy in load_cross():
            copy.start()
        load_cross_out().start()
        for copy in load_cross():
            copy.wait()
        load_cross_out().wait()
        repeat(rows, decoder_row)
        load_att().start()
        load_out().start()
        weight_gradient(CROSS, 0, mix_cross, low, 0)

        def gained(b):
            at = pl.ds(at128(b, 128), 128)
            low_t[:, at] = (unit_mid[at, :].astype(FULL) * cross_gain).astype(HALF).T

        repeat(tokens // 128, gained)
        weight_gradient(CROSS, 1, low_t, qkv_cross, 0)
        for row in range(rows):
            transpose_rows(low_t, x_recv, row)
        weight_gradient(CROSS, 2, low_t, qkv_cross, width)
        weight_gradient(CROSS, 3, low_t, qkv_cross, 2 * width)
        load_x_again().start()
        for row in range(rows):
            norm_back(as_full(res), as_full(unit_mid), row, 2, cross_gain, 2, as_full(grad), low)
        for item in range(4):
            add_first(CROSS, item)
        load_att().wait()
        load_out().wait()

    load_x_again().wait()

    def unit_self(at):
        return qkv_cross[at, :width].astype(FULL) * inverse[at, 0:1]

    def backward_row(row):
        at = row_slice(row)

        @pl.when(encoder)
        def _():
            memory_back(row).wait_recv()

            def memory_grads(at):
                return cot[at, :].astype(FULL) + x_recv[at, :].astype(FULL)

            norm_back(memory_grads, as_full(unit_mid), row, 2, final_gain, 2, None, cot)
            feed_forward(row, False, True, res, 0, encoder_unit, row + 1 < rows)
            norm_back(as_full(res), as_full(unit_ffn), row, 1, ffn_gain, 1, as_full(grad), low)

        def tick(hp):
            @pl.when(jnp.where(encoder, row == rows - 1, row == 0))
            def _():
                add_second(GATE_UP, hp)

            @pl.when(decoder & (row == rows - 1) & (hp < 2))
            def _():
                add_second(GATE_UP, PAIRS + hp)

        back_through_out(row)
        attend_back(qkv_self, self_probs, row, True, tick)
        for j in range(width // 256):
            n = slice(j * 256, (j + 1) * 256)
            res[at, n] = dot_outer(qkv_self[at, :], w_att[n, :])
        norm_back(as_full(res), unit_self, row, 0, attn_gain, 0, as_full(grad), None)

    repeat(rows, backward_row)
    write_grad = pltpu.make_async_copy(grad, v.grad_inputs, sem_out.at[1])
    write_grad.start()
    weight_gradient(SELF, 0, mix_self, low, 0)

    def gained_self(b):
        at = pl.ds(at128(b, 128), 128)
        low_t[:, at] = (unit_self(at) * attn_gain).astype(HALF).T

    repeat(tokens // 128, gained_self)
    for item in range(1, 4):
        weight_gradient(SELF, item, low_t, qkv_self, (item - 1) * width)
    for item in range(4):
        add_first(SELF, item)
    misc[0, 0:H, width : width + NBUCKET] = lax.dot_general(
        sums[0:H, :],
        v.summed[section].astype(FULL),
        (((1,), (1,)), ((), ())),
        precision=PRECISE,
        preferred_element_type=FULL,
    )

    def misc_copy(source, target, slot, to):
        return pltpu.make_async_remote_copy(
            misc.at[source],
            misc.at[target],
            sem_misc.at[slot, 0],
            sem_misc.at[slot, 1],
            device_id=to,
            device_id_type=MESH,
        )

    def misc_out(source, place, slot):
        return pltpu.make_async_copy(misc.at[source], v.out_misc.at[place], sem_out.at[slot])

    if reduce:
        first = misc_copy(0, 1, 0, sibling)
        first.start()
        first.wait_recv()
        misc[2] = misc[0] + misc[1]
        second = misc_copy(2, 3, 1, beside)
        second.start()

    def drain(name, done=0):
        count = by_name[name].count

        def step(i):
            @pl.when(i >= done)
            def _():
                add_second(name, i)

            @pl.when(i >= 2)
            def _():
                add_third(name, i - 2)

        repeat(count, step)
        for i in range(max(count - 2, 0), count):
            add_third(name, i)

    drain(GATE_UP, jnp.where(encoder, PAIRS, by_name[GATE_UP].count))
    drain(DOWN)

    @pl.when(decoder)
    def _():
        drain(CROSS)

    if reduce:
        second.wait_recv()
        misc[4 + z] = misc[2] + misc[3]
        thirds = [misc_copy(4 + z, 4 + z, 2 + d, device(peer_z[d], y, c)) for d in range(3)]
        for copy in thirds:
            copy.start()
    drain(SELF)
    if reduce:
        for d in range(3):
            came = misc_copy(4 + z, 4 + (z + 3 - d) % 4, 2 + d, device(peer_z[d], y, c))
            came.wait_recv()
        misc[8] = (misc[4] + misc[5]) + (misc[6] + misc[7])
        across = misc_copy(8, 9, 5, other)
        across.start()
        across.wait_recv()
        outs = [misc_out(8, section, 2), misc_out(9, 1 - section, 3)]
    else:
        outs = [misc_out(0, 0, 2)]
    for copy in outs:
        copy.start()
    for name in (GATE_UP, DOWN, SELF):
        repeat(by_name[name].count, functools.partial(finish, name))

    @pl.when(decoder)
    def _():
        repeat(by_name[CROSS].count, functools.partial(finish, CROSS))

    if reduce:

        @pl.when(encoder)
        def _():
            repeat(by_name[CROSS].count, lambda i: cross_over(i).wait_recv())

        for copy in [first, second, across] + thirds:
            copy.wait_send()
    for copy in outs:
        copy.wait()
    write_grad.wait()

    @pl.when(encoder)
    def _():
        for row in range(rows):
            memory_copy(row).wait_send()
            write_layer(row).wait()

    @pl.when(decoder)
    def _():
        for row in range(rows):
            memory_back(row).wait_send()


def run_layers(args, ways):
    (
        inputs,
        cotangent,
        enc_segments,
        dec_segments,
        rel_bias,
        attn_norm,
        ffn_norm,
        w_qkv,
        w_attn_out,
        w_gate_up,
        w_down,
        cross_norm,
        cross_query,
        cross_kv,
        cross_out,
        final_norm,
    ) = args
    _, rows, length, width = inputs.shape
    hidden = w_down.shape[1]
    tokens = rows * length
    reduce = ways == 16
    spread, summed = bucket_tables(length)
    operands = dict(
        inputs=inputs.reshape(tokens, width),
        cotangent=cotangent.reshape(tokens, width),
        w_qkv=w_qkv,
        w_attn_out=w_attn_out,
        w_gate_up=w_gate_up,
        w_down=w_down,
        cross_query=cross_query,
        cross_kv=cross_kv,
        cross_out=cross_out,
    )
    small = dict(
        enc_segments=enc_segments,
        dec_segments=dec_segments,
        rel_bias=rel_bias,
        attn_norm=attn_norm,
        ffn_norm=ffn_norm,
        cross_norm=cross_norm.reshape(1, width),
        final_norm=final_norm.reshape(1, width),
        spread=jnp.asarray(spread, HALF),
        summed=jnp.asarray(summed, HALF),
    )
    block = width // 16
    groups = [
        Group(GATE_UP, hidden // CHUNK, block, 2 * CHUNK),
        Group(DOWN, 3, hidden // 16, 256),
        Group(CROSS, 4, block, width),
        Group(SELF, 4, block, width),
    ]
    outs = dict(
        layer_out=((tokens, width), HALF),
        grad_inputs=((tokens, width), FULL),
    )
    for g in groups:
        outs[f"out{g.name}"] = ((g.count, g.rows if reduce else 16 * g.rows, g.cols), HALF)
    outs[MISC] = ((2 if reduce else 1, 16, width + 128), FULL)
    scratch = dict(
        x_send=pltpu.VMEM((tokens, width), HALF),
        x_recv=pltpu.VMEM((tokens, width), HALF),
        low=pltpu.VMEM((tokens, width), HALF),
        low_t=pltpu.VMEM((width, tokens), HALF),
        unit_ffn=pltpu.VMEM((tokens, width), HALF),
        unit_mid=pltpu.VMEM((tokens, width), HALF),
        cot=pltpu.VMEM((tokens, width), HALF),
        res=pltpu.VMEM((tokens, width), FULL),
        grad=pltpu.VMEM((tokens, width), FULL),
        w_att=pltpu.VMEM((width, 3 * width), HALF),
        w_out=pltpu.VMEM((width, width), HALF),
        w_pair=pltpu.VMEM((2, width, 2 * CHUNK), HALF),
        w_lower=pltpu.VMEM((2, CHUNK, width), HALF),
        qkv_self=pltpu.VMEM((tokens, 3 * width), HALF),
        qkv_cross=pltpu.VMEM((tokens, 3 * width), HALF),
        mix_self=pltpu.VMEM((width, tokens), HALF),
        mix_cross=pltpu.VMEM((width, tokens), HALF),
        probs=pltpu.VMEM((H * rows, length, length), HALF),
        big=pltpu.VMEM((4, width, width), HALF),
        inverse=pltpu.VMEM((tokens, 8), FULL),
        mask=pltpu.VMEM((length, length), HALF),
        near=pltpu.VMEM((length, length), HALF),
        past=pltpu.VMEM((length, length), HALF),
        flip=pltpu.VMEM((length, length), HALF),
        grad_mix=pltpu.VMEM((length, width), HALF),
        segments=pltpu.VMEM((8, length), jnp.int32),
        table=pltpu.VMEM((16, 2 * length), FULL),
        sums=pltpu.VMEM((16, 2 * length), FULL),
        misc=pltpu.VMEM((10 if reduce else 1, 16, width + 128), FULL),
        load=pltpu.SemaphoreType.DMA((11,)),
        sem_x=pltpu.SemaphoreType.DMA((4, rows)),
        sem_misc=pltpu.SemaphoreType.DMA((6, 2)),
        sem_out=pltpu.SemaphoreType.DMA((4 + rows,)),
    )
    for g in groups:
        if g.name != SELF:
            scratch[f"own{g.name}"] = pltpu.VMEM((g.count, 16 * g.rows, g.cols), HALF)
        if reduce:
            scratch[f"first{g.name}"] = pltpu.VMEM((g.count, 8 * g.rows, g.cols), HALF)
            scratch[f"second{g.name}"] = pltpu.VMEM((g.count, 4 * g.rows, g.cols), HALF)
            scratch[f"third{g.name}"] = pltpu.VMEM((g.count, 3, g.rows, g.cols), HALF)
        scratch[f"sem{g.name}"] = pltpu.SemaphoreType.DMA((g.count, 13))
    names = list(operands) + list(small) + list(outs) + list(scratch)
    results = pl.pallas_call(
        functools.partial(layer_kernel, names, groups, reduce, rows, length, width, hidden),
        out_shape=[jax.ShapeDtypeStruct(*out) for out in outs.values()],
        in_specs=[pl.BlockSpec(memory_space=pl.ANY)] * len(operands)
        + [pl.BlockSpec(memory_space=pltpu.VMEM)] * len(small),
        out_specs=[pl.BlockSpec(memory_space=pl.ANY)] * len(outs),
        scratch_shapes=list(scratch.values()),
        compiler_params=pltpu.CompilerParams(
            collective_id=1, has_side_effects=True, vmem_limit_bytes=VMEM_LIMIT
        ),
    )(*operands.values(), *small.values())
    return dict(zip(outs, results)), reduce


LAYER, INPUT, MISC = "layer_out", "grad_inputs", "out_misc"
VMEM_LIMIT = 64 * 2**20 - 64 * 2**10


def shards(*args):
    inputs, rel_bias = args[0], args[4]
    ways = lax.axis_size("dp")
    _, rows, length, width = inputs.shape
    hidden = args[10].shape[1]
    out, reduce = run_layers(args, ways)

    def wide(name):
        value = out[f"out{name}"]
        if reduce:
            return value.astype(FULL)
        total = lax.psum_scatter(value, "dp", scatter_dimension=1, tiled=True)
        if name == CROSS:
            total = lax.psum(jnp.where(lax.axis_index("section") == 1, total, 0), "section")
        return total.astype(FULL)

    def side_by_side(value):
        return jnp.swapaxes(value, 0, 1).reshape(value.shape[1], -1)

    gate_up = wide(GATE_UP)
    chunks, block, _ = gate_up.shape
    gate_up = gate_up.reshape(chunks, block, 2, CHUNK).transpose(1, 2, 0, 3).reshape(block, 2 * hidden)
    down, cross, late = wide(DOWN), wide(CROSS), wide(SELF)
    misc = out[MISC]
    section = lax.axis_index("section")
    if not reduce:
        mine = lax.psum(misc[0], "dp")
        misc = lax.all_gather(mine, "section", axis=0)
    own = lax.dynamic_index_in_dim(misc, section, 0, keepdims=False)
    start = lax.axis_index("dp") * block

    def piece(vector):
        return lax.dynamic_slice_in_dim(vector, start, block, 0)

    rel = (misc[0] + misc[1])[:H, width : width + NBUCKET].T
    return (
        out[LAYER].reshape(inputs.shape),
        out[INPUT].reshape(inputs.shape),
        side_by_side(late[1:])[None],
        late[0][None],
        gate_up[None],
        side_by_side(down)[None],
        piece(own[0, :width])[None],
        piece(own[1, :width])[None],
        cross[1],
        side_by_side(cross[2:]),
        cross[0],
        piece(misc[1, 2, :width]),
        piece(misc[0, 2, :width]),
        rel,
    )


def solution(mesh):
    layer = P("section", "dp", None, None)
    matrix = P("section", None, None)
    return jax.shard_map(
        shards,
        mesh=mesh,
        in_specs=(layer, layer, P("dp", None), P("dp", None), P())
        + (P("section", None),) * 2
        + (matrix,) * 4
        + (P(),) * 5,
        out_specs=(layer, layer)
        + (P("section", "dp", None),) * 4
        + (P("section", "dp"),) * 2
        + (P("dp", None),) * 3
        + (P("dp"),) * 2
        + (P(),),
        check_vma=False,
    )
```

time: 286 us -> 234 us (0.82)
  Pallas kernels: 270 us -> 217 us
    pallas_call x1, Pallas kernels: 270 us -> 217 us  [run_layers(): pl.pallas_call(functools.partial(layer_kernel, names, groups, reduce, row...]
where the time goes in v3:
time: 234 us; the launch traced here: 233 us
  Pallas kernels  217 us (93%)
  local copies, waits for them, and re-layouts  14.3 us (6%)
    pallas_call x1, Pallas kernels, run_layers(): pl.pallas_call(functools.partial(layer_kernel, names, groups, reduce, row...  217 us

profile of v3, /device:TPU:0, one launch (start us, length us, event | category | flops | bytes accessed | tf_op | source)
XLA Modules:
  0.0 232.8 jit_solution(1500785502861426977)
XLA Ops:
  0.6 1.4 copy.34.refs_11_
  2.0 1.3 reshape.62.refs_14_
  3.3 1.3 reshape.63.refs_15_
  4.5 216.6 %shard_map.281 = (bf16[512,768]{1,0:T(8,128)(2,1)}, f32[512,768]{1,0:T(8,128)}, bf16[8,48,512]{2,1,0:T(8,128)(2,1)}, bf16[3,128,256]{2,1,0:T(8,128)(2,1)}, bf16[...) custom-call(bf16[512,768]{1,0:T(8,128)(2,1)} %bitcast.33, bf16[512,768]{1,0:T(8,128)(2,1)} %bitcast.34, ...), custom_call_target="tpu_custom_call" | custom-call | tf_op jit(solution)/shard_map/pallas_call | solution.py:982
  221.1 1.0 convert_element_type.8
  222.1 0.0 copy-start.2
  222.2 0.0 copy-start.3
  222.2 0.3 copy.35
  222.5 1.1 broadcast_in_dim_reshape.15
  223.6 0.0 copy-done.2
  223.6 0.7 slice.49
  224.3 0.0 copy-done.3
  224.3 0.5 reshape.70
  224.8 0.0 copy-start.6
  224.8 0.5 copy.36
  225.2 0.0 copy-start.5
  225.2 1.0 reshape.68
  226.3 0.0 copy-done.6
  226.3 0.2 copy.37
  226.5 0.9 copy.39
  227.4 0.0 copy-done.5
  227.4 0.6 constant_dynamic-slice_fusion.2
  228.0 0.0 copy-done.4
  228.1 0.0 copy-start
  228.1 0.7 slice_bitcast_fusion.2
  228.8 0.7 copy.40
  229.6 0.6 fusion
  230.2 0.6 slice_bitcast_fusion.4
  230.8 0.0 copy-done.1
  230.8 0.9 copy.43
  231.6 0.0 copy-done
  231.6 1.1 copy.44
  (9 shorter events, 0.1 us)
Async XLA Ops:
  222.1 1.4 copy-start.2
  222.2 2.1 copy-start.3
  224.8 1.5 copy-start.6
  225.2 2.2 copy-start.5
  226.3 1.8 copy-start.4
  227.4 3.4 %copy-start.1 = (bf16[512,768]{1,0:T(8,128)(2,1)S(1)}, bf16[512,768]{1,0:T(8,128)(2,1)}, u32[]{:S(2)}) copy-start(bf16[512,768]{1,0:T(8,128)(2,1)} %get-tuple-element.21) | copy-start | bytes 2359300
  228.1 3.6 %copy-start = (f32[512,768]{1,0:T(8,128)S(1)}, f32[512,768]{1,0:T(8,128)}, u32[]{:S(2)}) copy-start(f32[512,768]{1,0:T(8,128)} %get-tuple-element.22) | copy-start | bytes 4718596

commit v4 on v3

--- a/solution.py
+++ b/solution.py
@@ -24,7 +24,8 @@
 CHUNK = 256
 BLOCK = 64
 UNROLL = 2
-GATE_UP, DOWN, CROSS, SELF = range(4)
+RING = 4
+GATE_UP, DOWN, CROSS, SELF, SMALL = range(5)
 GELU_SCALE = math.sqrt(2.0 / math.pi)
 GELU_CUBE = 0.044715
 
@@ -106,22 +107,21 @@
     joint, units = grad_mix.at[:, : 2 * CHUNK], grad_mix.at[:, 2 * CHUNK : 3 * CHUNK]
     unit_ffn, unit_mid, cot = v.unit_ffn, v.unit_mid, v.cot
     res, grad = v.res, v.grad
-    w_att, w_out, w_pair, w_lower = v.w_att, v.w_out, v.w_pair, v.w_lower
+    w_att, w_out = v.w_att, v.w_out
     qkv_self, qkv_cross = v.qkv_self, v.qkv_cross
     mix_self, mix_cross = v.mix_self, v.mix_cross
     probs, big = v.probs, v.big
     inverse, table, sums, mask = v.inverse, v.table, v.sums, v.mask
     misc = v.misc
-    load, sem_x, sem_misc, sem_out = v.load, v.sem_x, v.sem_misc, v.sem_out
+    load, sem_x, sem_out = v.load, v.sem_x, v.sem_out
 
     def device(zz, yy, cc):
         return (section, zz * 4 + yy * 2 + cc)
 
-    partners = [other]
-    if reduce:
-        sibling, beside = device(z, y, 1 - c), device(z, 1 - y, c)
-        peer_z = [(z + d) % 4 for d in (1, 2, 3)]
-        partners += [sibling, beside] + [device(p, y, c) for p in peer_z]
+    z_low, z_high = z % 2, z // 2
+    near_y, near_z = device(z, 1 - y, c), device(z + 1 - 2 * z_low, y, c)
+    sibling, far_z = device(z, y, 1 - c), device(z + 2 - 4 * z_high, y, c)
+    partners = [other] + ([sibling, near_y, near_z, far_z] if reduce else [])
     barrier = pltpu.get_barrier_semaphore()
     for target in partners:
         pl.semaphore_signal(barrier, inc=1, device_id=target, device_id_type=MESH)
@@ -150,158 +150,139 @@
     def load_cross_out():
         return copy_in(v.cross_out, w_out, 3)
 
+    ring = v.own2
+
     def load_chunk(index):
-        slot = index % 2
+        slot = index % RING
         at = at128(index, CHUNK)
-        return [
+        pieces = [
             copy_in(
-                v.w_gate_up.at[0, :, pl.ds(at, CHUNK)], w_pair.at[slot, :, pl.ds(0, CHUNK)], 5 + slot
+                v.w_down.at[0, pl.ds(at, CHUNK), pl.ds(j * 256, 256)],
+                ring.at[slot, pl.ds(j * 256, 256), pl.ds(2 * CHUNK, 256)],
+                7 + j + 5 * slot,
+            )
+            for j in range(width // 256)
+        ]
+        return pieces + [
+            copy_in(
+                v.w_gate_up.at[0, :, pl.ds(at, CHUNK)], ring.at[slot, :, pl.ds(0, CHUNK)], 5 + 5 * slot
             ),
             copy_in(
                 v.w_gate_up.at[0, :, pl.ds(pl.multiple_of(hidden + at, 128), CHUNK)],
-                w_pair.at[slot, :, pl.ds(CHUNK, CHUNK)],
-                7 + slot,
+                ring.at[slot, :, pl.ds(CHUNK, CHUNK)],
+                6 + 5 * slot,
             ),
-            copy_in(v.w_down.at[0, pl.ds(at, CHUNK), :], w_lower.at[slot], 9 + slot),
         ]
 
     load_x().start()
     load_att().start()
     load_out().start()
     load_cot().start()
-    misc[0] = jnp.zeros_like(misc[0])
+    misc[...] = jnp.zeros_like(misc)
     sums[...] = jnp.zeros_like(sums)
-    for copy in load_chunk(0):
-        copy.start()
+    for k in range(RING - 1):
+        for copy in load_chunk(k):
+            copy.start()
 
     by_name = {group.name: group for group in groups}
     stacks = {
         group.name: (big if group.name == SELF else getattr(v, f"own{group.name}")) for group in groups
     }
 
-    def block_place(shard):
-        if not reduce:
-            return shard
-        return (shard % 2) * 8 + ((shard // 2) % 2) * 4 + shard // 4
+    def block_place(zz, yy, cc):
+        return cc * 8 + yy * 4 + (zz % 2) * 2 + zz // 2
 
     def put(name, item, columns, tile):
         own, r = stacks[name], by_name[name].rows
         low_tile = tile.astype(HALF)
         for shard in range(16):
-            own[item, block_place(shard) * r : (block_place(shard) + 1) * r, columns] = low_tile[
+            place = shard
+            if reduce:
+                place = block_place(shard // 4, (shard // 2) % 2, shard % 2)
+            own[item, place * r : (place + 1) * r, columns] = low_tile[
                 shard * r : (shard + 1) * r
             ]
 
-    def send_first(name, i):
-        r = by_name[name].rows
+    def stages(name):
+        result, base, count = [], 0, 16 * by_name[name].rows
+        for bit, target in ((c, sibling), (y, near_y), (z_low, near_z), (z_high, far_z)):
+            count = count // 2
+            sent, base = base + (1 - bit) * count, base + bit * count
+            result.append((target, pl.multiple_of(sent, 16), pl.multiple_of(base, 16), count))
+        return result
+
+    def exchange(name, i, stage):
+        target, sent, _, count = stages(name)[stage]
+        sems = getattr(v, f"sem{name}")
         return pltpu.make_async_remote_copy(
-            stacks[name].at[i, pl.ds(pl.multiple_of((1 - c) * 8 * r, 16), 8 * r)],
-            getattr(v, f"first{name}").at[i],
-            getattr(v, f"sem{name}").at[i, 0],
-            getattr(v, f"sem{name}").at[i, 1],
-            device_id=sibling,
+            stacks[name].at[i, pl.ds(sent, count)],
+            getattr(v, f"came{stage}x{name}").at[i],
+            sems.at[i, 2 * stage],
+            sems.at[i, 2 * stage + 1],
+            device_id=target,
             device_id_type=MESH,
         )
 
-    def send_second(name, i):
-        r = by_name[name].rows
+    def kept_rows(name):
+        _, _, kept, count = stages(name)[3]
+        return pl.ds(kept, count)
+
+    def write_out(name, i):
+        source = stacks[name].at[i, kept_rows(name)] if reduce else stacks[name].at[i]
+        place = section if name == SMALL else i
+        return pltpu.make_async_copy(
+            source, getattr(v, f"out{name}").at[place], getattr(v, f"sem{name}").at[i, 8]
+        )
+
+    def cross_over(name, i, place):
+        sems = getattr(v, f"sem{name}")
         return pltpu.make_async_remote_copy(
-            stacks[name].at[i, pl.ds(pl.multiple_of(c * 8 * r + (1 - y) * 4 * r, 16), 4 * r)],
-            getattr(v, f"second{name}").at[i],
-            getattr(v, f"sem{name}").at[i, 2],
-            getattr(v, f"sem{name}").at[i, 3],
-            device_id=beside,
-            device_id_type=MESH,
-        )
-
-    def send_third(name, i, d):
-        r = by_name[name].rows
-        return pltpu.make_async_remote_copy(
-            stacks[name].at[i, pl.ds(pl.multiple_of(c * 8 * r + y * 4 * r + peer_z[d] * r, 16), r)],
-            getattr(v, f"third{name}").at[i, d],
-            getattr(v, f"sem{name}").at[i, 4 + d],
-            getattr(v, f"sem{name}").at[i, 7 + d],
-            device_id=device(peer_z[d], y, c),
-            device_id_type=MESH,
-        )
-
-    def kept_rows(name):
-        r = by_name[name].rows
-        return pl.ds(pl.multiple_of(c * 8 * r + y * 4 * r + z * r, 16), r)
-
-    def write_out(name, i):
-        if reduce:
-            source = stacks[name].at[i, kept_rows(name)]
-        else:
-            source = stacks[name].at[i]
-        return pltpu.make_async_copy(source, getattr(v, f"out{name}").at[i], getattr(v, f"sem{name}").at[i, 10])
-
-    def cross_over(i):
-        return pltpu.make_async_remote_copy(
-            stacks[CROSS].at[i, kept_rows(CROSS)],
-            v.out2.at[i],
-            v.sem2.at[i, 11],
-            v.sem2.at[i, 12],
+            stacks[name].at[i, kept_rows(name)],
+            getattr(v, f"out{name}").at[place],
+            sems.at[i, 9],
+            sems.at[i, 10],
             device_id=other,
             device_id_type=MESH,
         )
 
     def begin(name, i):
         if reduce:
-            send_first(name, i).start()
+            exchange(name, i, 0).start()
         else:
             write_out(name, i).start()
 
-    def add_first(name, i):
+    def add(name, i, stage):
         if not reduce:
             return
-        own, first, r = stacks[name], getattr(v, f"first{name}"), by_name[name].rows
-        send_first(name, i).wait_recv()
+        own, came = stacks[name], getattr(v, f"came{stage}x{name}")
+        exchange(name, i, stage).wait_recv()
+        _, _, kept, count = stages(name)[stage]
+        size = min(count, 2 * by_name[name].rows)
 
         def step(m):
-            kept = pl.ds(pl.multiple_of(c * 8 * r + m * r, 16), r)
-            own[i, kept] = own[i, kept] + first[i, pl.ds(pl.multiple_of(m * r, 16), r)]
-
-        repeat(8, step)
-        send_second(name, i).start()
-
-    def add_second(name, i):
-        if not reduce:
-            return
-        own, second, r = stacks[name], getattr(v, f"second{name}"), by_name[name].rows
-        send_second(name, i).wait_recv()
-
-        def step(m):
-            kept = pl.ds(pl.multiple_of(c * 8 * r + y * 4 * r + m * r, 16), r)
-            own[i, kept] = own[i, kept] + second[i, pl.ds(pl.multiple_of(m * r, 16), r)]
-
-        repeat(4, step)
-        for d in range(3):
-            send_third(name, i, d).start()
-
-    def add_third(name, i):
-        if reduce:
-            own, third = stacks[name], getattr(v, f"third{name}")
-            for d in range(3):
-                send_third(name, i, d).wait_recv()
-            kept = kept_rows(name)
-            total = (own[i, kept].astype(FULL) + third[i, 0].astype(FULL)) + (
-                third[i, 1].astype(FULL) + third[i, 2].astype(FULL)
-            )
-            own[i, kept] = total.astype(HALF)
+            at = pl.ds(pl.multiple_of(kept + m * size, 16), size)
+            own[i, at] = own[i, at] + came[i, pl.ds(pl.multiple_of(m * size, 16), size)]
+
+        repeat(count // size, step)
+        if stage < 3:
+            exchange(name, i, stage + 1).start()
+        else:
             write_out(name, i).start()
             if name == CROSS:
-                cross_over(i).start()
+                cross_over(name, i, i).start()
+            if name == SMALL:
+                cross_over(name, i, section).start()
+
+    def add_first(name, i):
+        add(name, i, 0)
 
     def finish(name, i):
         write_out(name, i).wait()
         if reduce:
-            send_first(name, i).wait_send()
-            send_second(name, i).wait_send()
-            for d in range(3):
-                send_third(name, i, d).wait_send()
-            if name == CROSS:
-                cross_over(i).wait_send()
+            for stage in range(4):
+                exchange(name, i, stage).wait_send()
+            if name in (CROSS, SMALL):
+                cross_over(name, i, i).wait_send()
 
     def block_of(ref, b):
         return ref.at[b // 9, pl.ds(at128((b % 9) // 3, 256), 256), pl.ds(at128(b % 3, 256), 256)]
@@ -451,7 +432,7 @@
 
         gain_sum = lax.fori_loop(0, length // BLOCK, step, jnp.zeros((8, width), FULL))
         line = slice(misc_row, misc_row + 1)
-        misc[0, line, :width] = misc[0, line, :width] + jnp.sum(gain_sum, 0, keepdims=True)
+        misc[line, :width] = misc[line, :width] + jnp.sum(gain_sum, 0, keepdims=True)
 
     def transpose_rows(target, source, row):
         for b in range(length // 128):
@@ -475,18 +456,20 @@
             total[at, :] = jnp.zeros((length, width), FULL)
 
         def step(k):
-            slot = k % 2
-
-            @pl.when((k + 1 < chunks) | more)
+            slot = k % RING
+            pair_weights = ring.at[slot, :, : 2 * CHUNK]
+            lower = [ring.at[slot, j * 256 : (j + 1) * 256, 2 * CHUNK :] for j in range(width // 256)]
+
+            @pl.when((k + RING - 1 < chunks) | more)
             def _():
-                for copy in load_chunk((k + 1) % chunks):
+                for copy in load_chunk((k + RING - 1) % chunks):
                     copy.start()
 
             for copy in load_chunk(k):
                 copy.wait()
             kept = [block_of(big, row * 2 * chunks + k * 2 + side) for side in range(2)]
             if forward:
-                joined = dot(low[at, :], w_pair[slot])
+                joined = dot(low[at, :], pair_weights[...])
                 gate, up = joined[:, :CHUNK], joined[:, CHUNK:]
                 if not backward:
                     kept[0][...] = gate.astype(HALF)
@@ -499,17 +482,21 @@
             bent = gate * rising
             unit = (bent * up).astype(HALF)
             if forward:
-                res[at, :] = res[at, :] + dot(unit, w_lower[slot])
+                for j in range(width // 256):
+                    n = slice(j * 256, (j + 1) * 256)
+                    res[at, n] = res[at, n] + dot(unit, lower[j][...])
             if not backward:
                 return
-            grad_hidden = dot_outer(cot[at, :], w_lower[slot])
+            grad_hidden = sum(
+                dot_outer(cot[at, j * 256 : (j + 1) * 256], lower[j][...]) for j in range(width // 256)
+            )
             slope = rising + 0.5 * gate * (1.0 - curve * curve) * (
                 GELU_SCALE + 3.0 * GELU_SCALE * GELU_CUBE * squared
             )
             pair = jnp.concatenate(
                 [(grad_hidden * up * slope).astype(HALF), (grad_hidden * bent).astype(HALF)], 1
             )
-            total[at, :] = total[at, :] + dot_outer(pair, w_pair[slot])
+            total[at, :] = total[at, :] + dot_outer(pair, pair_weights[...])
             joint[...] = pair
             units[...] = unit.T
             first = [block_of(big, base + k * 2 + side) for side in range(2)]
@@ -530,15 +517,15 @@
                 r = by_name[DOWN].rows
                 both = jnp.concatenate([unit_block(k)[...], units[...]], 1)
                 for part in range(3):
-                    lower = dot(both, cot[:, part * 256 : (part + 1) * 256]).astype(HALF)
+                    tile = dot(both, cot[:, part * 256 : (part + 1) * 256]).astype(HALF)
                     if reduce:
                         for shard in range(CHUNK // r):
-                            place = (shard % 2) * 8 + (k % 2) * 4 + k // 2
-                            v.own1[part, pl.ds(pl.multiple_of(place * r, 16), r)] = lower[
+                            place = block_place(k // 2, k % 2, shard)
+                            v.own1[part, pl.ds(pl.multiple_of(place * r, 16), r)] = tile[
                                 shard * r : (shard + 1) * r
                             ]
                     else:
-                        v.own1[part, pl.ds(at128(k, CHUNK), CHUNK)] = lower
+                        v.own1[part, pl.ds(at128(k, CHUNK), CHUNK)] = tile
 
                 @pl.when(k > 0)
                 def _():
@@ -598,8 +585,8 @@
 
     ffn_gain = v.ffn_norm[...].astype(FULL)
     attn_gain = v.attn_norm[...].astype(FULL)
-    cross_gain = v.cross_norm[...].astype(FULL)
-    final_gain = v.final_norm[...].astype(FULL)
+    cross_gain = v.mid_norms[...].astype(FULL)[0:1]
+    final_gain = v.mid_norms[...].astype(FULL)[1:2]
 
     def enter_feed_forward(row):
         normalise(as_full(res), row, 1, ffn_gain, unit_ffn, low)
@@ -728,6 +715,17 @@
     def unit_self(at):
         return qkv_cross[at, :width].astype(FULL) * inverse[at, 0:1]
 
+    def advance(i):
+        add(GATE_UP, i, 1)
+
+        @pl.when(i >= 1)
+        def _():
+            add(GATE_UP, i - 1, 2)
+
+        @pl.when(i >= 2)
+        def _():
+            add(GATE_UP, i - 2, 3)
+
     def backward_row(row):
         at = row_slice(row)
 
@@ -745,11 +743,11 @@
         def tick(hp):
             @pl.when(jnp.where(encoder, row == rows - 1, row == 0))
             def _():
-                add_second(GATE_UP, hp)
-
-            @pl.when(decoder & (row == rows - 1) & (hp < 2))
+                advance(hp)
+
+            @pl.when(decoder & (row == rows - 1) & (hp < chunks - PAIRS))
             def _():
-                add_second(GATE_UP, PAIRS + hp)
+                advance(PAIRS + hp)
 
         back_through_out(row)
         attend_back(qkv_self, self_probs, row, True, tick)
@@ -772,79 +770,44 @@
         weight_gradient(SELF, item, low_t, qkv_self, (item - 1) * width)
     for item in range(4):
         add_first(SELF, item)
-    misc[0, 0:H, width : width + NBUCKET] = lax.dot_general(
-        sums[0:H, :],
+    by_bucket = lax.dot_general(
+        sums[...],
         v.summed[section].astype(FULL),
         (((1,), (1,)), ((), ())),
         precision=PRECISE,
         preferred_element_type=FULL,
     )
-
-    def misc_copy(source, target, slot, to):
-        return pltpu.make_async_remote_copy(
-            misc.at[source],
-            misc.at[target],
-            sem_misc.at[slot, 0],
-            sem_misc.at[slot, 1],
-            device_id=to,
-            device_id_type=MESH,
-        )
-
-    def misc_out(source, place, slot):
-        return pltpu.make_async_copy(misc.at[source], v.out_misc.at[place], sem_out.at[slot])
-
     if reduce:
-        first = misc_copy(0, 1, 0, sibling)
-        first.start()
-        first.wait_recv()
-        misc[2] = misc[0] + misc[1]
-        second = misc_copy(2, 3, 1, beside)
-        second.start()
-
-    def drain(name, done=0):
-        count = by_name[name].count
-
-        def step(i):
-            @pl.when(i >= done)
-            def _():
-                add_second(name, i)
-
-            @pl.when(i >= 2)
-            def _():
-                add_third(name, i - 2)
-
-        repeat(count, step)
-        for i in range(max(count - 2, 0), count):
-            add_third(name, i)
-
-    drain(GATE_UP, jnp.where(encoder, PAIRS, by_name[GATE_UP].count))
-    drain(DOWN)
+        misc[:, width:] = misc[:, :128]
+        by_bucket = jnp.concatenate([by_bucket, jnp.zeros((16, 128 - NBUCKET), FULL)], 1)
+        for shard in range(16):
+            place = block_place(shard // 4, (shard // 2) % 2, shard % 2)
+            turned = pltpu.roll(misc[...], (width + 128 - shard * ways_rows) % (width + 128), 1)
+            block = jnp.concatenate([turned[:, :128], by_bucket, jnp.zeros((8, 128), FULL)], 0)
+            v.own4[0, place * 32 : (place + 1) * 32, :] = block.astype(HALF)
+        begin(SMALL, 0)
+        add_first(SMALL, 0)
+
+    def drain(names, done):
+        line = [(name, i) for name in names for i in range(by_name[name].count)]
+        for n in range(done, len(line) + 2):
+            for stage in (1, 2, 3):
+                if 0 <= n + 1 - stage < len(line):
+                    add(*line[n + 1 - stage], stage)
+
+    @pl.when(encoder)
+    def _():
+        drain([GATE_UP, DOWN, SELF] + ([SMALL] if reduce else []), PAIRS)
 
     @pl.when(decoder)
     def _():
-        drain(CROSS)
-
-    if reduce:
-        second.wait_recv()
-        misc[4 + z] = misc[2] + misc[3]
-        thirds = [misc_copy(4 + z, 4 + z, 2 + d, device(peer_z[d], y, c)) for d in range(3)]
-        for copy in thirds:
-            copy.start()
-    drain(SELF)
-    if reduce:
-        for d in range(3):
-            came = misc_copy(4 + z, 4 + (z + 3 - d) % 4, 2 + d, device(peer_z[d], y, c))
-            came.wait_recv()
-        misc[8] = (misc[4] + misc[5]) + (misc[6] + misc[7])
-        across = misc_copy(8, 9, 5, other)
-        across.start()
-        across.wait_recv()
-        outs = [misc_out(8, section, 2), misc_out(9, 1 - section, 3)]
-    else:
-        outs = [misc_out(0, 0, 2)]
-    for copy in outs:
-        copy.start()
-    for name in (GATE_UP, DOWN, SELF):
+        drain([GATE_UP, DOWN, CROSS, SELF] + ([SMALL] if reduce else []), chunks)
+
+    if not reduce:
+        misc[8:24, :NBUCKET] = by_bucket
+        outs = pltpu.make_async_copy(misc, v.out_misc, sem_out.at[2])
+        outs.start()
+    for name in [GATE_UP, DOWN, SELF] + ([SMALL] if reduce else []):
         repeat(by_name[name].count, functools.partial(finish, name))
 
     @pl.when(decoder)
@@ -855,12 +818,11 @@
 
         @pl.when(encoder)
         def _():
-            repeat(by_name[CROSS].count, lambda i: cross_over(i).wait_recv())
-
-        for copy in [first, second, across] + thirds:
-            copy.wait_send()
-    for copy in outs:
-        copy.wait()
+            repeat(by_name[CROSS].count, lambda i: cross_over(CROSS, i, i).wait_recv())
+
+        cross_over(SMALL, 0, 1 - section).wait_recv()
+    else:
+        outs.wait()
     write_grad.wait()
 
     @pl.when(encoder)
@@ -916,8 +878,7 @@
         rel_bias=rel_bias,
         attn_norm=attn_norm,
         ffn_norm=ffn_norm,
-        cross_norm=cross_norm.reshape(1, width),
-        final_norm=final_norm.reshape(1, width),
+        mid_norms=jnp.stack([cross_norm, final_norm]),
         spread=jnp.asarray(spread, HALF),
         summed=jnp.asarray(summed, HALF),
     )
@@ -932,9 +893,14 @@
         layer_out=((tokens, width), HALF),
         grad_inputs=((tokens, width), FULL),
     )
+    if reduce:
+        groups.append(Group(SMALL, 1, 32, 128))
     for g in groups:
         outs[f"out{g.name}"] = ((g.count, g.rows if reduce else 16 * g.rows, g.cols), HALF)
-    outs[MISC] = ((2 if reduce else 1, 16, width + 128), FULL)
+    if reduce:
+        outs[f"out{SMALL}"] = ((2, 32, 128), HALF)
+    else:
+        outs[MISC] = ((24, width + 128), FULL)
     scratch = dict(
         x_send=pltpu.VMEM((tokens, width), HALF),
         x_recv=pltpu.VMEM((tokens, width), HALF),
@@ -947,8 +913,6 @@
         grad=pltpu.VMEM((tokens, width), FULL),
         w_att=pltpu.VMEM((width, 3 * width), HALF),
         w_out=pltpu.VMEM((width, width), HALF),
-        w_pair=pltpu.VMEM((2, width, 2 * CHUNK), HALF),
-        w_lower=pltpu.VMEM((2, CHUNK, width), HALF),
         qkv_self=pltpu.VMEM((tokens, 3 * width), HALF),
         qkv_cross=pltpu.VMEM((tokens, 3 * width), HALF),
         mix_self=pltpu.VMEM((width, tokens), HALF),
@@ -964,20 +928,18 @@
         segments=pltpu.VMEM((8, length), jnp.int32),
         table=pltpu.VMEM((16, 2 * length), FULL),
         sums=pltpu.VMEM((16, 2 * length), FULL),
-        misc=pltpu.VMEM((10 if reduce else 1, 16, width + 128), FULL),
-        load=pltpu.SemaphoreType.DMA((11,)),
+        misc=pltpu.VMEM((8 if reduce else 24, width + 128), FULL),
+        load=pltpu.SemaphoreType.DMA((5 + 5 * RING,)),
         sem_x=pltpu.SemaphoreType.DMA((4, rows)),
-        sem_misc=pltpu.SemaphoreType.DMA((6, 2)),
         sem_out=pltpu.SemaphoreType.DMA((4 + rows,)),
     )
     for g in groups:
         if g.name != SELF:
             scratch[f"own{g.name}"] = pltpu.VMEM((g.count, 16 * g.rows, g.cols), HALF)
         if reduce:
-            scratch[f"first{g.name}"] = pltpu.VMEM((g.count, 8 * g.rows, g.cols), HALF)
-            scratch[f"second{g.name}"] = pltpu.VMEM((g.count, 4 * g.rows, g.cols), HALF)
-            scratch[f"third{g.name}"] = pltpu.VMEM((g.count, 3, g.rows, g.cols), HALF)
-        scratch[f"sem{g.name}"] = pltpu.SemaphoreType.DMA((g.count, 13))
+            for stage in range(4):
+                scratch[f"came{stage}x{g.name}"] = pltpu.VMEM((g.count, (8 >> stage) * g.rows, g.cols), HALF)
+        scratch[f"sem{g.name}"] = pltpu.SemaphoreType.DMA((g.count, 11))
     names = list(operands) + list(small) + list(outs) + list(scratch)
     results = pl.pallas_call(
         functools.partial(layer_kernel, names, groups, reduce, rows, length, width, hidden),
@@ -997,17 +959,103 @@
 VMEM_LIMIT = 64 * 2**20 - 64 * 2**10
 
 
+def finish_kernel(width, pair, lower, cross, own, small, layer, grad, *refs):
+    layer_out, grad_out, qkv, attn_out, gate_up, down, attn, ffn, query, kv, outer, mid, final, rel = refs[:14]
+    layer_held, grad_held, sem = refs[14:]
+    through = [(layer, layer_held, layer_out), (grad, grad_held, grad_out)]
+    arriving = [pltpu.make_async_copy(a, b, sem.at[n]) for n, (a, b, _) in enumerate(through)]
+    leaving = [pltpu.make_async_copy(b, c, sem.at[2 + n]) for n, (_, b, c) in enumerate(through)]
+    for copy in arriving:
+        copy.start()
+    for came, copy in zip(arriving, leaving):
+        came.wait()
+        copy.start()
+    chunks = pair.shape[0]
+    for k in range(chunks):
+        gate_up[:, k * CHUNK : (k + 1) * CHUNK] = pair[k, :, :CHUNK].astype(FULL)
+        up = (chunks + k) * CHUNK
+        gate_up[:, up : up + CHUNK] = pair[k, :, CHUNK:].astype(FULL)
+    for j in range(3):
+        down[:, j * 256 : (j + 1) * 256] = lower[j].astype(FULL)
+        qkv[:, j * width : (j + 1) * width] = own[1 + j].astype(FULL)
+    attn_out[...] = own[0].astype(FULL)
+    outer[...] = cross[0].astype(FULL)
+    query[...] = cross[1].astype(FULL)
+    for j in range(2):
+        kv[:, j * width : (j + 1) * width] = cross[2 + j].astype(FULL)
+    block = attn.shape[1]
+    mine = small[lax.axis_index("section")].astype(FULL)
+    attn[...] = mine[0:1, :block]
+    ffn[...] = mine[1:2, :block]
+    encoder, decoder = small[0].astype(FULL), small[1].astype(FULL)
+    mid[...] = decoder[2:3, :block]
+    final[...] = encoder[2:3, :block]
+    rel[...] = (encoder[8:24] + decoder[8:24]).T[:NBUCKET, :H]
+    for copy in leaving:
+        copy.wait()
+
+
+def finished(out, inputs, hidden):
+    tokens, width = out[LAYER].shape
+    block = width // 16
+    shapes = [(out[LAYER].shape, HALF), (out[INPUT].shape, FULL)] + [
+        (shape, FULL)
+        for shape in [
+            (block, 3 * width),
+            (block, width),
+            (block, 2 * hidden),
+            (hidden // 16, width),
+            (1, block),
+            (1, block),
+            (block, width),
+            (block, 2 * width),
+            (block, width),
+            (1, block),
+            (1, block),
+            (NBUCKET, H),
+        ]
+    ]
+    layer, grad, qkv, attn_out, gate_up, down, attn, ffn, query, kv, outer, mid, final, rel = pl.pallas_call(
+        functools.partial(finish_kernel, width),
+        out_shape=[jax.ShapeDtypeStruct(*shape) for shape in shapes],
+        in_specs=[pl.BlockSpec(memory_space=pltpu.VMEM)] * 5 + [pl.BlockSpec(memory_space=pl.ANY)] * 2,
+        out_specs=[pl.BlockSpec(memory_space=pl.ANY)] * 2 + [pl.BlockSpec(memory_space=pltpu.VMEM)] * 12,
+        scratch_shapes=[
+            pltpu.VMEM(out[LAYER].shape, HALF),
+            pltpu.VMEM(out[INPUT].shape, FULL),
+            pltpu.SemaphoreType.DMA((4,)),
+        ],
+        compiler_params=pltpu.CompilerParams(vmem_limit_bytes=VMEM_LIMIT),
+    )(*[out[f"out{name}"] for name in range(5)], out[LAYER], out[INPUT])
+    return (
+        layer.reshape(inputs.shape),
+        grad.reshape(inputs.shape),
+        qkv[None],
+        attn_out[None],
+        gate_up[None],
+        down[None],
+        attn,
+        ffn,
+        query,
+        kv,
+        outer,
+        mid.reshape(block),
+        final.reshape(block),
+        rel,
+    )
+
+
 def shards(*args):
-    inputs, rel_bias = args[0], args[4]
+    inputs = args[0]
     ways = lax.axis_size("dp")
-    _, rows, length, width = inputs.shape
+    width = inputs.shape[3]
     hidden = args[10].shape[1]
     out, reduce = run_layers(args, ways)
+    if reduce:
+        return finished(out, inputs, hidden)
 
     def wide(name):
         value = out[f"out{name}"]
-        if reduce:
-            return value.astype(FULL)
         total = lax.psum_scatter(value, "dp", scatter_dimension=1, tiled=True)
         if name == CROSS:
             total = lax.psum(jnp.where(lax.axis_index("section") == 1, total, 0), "section")
@@ -1020,18 +1068,13 @@
     chunks, block, _ = gate_up.shape
     gate_up = gate_up.reshape(chunks, block, 2, CHUNK).transpose(1, 2, 0, 3).reshape(block, 2 * hidden)
     down, cross, late = wide(DOWN), wide(CROSS), wide(SELF)
-    misc = out[MISC]
-    section = lax.axis_index("section")
-    if not reduce:
-        mine = lax.psum(misc[0], "dp")
-        misc = lax.all_gather(mine, "section", axis=0)
-    own = lax.dynamic_index_in_dim(misc, section, 0, keepdims=False)
+    own = lax.psum(out[MISC], "dp")
+    misc = lax.all_gather(own, "section", axis=0)
     start = lax.axis_index("dp") * block
 
     def piece(vector):
         return lax.dynamic_slice_in_dim(vector, start, block, 0)
 
-    rel = (misc[0] + misc[1])[:H, width : width + NBUCKET].T
     return (
         out[LAYER].reshape(inputs.shape),
         out[INPUT].reshape(inputs.shape),
@@ -1046,7 +1089,7 @@
         cross[0],
         piece(misc[1, 2, :width]),
         piece(misc[0, 2, :width]),
-        rel,
+        (misc[0] + misc[1])[8 : 8 + H, :NBUCKET].T,
     )
 
 

time: 234 us -> 206 us (0.88)
  Pallas kernels: 217 us -> 200 us
  local copies, waits for them, and re-layouts: 14.3 us -> 4.14 us
    pallas_call x1, Pallas kernels: 217 us -> 195 us  [run_layers(): pl.pallas_call(functools.partial(layer_kernel, names, groups, reduce, row...]
    pallas_call x0 -> x1, Pallas kernels: none -> 5.53 us  [finished(): pl.pallas_call(functools.partial(finish_kernel, width), out_shape=[jax.Sh...]
    reshape x3 -> x0, local copies, waits for them, and re-layouts: 3.26 us -> none  [the longest x1 1.26 us: run_layers(): cross_norm.reshape(1, width)]
where the time goes in v4:
time: 206 us
  Pallas kernels  200 us (97%)
  local copies, waits for them, and re-layouts  4.14 us (2%)
    pallas_call x1, Pallas kernels, run_layers(): pl.pallas_call(functools.partial(layer_kernel, names, groups, reduce, row...  195 us
    pallas_call x1, Pallas kernels, finished(): pl.pallas_call(functools.partial(finish_kernel, width), out_shape=[jax.Sh...  5.53 us

profile of v4, /device:TPU:0, one launch (start us, length us, event | category | flops | bytes accessed | tf_op | source)
XLA Modules:
  0.0 205.6 jit_solution(10616353873484929115)
XLA Ops:
  0.6 0.7 stack.9
  1.3 0.7 stack.10
  2.0 0.6 pad_maximum_fusion.refs_14_
  2.6 1.4 copy.32.refs_11_
  4.0 194.7 %shard_map.281 = (bf16[512,768]{1,0:T(8,128)(2,1)}, f32[512,768]{1,0:T(8,128)}, bf16[8,48,512]{2,1,0:T(8,128)(2,1)}, bf16[3,128,256]{2,1,0:T(8,128)(2,1)}, bf16[...) custom-call(bf16[512,768]{1,0:T(8,128)(2,1)} %bitcast.10, ...), custom_call_target="tpu_custom_call" | custom-call | tf_op jit(solution)/shard_map/pallas_call | solution.py:944
  198.7 5.5 %shard_map.282 = (bf16[512,768]{1,0:T(8,128)(2,1)}, f32[512,768]{1,0:T(8,128)}, f32[48,2304]{1,0:T(8,128)}, f32[48,768]{1,0:T(8,128)}, f32[48,4096]{1,0:T(8,128)...) custom-call(bf16[8,48,512]{2,1,0:T(8,128)(2,1)} %get-tuple-element.3, ...), custom_call_target="tpu_custom_call" | custom-call | tf_op jit(solution)/shard_map/pallas_call | solution.py:1018
  204.2 1.4 copy.33

commit v5 on v4

--- a/solution.py
+++ b/solution.py
@@ -23,8 +23,8 @@
 PAIRS = H // 2
 CHUNK = 256
 BLOCK = 64
-UNROLL = 2
 RING = 4
+DECODER_TICKS = 4
 GATE_UP, DOWN, CROSS, SELF, SMALL = range(5)
 GELU_SCALE = math.sqrt(2.0 / math.pi)
 GELU_CUBE = 0.044715
@@ -283,6 +283,18 @@
                 exchange(name, i, stage).wait_send()
             if name in (CROSS, SMALL):
                 cross_over(name, i, i).wait_send()
+
+    def items_of(*names):
+        return [(name, i) for name in names for i in range(by_name[name].count)]
+
+    last = items_of(SELF, SMALL) if reduce else items_of(SELF)
+    encoder_line = items_of(GATE_UP, DOWN) + last
+    decoder_line = items_of(GATE_UP, DOWN, CROSS) + last
+
+    def advance(line, n):
+        for stage in (1, 2, 3):
+            if 0 <= n + 1 - stage < len(line):
+                add(*line[n + 1 - stage], stage)
 
     def block_of(ref, b):
         return ref.at[b // 9, pl.ds(at128((b % 9) // 3, 256), 256), pl.ds(at128(b % 3, 256), 256)]
@@ -351,16 +363,10 @@
                 mixed = dot(values_t[e * HD : (e + 1) * HD], softmaxed)
                 mix[pl.ds(pl.multiple_of(hp * 128 + e * HD, 16), HD), at] = mixed.astype(HALF)
 
-        repeat_pairs(pair)
-
-    def repeat_pairs(pair):
-        def step(g):
-            for u in range(UNROLL):
-                pair(g * UNROLL + u)
-
-        repeat(PAIRS // UNROLL, step)
-
-    def attend_back(qkv, probs_of, row, with_bias, tick):
+        for hp in range(PAIRS):
+            pair(hp)
+
+    def attend_back(qkv, probs_of, row, with_bias):
         at = row_slice(row)
         left = lax.broadcasted_iota(jnp.int32, (length, 128), 1) < HD
         def pair(hp):
@@ -398,10 +404,9 @@
             qkv[at, q_lanes] = jnp.concatenate(parts, 0).T.astype(HALF)
             qkv[at, k_lanes] = jnp.where(left, grad_keys[:length], grad_keys[length:]).astype(HALF)
             qkv[at, v_lanes] = jnp.where(left, grad_values[:length], grad_values[length:]).astype(HALF)
-            if tick is not None:
-                tick(hp)
-
-        repeat_pairs(pair)
+
+        for hp in range(PAIRS):
+            pair(hp)
 
     def normalise(load_rows, row, column, gain, unit_ref, target):
         for b in range(length // BLOCK):
@@ -543,11 +548,9 @@
                     add_first(DOWN, part)
 
     def weight_gradient(name, item, left_t, right, at):
-        def step(j):
-            tile = dot(left_t[...], right[:, pl.ds(pl.multiple_of(at + j * 256, 128), 256)])
-            put(name, item, pl.ds(at128(j, 256), 256), tile)
-
-        repeat(width // 256, step)
+        for j in range(width // 256):
+            n = slice(j * 256, (j + 1) * 256)
+            put(name, item, n, dot(left_t[...], right[:, at + j * 256 : at + (j + 1) * 256]))
         begin(name, item)
 
     def back_through_out(row):
@@ -617,11 +620,9 @@
         at = row_slice(row)
         normalise(as_full(x_send), row, 0, attn_gain, None, low)
 
-        def project(j):
-            columns = pl.ds(at128(j, 256), 256)
-            qkv_self[at, columns] = dot(low[at, :], w_att[:, columns]).astype(HALF)
-
-        repeat(3 * width // 256, project)
+        for j in range(3 * width // 256):
+            n = slice(j * 256, (j + 1) * 256)
+            qkv_self[at, n] = dot(low[at, :], w_att[:, n]).astype(HALF)
         make_mask(v.segments, v.segments, row, encoder)
         attend(qkv_self, self_probs, mix_self, row, True)
         transpose_back(low, mix_self, row)
@@ -646,11 +647,9 @@
         make_mask(v.enc_segments, v.dec_segments, row, None)
         memory_copy(row).wait_recv()
 
-        def project_memory(j):
-            columns = pl.ds(pl.multiple_of(width + j * 256, 128), 256)
-            qkv_cross[at, columns] = dot(x_recv[at, :], w_att[:, columns]).astype(HALF)
-
-        repeat(2 * width // 256, project_memory)
+        for j in range(width // 256, 3 * width // 256):
+            n = slice(j * 256, (j + 1) * 256)
+            qkv_cross[at, n] = dot(x_recv[at, :], w_att[:, n]).astype(HALF)
         attend(qkv_cross, cross_probs, mix_cross, row, False)
         transpose_back(low, mix_cross, row)
         add_projection(w_out, res, row)
@@ -660,7 +659,7 @@
         write_layer(row).start()
         norm_back(as_full(grad), as_full(unit_ffn), row, 1, ffn_gain, 1, as_full(cot), low)
         back_through_out(row)
-        attend_back(qkv_cross, cross_probs, row, False, None)
+        attend_back(qkv_cross, cross_probs, row, False)
         write_layer(row).wait()
         for j in range(width // 256):
             n = slice(j * 256, (j + 1) * 256)
@@ -697,16 +696,22 @@
             low_t[:, at] = (unit_mid[at, :].astype(FULL) * cross_gain).astype(HALF).T
 
         repeat(tokens // 128, gained)
+        add_first(CROSS, 0)
+        advance(decoder_line, 0)
         weight_gradient(CROSS, 1, low_t, qkv_cross, 0)
+        advance(decoder_line, 1)
         for row in range(rows):
             transpose_rows(low_t, x_recv, row)
+        add_first(CROSS, 1)
         weight_gradient(CROSS, 2, low_t, qkv_cross, width)
+        advance(decoder_line, 2)
+        add_first(CROSS, 2)
         weight_gradient(CROSS, 3, low_t, qkv_cross, 2 * width)
+        advance(decoder_line, 3)
         load_x_again().start()
         for row in range(rows):
             norm_back(as_full(res), as_full(unit_mid), row, 2, cross_gain, 2, as_full(grad), low)
-        for item in range(4):
-            add_first(CROSS, item)
+        add_first(CROSS, 3)
         load_att().wait()
         load_out().wait()
 
@@ -714,17 +719,6 @@
 
     def unit_self(at):
         return qkv_cross[at, :width].astype(FULL) * inverse[at, 0:1]
-
-    def advance(i):
-        add(GATE_UP, i, 1)
-
-        @pl.when(i >= 1)
-        def _():
-            add(GATE_UP, i - 1, 2)
-
-        @pl.when(i >= 2)
-        def _():
-            add(GATE_UP, i - 2, 3)
 
     def backward_row(row):
         at = row_slice(row)
@@ -740,17 +734,26 @@
             feed_forward(row, False, True, res, 0, encoder_unit, row + 1 < rows)
             norm_back(as_full(res), as_full(unit_ffn), row, 1, ffn_gain, 1, as_full(grad), low)
 
-        def tick(hp):
-            @pl.when(jnp.where(encoder, row == rows - 1, row == 0))
+        def ticks(first, count):
+            @pl.when(encoder & (row == rows - 1))
             def _():
-                advance(hp)
-
-            @pl.when(decoder & (row == rows - 1) & (hp < chunks - PAIRS))
+                for j in range(first, first + count):
+                    advance(encoder_line, j)
+
+            @pl.when(decoder & (row == 0))
             def _():
-                advance(PAIRS + hp)
+                for j in range(first, first + count):
+                    advance(decoder_line, DECODER_TICKS + j)
 
         back_through_out(row)
-        attend_back(qkv_self, self_probs, row, True, tick)
+        ticks(0, 1)
+        attend_back(qkv_self, self_probs, row, True)
+        ticks(1, PAIRS - 1)
+
+        @pl.when(decoder & (row == rows - 1))
+        def _():
+            advance(decoder_line, DECODER_TICKS + PAIRS)
+
         for j in range(width // 256):
             n = slice(j * 256, (j + 1) * 256)
             res[at, n] = dot_outer(qkv_self[at, :], w_att[n, :])
@@ -788,20 +791,17 @@
         begin(SMALL, 0)
         add_first(SMALL, 0)
 
-    def drain(names, done):
-        line = [(name, i) for name in names for i in range(by_name[name].count)]
+    def drain(line, done):
         for n in range(done, len(line) + 2):
-            for stage in (1, 2, 3):
-                if 0 <= n + 1 - stage < len(line):
-                    add(*line[n + 1 - stage], stage)
+            advance(line, n)
 
     @pl.when(encoder)
     def _():
-        drain([GATE_UP, DOWN, SELF] + ([SMALL] if reduce else []), PAIRS)
+        drain(encoder_line, PAIRS)
 
     @pl.when(decoder)
     def _():
-        drain([GATE_UP, DOWN, CROSS, SELF] + ([SMALL] if reduce else []), chunks)
+        drain(decoder_line, DECODER_TICKS + PAIRS + 1)
 
     if not reduce:
         misc[8:24, :NBUCKET] = by_bucket

time: 206 us -> 196 us (0.951)
  Pallas kernels: 200 us -> 190 us
    pallas_call x1, Pallas kernels: 195 us -> 184 us  [run_layers(): pl.pallas_call(functools.partial(layer_kernel, names, groups, reduce, row...]
where the time goes in v5:
time: 196 us; the launch traced here: 195 us
  Pallas kernels  190 us (97%)
  local copies, waits for them, and re-layouts  4.14 us (2%)
    pallas_call x1, Pallas kernels, run_layers(): pl.pallas_call(functools.partial(layer_kernel, names, groups, reduce, row...  184 us
    pallas_call x1, Pallas kernels, finished(): pl.pallas_call(functools.partial(finish_kernel, width), out_shape=[jax.Sh...  5.53 us

profile of v5, /device:TPU:0, one launch (start us, length us, event | category | flops | bytes accessed | tf_op | source)
XLA Modules:
  0.0 195.4 jit_solution(15151239900835676164)
XLA Ops:
  0.6 0.7 stack.9
  1.3 0.7 stack.10
  2.0 0.6 pad_maximum_fusion.refs_14_
  2.6 1.4 copy.32.refs_11_
  4.0 184.5 %shard_map.281 = (bf16[512,768]{1,0:T(8,128)(2,1)}, f32[512,768]{1,0:T(8,128)}, bf16[8,48,512]{2,1,0:T(8,128)(2,1)}, bf16[3,128,256]{2,1,0:T(8,128)(2,1)}, bf16[...) custom-call(bf16[512,768]{1,0:T(8,128)(2,1)} %bitcast.10, ...), custom_call_target="tpu_custom_call" | custom-call | tf_op jit(solution)/shard_map/pallas_call | solution.py:944
  188.5 5.5 %shard_map.282 = (bf16[512,768]{1,0:T(8,128)(2,1)}, f32[512,768]{1,0:T(8,128)}, f32[48,2304]{1,0:T(8,128)}, f32[48,768]{1,0:T(8,128)}, f32[48,4096]{1,0:T(8,128)...) custom-call(bf16[8,48,512]{2,1,0:T(8,128)(2,1)} %get-tuple-element.3, ...), custom_call_target="tpu_custom_call" | custom-call | tf_op jit(solution)/shard_map/pallas_call | solution.py:1018
  194.0 1.4 copy.33

commit v6 on v5

--- a/solution.py
+++ b/solution.py
@@ -514,6 +514,10 @@
 
             @pl.when(row == rows - 1)
             def _():
+                @pl.when(k > 0)
+                def _():
+                    add_first(GATE_UP, k - 1)
+
                 for part in range(2):
                     columns = slice(part * CHUNK, (part + 1) * CHUNK)
                     right = jnp.concatenate([first[part][...], joint[:, columns]], 0)
@@ -531,10 +535,6 @@
                             ]
                     else:
                         v.own1[part, pl.ds(at128(k, CHUNK), CHUNK)] = tile
-
-                @pl.when(k > 0)
-                def _():
-                    add_first(GATE_UP, k - 1)
 
         repeat(chunks, step)
         if backward:

time: 196 us -> 197 us (level)
  no operation moved by 1% of the time
where the time goes in v6:
time: 197 us; the launch traced here: 196 us
  Pallas kernels  191 us (97%)
  local copies, waits for them, and re-layouts  4.14 us (2%)
    pallas_call x1, Pallas kernels, run_layers(): pl.pallas_call(functools.partial(layer_kernel, names, groups, reduce, row...  186 us
    pallas_call x1, Pallas kernels, finished(): pl.pallas_call(functools.partial(finish_kernel, width), out_shape=[jax.Sh...  5.53 us

profile of v6, /device:TPU:0, one launch (start us, length us, event | category | flops | bytes accessed | tf_op | source)
XLA Modules:
  0.0 196.5 jit_solution(6594268778280978842)
XLA Ops:
  0.6 0.7 stack.9
  1.3 0.7 stack.10
  2.0 0.6 pad_maximum_fusion.refs_14_
  2.6 1.4 copy.32.refs_11_
  4.0 185.6 %shard_map.281 = (bf16[512,768]{1,0:T(8,128)(2,1)}, f32[512,768]{1,0:T(8,128)}, bf16[8,48,512]{2,1,0:T(8,128)(2,1)}, bf16[3,128,256]{2,1,0:T(8,128)(2,1)}, bf16[...) custom-call(bf16[512,768]{1,0:T(8,128)(2,1)} %bitcast.10, ...), custom_call_target="tpu_custom_call" | custom-call | tf_op jit(solution)/shard_map/pallas_call | solution.py:944
  189.6 5.5 %shard_map.282 = (bf16[512,768]{1,0:T(8,128)(2,1)}, f32[512,768]{1,0:T(8,128)}, f32[48,2304]{1,0:T(8,128)}, f32[48,768]{1,0:T(8,128)}, f32[48,4096]{1,0:T(8,128)...) custom-call(bf16[8,48,512]{2,1,0:T(8,128)(2,1)} %get-tuple-element.3, ...), custom_call_target="tpu_custom_call" | custom-call | tf_op jit(solution)/shard_map/pallas_call | solution.py:1018
  195.1 1.4 copy.33
